TPU v7x, 32 devices: a whole 2x2x4 slice. The times are simulated.
32 devices in a mesh: dp: 4 (over y, x), ctx: 4 (over z), wt: 2 (over core).
Axes of the slice: x: 2, y: 2, z: 4, core: 2. Of those that a mesh axis runs over, the one named last changes fastest.
Arguments:
- hidden: bfloat16 [8, 1024, 1088], P('dp', ('ctx', 'wt')), may hold values from -6 to 6
- block_order: int32 [8], replicated, may hold values from 0 to 7, as said below
- ln1_gain: bfloat16 [1088], replicated, may hold values from 0.5 to 1.5
- ln1_bias: bfloat16 [1088], replicated, may hold values from -1.796875 to 1.796875
- w_qkv: bfloat16 [1088, 3264], P('wt'), may hold values from -0.1875 to 0.1875
- q_bias: bfloat16 [1088], replicated, may hold values from -3 to 3
- v_bias: bfloat16 [1088], replicated, may hold values from -0.59765625 to 0.59765625
- w_proj: bfloat16 [1088, 1088], P('wt'), may hold values from -0.75 to 0.75
- proj_bias: bfloat16 [1088], replicated, may hold values from -1.796875 to 1.796875
- ln2_gain: bfloat16 [1088], replicated, may hold values from 0.5 to 1.5
- ln2_bias: bfloat16 [1088], replicated, may hold values from -1.796875 to 1.796875
- w_up: bfloat16 [1088, 4352], P(None, 'wt'), may hold values from -0.1875 to 0.1875
- up_bias: bfloat16 [4352], P('wt'), may hold values from -3 to 3
- w_down: bfloat16 [4352, 1088], P('wt'), may hold values from -0.09375 to 0.09375
- down_bias: bfloat16 [1088], replicated, may hold values from -1.796875 to 1.796875
- cotangent: bfloat16 [8, 1024, 1088], P('dp', ('ctx', 'wt')), may hold values from -6 to 6
Outputs:
- output: bfloat16 [8, 1024, 1088], P('dp', ('ctx', 'wt'))
- grad_hidden: bfloat16 [8, 1024, 1088], P('dp', ('ctx', 'wt'))
- grad_ln1_gain: float32 [1088], P('wt')
- grad_ln1_bias: float32 [1088], P('wt')
- grad_w_qkv: float32 [1088, 3264], P('wt')
- grad_q_bias: float32 [1088], P('wt')
- grad_v_bias: float32 [1088], P('wt')
- grad_w_proj: float32 [1088, 1088], P('wt')
- grad_proj_bias: float32 [1088], P('wt')
- grad_ln2_gain: float32 [1088], P('wt')
- grad_ln2_bias: float32 [1088], P('wt')
- grad_w_up: float32 [1088, 4352], P(None, 'wt')
- grad_up_bias: float32 [4352], P('wt')
- grad_w_down: float32 [4352, 1088], P('wt')
- grad_down_bias: float32 [1088], P('wt')
Inputs may be any that keep to these rules, and one draw needn't show every extreme that they name: `block_order`: entries 2 r and 2 r + 1 are the causal blocks stored at cycle position r: every block number appears once, and the two of one cycle position add up to 7.
All inputs are finite; a program needn't handle non-finite values.
Results may differ from a plain program's by a relative error of at most 0.019.
Values may be sent and summed in bfloat16 or wider, within the bound.
No kernel may reach another device: no remote copies, remote signals or barrier semaphores. Data moves between devices by JAX's collectives and lax.ppermute only.
A program may use at most 320 MiB of HBM per device.

v0:
```python
import math

import jax
import jax.numpy as jnp
from jax import lax
from jax.sharding import PartitionSpec as P

HEADS = 17


epsilon = 1e-05
masked_value = -1e30


def merged(part, axis, combine):
    gathered = jax.tree.map(lambda a: lax.all_gather(a, axis), part)

    def take(source):
        return jax.tree.map(lambda a: lax.dynamic_index_in_dim(a, source, 0, False), gathered)

    return lax.fori_loop(
        1, lax.axis_size(axis), lambda source, state: combine(state, take(source)), take(0)
    )


def layer_norm(values, gain, offset):
    average = jnp.mean(values, axis=-1, keepdims=True)
    mean_shifted_input = values - average
    variance = jnp.mean(mean_shifted_input * mean_shifted_input, axis=-1, keepdims=True)
    return mean_shifted_input * lax.rsqrt(variance + epsilon) * gain + offset


def gelu_tanh(values):
    return jax.nn.gelu(values, approximate=True)


def lookup(table, position):
    slots = jnp.arange(table.shape[0], dtype=jnp.int32)
    return jnp.sum(jnp.where(slots == position, table, 0))


def merge_stats(first, second):
    highest = jnp.maximum(first[0], second[0])
    return (
        highest,
        first[1] * jnp.exp(first[0] - highest) + second[1] * jnp.exp(second[0] - highest),
    )


def keep_state(current):
    return current


def local(
    hidden,
    block_order,
    ln1_gain,
    ln1_bias,
    w_qkv,
    q_bias,
    v_bias,
    w_proj,
    proj_bias,
    ln2_gain,
    ln2_bias,
    w_up,
    up_bias,
    w_down,
    down_bias,
    cotangent,
):
    seqs, seq_dev, width = hidden.shape
    head_dim = width // HEADS
    scale = 1.0 / math.sqrt(head_dim)
    ctx_count = lax.axis_size("ctx")
    wt_count = lax.axis_size("wt")
    ctx_index = lax.axis_index("ctx")
    wt_index = lax.axis_index("wt")
    group_rows = wt_count * seq_dev
    half_rows = group_rows // 2
    inputs = hidden.astype(jnp.float32)
    normed, norm_one_pull = jax.vjp(
        layer_norm, inputs, ln1_gain.astype(jnp.float32), ln1_bias.astype(jnp.float32)
    )
    standardized_summed_output = normed.astype(jnp.bfloat16)
    query_key_value_complete, projection_complete = (
        lax.all_gather(w_qkv, "wt", axis=0, tiled=True),
        lax.all_gather(w_proj, "wt", axis=0, tiled=True),
    )
    blended_rows = jnp.einsum(
        "vox,xg->vog",
        standardized_summed_output,
        query_key_value_complete,
        preferred_element_type=jnp.float32,
    )
    query = ((blended_rows[..., :width] + q_bias.astype(jnp.float32)) * scale).astype(jnp.bfloat16)
    keys = blended_rows[..., width : 2 * width].astype(jnp.bfloat16)
    values = (blended_rows[..., 2 * width :] + v_bias.astype(jnp.float32)).astype(jnp.bfloat16)
    query_group = lax.all_gather(query, "wt", axis=1, tiled=True)
    key_all, value_all = (
        lax.all_gather(keys[None], "ctx", axis=0, tiled=True),
        lax.all_gather(values[None], "ctx", axis=0, tiled=True),
    )
    query_heads = query_group.reshape(seqs, 2, half_rows, HEADS, head_dim)
    query_parts = [query_heads[:, 0], query_heads[:, 1]]
    query_ranks = [lookup(block_order, 2 * ctx_index + which_half) for which_half in range(2)]
    query_places = [
        query_ranks[which_half] * half_rows + jnp.arange(half_rows, dtype=jnp.int32)
        for which_half in range(2)
    ]
    first_column_offset = wt_index * seq_dev

    def key_place(source):
        key_rank = lookup(block_order, 2 * source + first_column_offset // half_rows)
        return (
            key_rank,
            key_rank * half_rows
            + first_column_offset % half_rows
            + jnp.arange(seq_dev, dtype=jnp.int32),
        )

    def head_piece(stacked, source):
        return stacked[source].reshape(seqs, seq_dev, HEADS, head_dim)

    def score_block(which_half, key_piece):
        return jnp.einsum(
            "sqhe,skhe->shqk",
            query_parts[which_half],
            key_piece,
            preferred_element_type=jnp.float32,
        )

    def stats_step(source, carry):
        running_max, running_sum = carry
        key_rank, key_places = key_place(source)
        key_piece = head_piece(key_all, source)
        for which_half in range(2):

            def stats_visit(current, which_half=which_half):
                old_max, old_sum = current
                visible = key_places[None, :] <= query_places[which_half][:, None]
                scores = jnp.where(visible, score_block(which_half, key_piece), masked_value)
                new_max = jnp.maximum(old_max, jnp.max(scores, axis=-1))
                weights = jnp.exp(jnp.where(visible, scores - new_max[..., None], masked_value))
                return (new_max, old_sum * jnp.exp(old_max - new_max) + jnp.sum(weights, axis=-1))

            updated = lax.cond(
                key_rank <= query_ranks[which_half],
                stats_visit,
                keep_state,
                (running_max[which_half], running_sum[which_half]),
            )
            running_max = running_max.at[which_half].set(updated[0])
            running_sum = running_sum.at[which_half].set(updated[1])
        return (running_max, running_sum)

    start_max = jnp.full((2, seqs, HEADS, half_rows), masked_value, jnp.float32)
    start_sum = jnp.zeros((2, seqs, HEADS, half_rows), jnp.float32)
    local_max, local_sum = lax.fori_loop(0, ctx_count, stats_step, (start_max, start_sum))
    total_max, total_sum = merged((local_max, local_sum), "wt", merge_stats)
    log_total = total_max + jnp.log(total_sum)

    def output_step(source, accum):
        key_rank, key_places = key_place(source)
        key_piece = head_piece(key_all, source)
        value_piece = head_piece(value_all, source)
        for which_half in range(2):

            def output_visit(current, which_half=which_half):
                visible = key_places[None, :] <= query_places[which_half][:, None]
                shifted = score_block(which_half, key_piece) - log_total[which_half][..., None]
                probs = jnp.exp(jnp.where(visible, shifted, masked_value)).astype(jnp.bfloat16)
                return current + jnp.einsum(
                    "shqk,skhe->sqhe", probs, value_piece, preferred_element_type=jnp.float32
                )

            updated = lax.cond(
                key_rank <= query_ranks[which_half], output_visit, keep_state, accum[:, which_half]
            )
            accum = accum.at[:, which_half].set(updated)
        return accum

    start_out = jnp.zeros((seqs, 2, half_rows, HEADS, head_dim), jnp.float32)
    partial_out = lax.fori_loop(0, ctx_count, output_step, start_out)
    attended = lax.psum(
        partial_out.reshape(seqs, group_rows, width).astype(jnp.bfloat16), "wt"
    ).astype(jnp.float32)
    attention_reduced = lax.dynamic_slice_in_dim(attended, wt_index * seq_dev, seq_dev, 1).astype(
        jnp.bfloat16
    )
    branch = jnp.einsum(
        "vox,xg->vog", attention_reduced, projection_complete, preferred_element_type=jnp.float32
    ) + proj_bias.astype(jnp.float32)
    middle = inputs + branch
    normed_two, norm_two_pull = jax.vjp(
        layer_norm, middle, ln2_gain.astype(jnp.float32), ln2_bias.astype(jnp.float32)
    )
    normed_two_low = normed_two.astype(jnp.bfloat16)
    rows_two = lax.all_gather(normed_two_low, "wt", axis=1, tiled=True)
    pre_act = jnp.einsum(
        "snd,df->snf", rows_two, w_up, preferred_element_type=jnp.float32
    ) + up_bias.astype(jnp.float32)
    activated, gelu_pull = jax.vjp(gelu_tanh, pre_act)
    act_low = activated.astype(jnp.bfloat16)
    down_terms = jnp.einsum("snf,fd->snd", act_low, w_down, preferred_element_type=jnp.float32)
    mlp_sum = lax.psum_scatter(
        down_terms.astype(jnp.bfloat16), "wt", scatter_dimension=1, tiled=True
    ).astype(jnp.float32)
    output = (middle + mlp_sum + down_bias.astype(jnp.float32)).astype(jnp.bfloat16)
    grad_out = cotangent.astype(jnp.float32)
    grad_down_bias = jnp.sum(grad_out, axis=(0, 1))
    grad_rows = lax.all_gather(cotangent, "wt", axis=1, tiled=True)
    grad_act = jnp.einsum("snd,fd->snf", grad_rows, w_down, preferred_element_type=jnp.float32)
    grad_w_down = jnp.einsum("snf,snd->fd", act_low, grad_rows, preferred_element_type=jnp.float32)
    grad_pre = gelu_pull(grad_act)[0].astype(jnp.bfloat16)
    grad_up_bias = jnp.sum(grad_pre.astype(jnp.float32), axis=(0, 1))
    grad_w_up = jnp.einsum("snd,snf->df", rows_two, grad_pre, preferred_element_type=jnp.float32)
    back_terms = jnp.einsum("snf,df->snd", grad_pre, w_up, preferred_element_type=jnp.float32)
    grad_norm_two = lax.psum_scatter(
        back_terms.astype(jnp.bfloat16), "wt", scatter_dimension=1, tiled=True
    ).astype(jnp.float32)
    grad_mid_norm, grad_ln2_gain, grad_ln2_bias = norm_two_pull(grad_norm_two)
    grad_mid = grad_out + grad_mid_norm
    gradient_residual_branch = grad_mid.astype(jnp.bfloat16)
    grad_proj_bias = jnp.sum(gradient_residual_branch.astype(jnp.float32), axis=(0, 1))
    grad_w_proj = jnp.einsum(
        "vzo,vzf->of",
        attention_reduced,
        gradient_residual_branch,
        preferred_element_type=jnp.float32,
    )
    grad_attn = jnp.einsum(
        "izj,lj->izl",
        gradient_residual_branch,
        projection_complete,
        preferred_element_type=jnp.float32,
    ).astype(jnp.bfloat16)
    grad_attn_rows = lax.all_gather(grad_attn, "wt", axis=1, tiled=True)
    grad_heads = grad_attn_rows.reshape(seqs, 2, half_rows, HEADS, head_dim)
    delta_rows = jnp.sum(
        grad_heads.astype(jnp.float32) * attended.reshape(seqs, 2, half_rows, HEADS, head_dim),
        axis=-1,
    )
    delta = jnp.transpose(delta_rows, (1, 0, 3, 2))

    def backward_step(source, carry):
        query_grad, pair_grad = carry
        key_rank, key_places = key_place(source)
        key_piece = head_piece(key_all, source)
        value_piece = head_piece(value_all, source)
        key_sum = jnp.zeros((seqs, seq_dev, HEADS, head_dim), jnp.float32)
        value_sum = jnp.zeros((seqs, seq_dev, HEADS, head_dim), jnp.float32)
        for which_half in range(2):

            def backward_visit(current, which_half=which_half):
                half_grad, key_acc, value_acc = current
                visible = key_places[None, :] <= query_places[which_half][:, None]
                shifted = score_block(which_half, key_piece) - log_total[which_half][..., None]
                probs = jnp.exp(jnp.where(visible, shifted, masked_value))
                grad_probs = jnp.einsum(
                    "sqhe,skhe->shqk",
                    grad_heads[:, which_half],
                    value_piece,
                    preferred_element_type=jnp.float32,
                )
                grad_scores = (probs * (grad_probs - delta[which_half][..., None])).astype(
                    jnp.bfloat16
                )
                half_grad = half_grad + jnp.einsum(
                    "shqk,skhe->sqhe", grad_scores, key_piece, preferred_element_type=jnp.float32
                )
                key_acc = key_acc + jnp.einsum(
                    "shqk,sqhe->skhe",
                    grad_scores,
                    query_parts[which_half],
                    preferred_element_type=jnp.float32,
                )
                value_acc = value_acc + jnp.einsum(
                    "shqk,sqhe->skhe",
                    probs.astype(jnp.bfloat16),
                    grad_heads[:, which_half],
                    preferred_element_type=jnp.float32,
                )
                return (half_grad, key_acc, value_acc)

            half_grad, key_sum, value_sum = lax.cond(
                key_rank <= query_ranks[which_half],
                backward_visit,
                keep_state,
                (query_grad[:, which_half], key_sum, value_sum),
            )
            query_grad = query_grad.at[:, which_half].set(half_grad)
        block_grad = jnp.concatenate(
            [key_sum.reshape(seqs, seq_dev, width), value_sum.reshape(seqs, seq_dev, width)],
            axis=-1,
        )
        pair_grad = pair_grad.at[source].set(block_grad)
        return (query_grad, pair_grad)

    start_query = jnp.zeros((seqs, 2, half_rows, HEADS, head_dim), jnp.float32)
    start_pair = jnp.zeros((ctx_count, seqs, seq_dev, 2 * width), jnp.float32)
    query_grad, pair_grad = lax.fori_loop(0, ctx_count, backward_step, (start_query, start_pair))
    query_grad_own = lax.psum_scatter(
        query_grad.reshape(seqs, group_rows, width).astype(jnp.bfloat16),
        "wt",
        scatter_dimension=1,
        tiled=True,
    )
    pair_grad_own = lax.psum_scatter(
        pair_grad.astype(jnp.bfloat16), "ctx", scatter_dimension=0, tiled=True
    ).astype(jnp.float32)[0]
    grad_query_low = query_grad_own * scale
    grad_keys_low = pair_grad_own[..., :width].astype(jnp.bfloat16)
    grad_values_low = pair_grad_own[..., width:].astype(jnp.bfloat16)
    grad_q_bias = jnp.sum(grad_query_low.astype(jnp.float32), axis=(0, 1))
    grad_v_bias = jnp.sum(grad_values_low.astype(jnp.float32), axis=(0, 1))
    mixture_derivative = jnp.concatenate([grad_query_low, grad_keys_low, grad_values_low], axis=-1)
    grad_w_qkv = jnp.einsum(
        "vzo,vzf->of",
        standardized_summed_output,
        mixture_derivative,
        preferred_element_type=jnp.float32,
    )
    gradient_normalized_rows = jnp.einsum(
        "izj,lj->izl",
        mixture_derivative,
        query_key_value_complete,
        preferred_element_type=jnp.float32,
    )
    grad_in_norm, grad_ln1_gain, grad_ln1_bias = norm_one_pull(gradient_normalized_rows)
    grad_hidden = (grad_mid + grad_in_norm).astype(jnp.bfloat16)
    small_grads = jnp.stack(
        [
            grad_ln1_gain,
            grad_ln1_bias,
            grad_q_bias,
            grad_v_bias,
            grad_proj_bias,
            grad_ln2_gain,
            grad_ln2_bias,
            grad_down_bias,
        ]
    )
    qkv_shard, proj_shard, small_shard = (
        lax.psum_scatter(
            grad_w_qkv.astype(jnp.bfloat16), "wt", scatter_dimension=0, tiled=True
        ).astype(jnp.float32),
        lax.psum_scatter(
            grad_w_proj.astype(jnp.bfloat16), "wt", scatter_dimension=0, tiled=True
        ).astype(jnp.float32),
        lax.psum_scatter(
            small_grads.astype(jnp.bfloat16), "wt", scatter_dimension=1, tiled=True
        ).astype(jnp.float32),
    )
    qkv_total, proj_total, small_total, up_total, up_bias_total, down_total = lax.psum(
        (qkv_shard, proj_shard, small_shard, grad_w_up, grad_up_bias, grad_w_down), ("dp", "ctx")
    )
    return (
        output,
        grad_hidden,
        small_total[0],
        small_total[1],
        qkv_total,
        small_total[2],
        small_total[3],
        proj_total,
        small_total[4],
        small_total[5],
        small_total[6],
        up_total,
        up_bias_total,
        down_total,
        small_total[7],
    )


def solution(mesh):
    placed = (
        P("dp", ("ctx", "wt"), None),
        P(),
        P(),
        P(),
        P("wt", None),
        P(),
        P(),
        P("wt", None),
        P(),
        P(),
        P(),
        P(None, "wt"),
        P("wt"),
        P("wt", None),
        P(),
        P("dp", ("ctx", "wt"), None),
    )
    return jax.shard_map(
        local,
        mesh=mesh,
        in_specs=placed,
        out_specs=(
            P("dp", ("ctx", "wt"), None),
            P("dp", ("ctx", "wt"), None),
            P("wt"),
            P("wt"),
            P("wt", None),
            P("wt"),
            P("wt"),
            P("wt", None),
            P("wt"),
            P("wt"),
            P("wt"),
            P(None, "wt"),
            P("wt"),
            P("wt", None),
            P("wt"),
        ),
        check_vma=False,
    )
```

profile of v0, /device:TPU:0, one launch (start us, length us, event | category | flops | bytes accessed | tf_op | source)
XLA Modules:
  0.0 1442.7 jit_solution(3778340045405948994)
XLA Ops:
  8.7 21.8 %all-gather.13.cloned.1.call-done = bf16[1088,3264]{1,0:T(8,128)(2,1)} async-done(((bf16[544,3264]{1,0:T(8,128)(2,1)}), bf16[1088,3264]{1,0:T(8,128)(2,1)}) %all-gather.13.cloned.1.call-update) | async-done | bytes 7102480 | tf_op jit(solution)/shard_map/all_gather | solution.py:87
  30.5 6.7 fusion.62
  55.0 46.5 %all-gather.25.cloned.1.call-done = bf16[8,128,1088]{1,2,0:T(8,128)(2,1)} async-done(((bf16[2,128,1088]{1,2,0:T(8,128)(2,1)}), bf16[8,128,1088]{1,2,0:T(8,128)(2,1)}) %all-gather.25.cloned.1.call-update) | async-done | bytes 2228240 | tf_op jit(solution)/shard_map/all_gather | solution.py:101
  101.5 50.1 %while.73 = (s32[]{:T(128)}, f32[2,2,17,128]{3,2,1,0:T(8,128)S(1)}, f32[2,2,17,128]{3,2,1,0:T(8,128)S(1)}, s32[]{:T(128)}, s32[8]{0:T(128)S(1)}, /*index=5*/s32[...) while((s32[]{:T(128)}, f32[2,2,17,128]{3,2,1,0:T(8,128)S(1)}, ...), condition=%wide.region_14.15_spmd.clone, body=%wide.region_4.14_spmd.clone.sunk | while | flops 149341600 | bytes 13133777 | solution.py:159
  160.0 53.7 %while.74 = (s32[]{:T(128)}, f32[2,2,128,17,64]{2,4,3,0,1:T(8,128)}, s32[]{:T(128)}, s32[8]{0:T(128)S(1)}, s32[]{:T(128)}, /*index=5*/s32[]{:T(128)}, bf16[4,2,1...) while((s32[]{:T(128)}, ...), condition=%wide.region_21.22_spmd.clone, body=%wide.region_15.21_spmd.clone.sunk | while | flops 289145248 | bytes 19115960 | solution.py:184
  222.1 26.5 %all-reduce.6.cloned.1.call-done = bf16[2,256,1088]{1,2,0:T(8,128)(2,1)} async-done(((bf16[2,256,1088]{1,2,0:T(8,128)(2,1)}), bf16[2,256,1088]{1,2,0:T(8,128)(2,1)}) %all-reduce.6.cloned.1.call-update) | async-done | bytes 1114128 | tf_op jit(solution)/shard_map/psum | solution.py:185
  254.4 9.2 all-gather.19.cloned.1.call-done
  263.6 8.1 convolution_add_fusion
  275.5 10.0 convert_reduce_fusion
  298.5 9.7 reduce-scatter.24.cloned.1.call-done
  320.4 8.2 all-gather.23.cloned.1.call-done
  338.9 86.7 %while.75 = (s32[]{:T(128)}, f32[2,2,128,17,64]{2,4,3,0,1:T(8,128)}, bf16[4,2,128,2176]{2,3,1,0:T(8,128)(2,1)}, s32[]{:T(128)}, s32[8]{0:T(128)S(1)}, /*index=5*...) while((s32[]{:T(128)}, ...), condition=%wide.region_37.38_spmd.clone, body=%wide.region_30.0_spmd.clone.sunk | while | flops 725877120 | bytes 83950944 | solution.py:302
  354.3 6.0 conditional.23
  392.6 6.0 conditional.23
  414.7 6.0 conditional.23
  433.6 6.6 fusion.83
  454.8 81.6 %reduce-scatter.16.cloned.1.call-done = bf16[1,2,128,2176]{2,3,1,0:T(8,128)(2,1)} async-done(((bf16[4,2,128,2176]{2,3,1,0:T(8,128)(2,1)}), bf16[1,2,128,2176]{2,3,1,0:T(8,128)(2,1)}) %reduce-scatter.16.cloned.1.call-update) | async-done | bytes 1114128 | tf_op jit(solution)/shard_map/reduce_scatter | solution.py:309
  536.4 5.5 fusion.125
  551.0 6.8 convolution_bitcast_fusion.8
  557.9 9.0 convolution_bitcast_fusion.7
  575.9 16.8 %reduce-scatter.18.cloned.1.call-done = bf16[544,3264]{1,0:T(8,128)(2,1)} async-done(((bf16[1088,3264]{1,0:T(8,128)(2,1)}), bf16[544,3264]{1,0:T(8,128)(2,1)}) %reduce-scatter.18.cloned.1.call-update) | async-done | bytes 3551248 | tf_op jit(solution)/shard_map/reduce_scatter | solution.py:345
  592.7 734.4 %all-reduce.9 = (f32[8,544]{1,0:T(8,128)S(1)}, f32[544,3264]{1,0:T(8,128)}, f32[544,1088]{1,0:T(8,128)}, f32[2176]{0:T(1024)}) all-reduce(bf16[8,544]{1,0:T(8,128)(2,1)S(1)} %copy.65, bf16[544,3264]{1,0:T(8,128)(2,1)} %reduce-scatter.18.cloned.1.call-done, ...), channel_id=1, replica_groups=mesh['dp'=4,'ctx'=4,'wt'=2] {'dp','ctx'}, use_global_device_ids=true, to_apply=%region_51.52 | all-reduce | flops 2374016 | bytes 14248448 | tf_op jit(solution)/shard_map/psum | solution.py:355
  1327.7 95.6 %all-reduce.8.cloned.1.call-done = (f32[1088,2176]{1,0:T(8,128)}, f32[2176,1088]{0,1:T(8,128)}) async-done(((f32[1088,2176]{1,0:T(8,128)}, f32[2176,1088]{0,1:T(8,128)}), (f32[1088,2176]{1,0:T(8,128)}, f32[2176,1088]{0,1:T(8,128)})) %all-reduce.8.cloned.1.call-update) | async-done | bytes 18939920 | tf_op jit(solution)/shard_map/psum | solution.py:355
  1423.3 8.7 copy.158
  (518 shorter events, 302.4 us)
Async XLA Ops:
  7.2 23.3 %all-gather.13.cloned.1.call-start = ((), (), s32[]{:S(2)}) async-start(), calls=%async_computation.7 | async-start | bytes 10862592 | tf_op jit(solution)/shard_map/all_gather | solution.py:87
  8.0 41.8 %all-gather.15.cloned.1.call-start = ((), (), s32[]{:S(2)}) async-start(), calls=%async_computation.8 | async-start | bytes 1671168 | tf_op jit(solution)/shard_map/all_gather | solution.py:99
  8.0 29.1 %copy-start.28 = (f32[1088]{0:T(1024)}, f32[1088]{0:T(1024)S(1)}, u32[]{:S(2)}) copy-start(f32[1088]{0:T(1024)S(1)} %convert_element_type.222) | copy-start | bytes 13060
  8.1 29.1 %copy-start.30 = (f32[1088]{0:T(1024)}, f32[1088]{0:T(1024)S(1)}, u32[]{:S(2)}) copy-start(f32[1088]{0:T(1024)S(1)} %convert_element_type.223) | copy-start | bytes 13060
  8.5 28.7 %copy-start.32 = (f32[2,128]{1,0:T(2,128)}, f32[2,128]{1,0:T(2,128)S(1)}, u32[]{:S(2)}) copy-start(f32[2,128]{1,0:T(2,128)S(1)} %broadcast_multiply_fusion.2) | copy-start | bytes 3076
  39.4 62.1 %all-gather.25.cloned.1.call-start = ((), (), s32[]{:S(2)}) async-start(), calls=%async_computation.17 | async-start | bytes 2785280 | tf_op jit(solution)/shard_map/all_gather | solution.py:101
  41.6 116.8 %all-gather.27.cloned.1.call-start = ((), (), s32[]{:S(2)}) async-start(), calls=%async_computation.18 | async-start | bytes 2785280 | tf_op jit(solution)/shard_map/all_gather | solution.py:102
  42.1 180.0 %all-gather.17.cloned.1.call-start = ((), (), s32[]{:S(2)}) async-start(), calls=%async_computation.10 | async-start | bytes 3760128 | tf_op jit(solution)/shard_map/all_gather | solution.py:88
  42.7 205.9 %all-reduce.6.cloned.1.call-start = ((), (), s32[]{:S(2)}) async-start(), calls=%async_computation.9 | async-start | bytes 2228224 | tf_op jit(solution)/shard_map/psum | solution.py:185
  221.4 42.1 %all-gather.19.cloned.1.call-start = ((), (), s32[]{:S(2)}) async-start(), calls=%async_computation.11 | async-start | bytes 1671168 | tf_op jit(solution)/shard_map/all_gather | solution.py:199
  251.7 62.8 %copy-start.7 = (f32[2,128,1088]{1,2,0:T(8,128)}, f32[2,128,1088]{1,2,0:T(8,128)S(1)}, u32[]{:S(2)}) copy-start(f32[2,128,1088]{1,2,0:T(8,128)S(1)} %get-tuple-element.2498) | copy-start | bytes 3342340
  253.1 22.3 %all-gather.21.cloned.1.call-start = ((), (), s32[]{:S(2)}) async-start(), calls=%async_computation.12 | async-start | bytes 1671168 | tf_op jit(solution)/shard_map/all_gather | solution.py:212
  253.9 54.4 %reduce-scatter.24.cloned.1.call-start = ((), (), s32[]{:S(2)}) async-start(), calls=%async_computation.20 | async-start | bytes 1671168
  298.3 30.4 %all-gather.23.cloned.1.call-start = ((), (), s32[]{:S(2)}) async-start(), calls=%async_computation.13 | async-start | bytes 1671168 | tf_op jit(solution)/shard_map/all_gather | solution.py:238
  318.3 133.1 %reduce-scatter.26.cloned.1.call-start = ((), (), s32[]{:S(2)}) async-start(), calls=%async_computation.21 | async-start | bytes 1671168
  433.0 103.4 %reduce-scatter.16.cloned.1.call-start = ((), (), s32[]{:S(2)}) async-start(), calls=%async_computation.14 | async-start | bytes 5570560 | tf_op jit(solution)/shard_map/reduce_scatter | solution.py:309
  433.6 134.0 %reduce-scatter.22.cloned.1.call-start = ((), (), s32[]{:S(2)}) async-start(), calls=%async_computation.19 | async-start | bytes 1671168
  443.7 128.0 %reduce-scatter.20.cloned.1.call-start = ((), (), s32[]{:S(2)}) async-start(), calls=%async_computation.16 | async-start | bytes 3760128 | tf_op jit(solution)/shard_map/reduce_scatter | solution.py:348
  447.3 127.6 %reduce-scatter.28.cloned.1.call-start = ((), (), s32[]{:S(2)}) async-start(), calls=%async_computation.22 | async-start | bytes 417792
  453.5 82.9 %copy-start.10 = (bf16[2,128,1088]{1,2,0:T(8,128)(2,1)S(1)}, bf16[2,128,1088]{1,2,0:T(8,128)(2,1)}, u32[]{:S(2)}) copy-start(bf16[2,128,1088]{1,2,0:T(8,128)(2,1)} %param.52) | copy-start | bytes 1671172
  453.5 82.9 %copy-start.29 = (f32[1088]{0:T(1024)S(1)}, f32[1088]{0:T(1024)}, u32[]{:S(2)}) copy-start(f32[1088]{0:T(1024)} %copy-done.28) | copy-start | bytes 13060
  453.6 82.8 %copy-start.33 = (f32[2,128]{1,0:T(2,128)S(1)}, f32[2,128]{1,0:T(2,128)}, u32[]{:S(2)}) copy-start(f32[2,128]{1,0:T(2,128)} %copy-done.32) | copy-start | bytes 3076
  544.8 47.9 %reduce-scatter.18.cloned.1.call-start = ((), (), s32[]{:S(2)}) async-start(), calls=%async_computation.15 | async-start | bytes 10862592 | tf_op jit(solution)/shard_map/reduce_scatter | solution.py:345
  549.8 873.5 %all-reduce.8.cloned.1.call-start = ((), (), s32[]{:S(2)}) async-start(), calls=%async_computation.23 | async-start | bytes 37879808 | tf_op jit(solution)/shard_map/psum | solution.py:355
  (70 other events, 201.3 us)
Sparse Core Ops, SparseCore 0:
  9.6 20.8 all-gather.12
  39.5 10.2 all-gather.14
  51.9 49.5 all-gather.24
  103.5 47.1 all-gather.26
  152.0 9.9 all-gather.16
  221.6 27.0 all-reduce.5
  253.3 10.2 all-gather.18
  265.2 10.2 all-gather.20
  298.4 9.7 reduce-scatter.23
  318.4 10.2 all-gather.22
  433.1 18.2 reduce-scatter.25
  454.2 82.1 reduce-scatter.15
  538.7 9.1 reduce-scatter.21
  550.6 11.2 reduce-scatter.19
  564.0 8.9 reduce-scatter.27
  575.7 16.8 reduce-scatter.17
  599.5 823.7 all-reduce.7
where the time goes:
time: 1460 us; the launch traced here: 1440 us
  blocking collectives  741 us (51%)
  waiting for transfers between devices  330 us (23%)
  local copies, waits for them, and re-layouts  159 us (11%)
  matrix products  103 us (7%)
  other arithmetic  50.8 us (3%)
  loops' own time  40.7 us (3%)
  between operations  16.5 us (1%)
    psum x1, blocking collectives, local(): lax.psum((qkv_shard, proj_shard, small_shard, grad_w_up, grad_up_bias, gr...  734 us
    psum x1, waiting for transfers between devices, local(): lax.psum((qkv_shard, proj_shard, small_shard, grad_w_up, grad_up_bias, gr...  95.6 us
    reduce_scatter x1, waiting for transfers between devices, local(): lax.psum_scatter(pair_grad.astype(jnp.bfloat16), 'ctx', scatter_dimension...  81.6 us
    unnamed x105, local copies, waits for them, and re-layouts  50.6 us
    all_gather x1, waiting for transfers between devices, local(): lax.all_gather(keys[None], 'ctx', axis=0, tiled=True)  46.5 us
  transfers between devices with their start and end apart: 17, of which 12 were waited for; matrix products, arithmetic and copies ran while one was open for 11% of the time, Pallas kernels for 0%

commit v1 on v0

v1 whole, which is shorter than its diff:
```python
import math

import jax
import jax.numpy as jnp
from jax import lax
from jax.experimental import pallas as pl
from jax.experimental.layout import Layout, with_layout_constraint
from jax.experimental.pallas import tpu as pltpu
from jax.sharding import PartitionSpec as P

HEADS = 17

epsilon = 1e-05
masked_value = -1e30
low_type = jnp.bfloat16
full_type = jnp.float32


def wide(array):
    return array.astype(full_type)


def layer_norm(values, gain, offset):
    average = jnp.mean(values, axis=-1, keepdims=True)
    shifted = values - average
    variance = jnp.mean(shifted * shifted, axis=-1, keepdims=True)
    return shifted * lax.rsqrt(variance + epsilon) * gain + offset


def gelu_tanh(values):
    return jax.nn.gelu(values, approximate=True)


def contract(first, second, first_dim, second_dim):
    return lax.dot_general(
        first, second, (((first_dim,), (second_dim,)), ((), ())), preferred_element_type=full_type
    )


def repeat(start, stop, body, carry):
    if isinstance(start, int) and isinstance(stop, int) and stop - start <= 4:
        for index in range(start, stop):
            carry = body(index, carry)
        return carry
    return lax.fori_loop(start, stop, body, carry)


def pair_of(ref, index):
    return jnp.concatenate([ref[2 * index], ref[2 * index + 1]], axis=-1)


def put_pair(ref, index, tile):
    half = tile.shape[-1] // 2
    ref[2 * index] = tile[:, :half].astype(ref.dtype)
    ref[2 * index + 1] = tile[:, half:].astype(ref.dtype)


def causal(scores):
    key_at = lax.broadcasted_iota(jnp.int32, scores.shape, 0)
    query_at = lax.broadcasted_iota(jnp.int32, scores.shape, 1)
    return jnp.where(key_at <= query_at, scores, masked_value)


def forward_kernel(ranks, mixed_ref, out_ref, lse_ref, queries, keys, values, outs):
    count = mixed_ref.shape[0]
    block = mixed_ref.shape[-1] // 2
    for piece in range(count):
        for half in range(2):
            rank = ranks[2 * piece + half]
            span = slice(half * block, (half + 1) * block)
            queries[rank] = mixed_ref[piece, 0, 0, :, span]
            keys[rank] = mixed_ref[piece, 1, 0, :, span]
            values[rank] = mixed_ref[piece, 2, 0, :, span]

    def query_tile(at, unused):
        query = pair_of(queries, at)

        def scores_at(key_at, diagonal=False):
            scores = contract(pair_of(keys, key_at), query, 0, 0)
            return causal(scores) if diagonal else scores

        def key_tile(key_at, carry, diagonal=False):
            highest, total, accum = carry
            scores = scores_at(key_at, diagonal)
            new_highest = jnp.maximum(highest, jnp.max(scores, axis=0, keepdims=True))
            probs = jnp.exp(scores - new_highest)
            shrink = jnp.exp(highest - new_highest)
            total = total * shrink + jnp.sum(probs, axis=0, keepdims=True)
            accum = accum * shrink + contract(
                pair_of(values, key_at), probs.astype(low_type), 1, 0
            )
            return new_highest, total, accum

        if isinstance(at, int):
            tiles = [scores_at(key_at, key_at == at) for key_at in range(at + 1)]
            highest = jnp.max(tiles[0], axis=0, keepdims=True)
            for tile in tiles[1:]:
                highest = jnp.maximum(highest, jnp.max(tile, axis=0, keepdims=True))
            total = jnp.zeros((1, 2 * block), full_type)
            accum = jnp.zeros(query.shape, full_type)
            for key_at, tile in enumerate(tiles):
                probs = jnp.exp(tile - highest)
                total = total + jnp.sum(probs, axis=0, keepdims=True)
                accum = accum + contract(pair_of(values, key_at), probs.astype(low_type), 1, 0)
        else:
            start = (
                jnp.full((1, 2 * block), masked_value, full_type),
                jnp.zeros((1, 2 * block), full_type),
                jnp.zeros(query.shape, full_type),
            )
            carry = lax.fori_loop(0, at, key_tile, start)
            highest, total, accum = key_tile(at, carry, True)
        put_pair(outs, at, accum / total)
        lse_ref[0, pl.ds(at, 1), :] = highest + jnp.log(total)
        return unused

    repeat(0, count, query_tile, 0)
    for piece in range(count):
        for half in range(2):
            rank = ranks[2 * piece + half]
            out_ref[piece, 0, :, half * block : (half + 1) * block] = outs[rank]


def backward_kernel(
    ranks,
    mixed_ref,
    out_ref,
    grad_ref,
    lse_ref,
    result_ref,
    queries,
    keys,
    values,
    outs,
    grads,
    query_grads,
    key_grads,
    value_grads,
    deltas,
):
    count = mixed_ref.shape[0]
    block = mixed_ref.shape[-1] // 2
    for piece in range(count):
        for half in range(2):
            rank = ranks[2 * piece + half]
            span = slice(half * block, (half + 1) * block)
            queries[rank] = mixed_ref[piece, 0, 0, :, span]
            keys[rank] = mixed_ref[piece, 1, 0, :, span]
            values[rank] = mixed_ref[piece, 2, 0, :, span]
            outs[rank] = out_ref[piece, 0, :, span]
            grads[rank] = grad_ref[piece, 0, :, span]

    def delta_tile(at, unused):
        terms = pair_of(outs, at).astype(full_type) * pair_of(grads, at).astype(full_type)
        deltas[pl.ds(at, 1), :] = jnp.sum(terms, axis=0, keepdims=True)
        zeros = jnp.zeros(query_grads.shape[1:], full_type)
        query_grads[2 * at] = zeros
        query_grads[2 * at + 1] = zeros
        return unused

    repeat(0, count, delta_tile, 0)

    def key_tile(key_at, unused):
        key = pair_of(keys, key_at)
        value = pair_of(values, key_at)

        def query_tile(at, carry, diagonal=False):
            key_grad, value_grad = carry
            query = pair_of(queries, at)
            grad = pair_of(grads, at)
            scores = contract(key, query, 0, 0)
            if diagonal:
                scores = causal(scores)
            probs = jnp.exp(scores - lse_ref[0, pl.ds(at, 1), :])
            grad_probs = contract(value, grad, 0, 0)
            grad_scores = (probs * (grad_probs - deltas[pl.ds(at, 1), :])).astype(low_type)
            value_grad = value_grad + contract(grad, probs.astype(low_type), 1, 1)
            key_grad = key_grad + contract(query, grad_scores, 1, 1)
            query_grad = contract(key, grad_scores, 1, 0)
            query_grads[2 * at] += query_grad[:, :block]
            query_grads[2 * at + 1] += query_grad[:, block:]
            return key_grad, value_grad

        start = (jnp.zeros(key.shape, full_type), jnp.zeros(key.shape, full_type))
        carry = query_tile(key_at, start, True)
        key_grad, value_grad = repeat(key_at + 1, count, query_tile, carry)
        put_pair(key_grads, key_at, key_grad)
        put_pair(value_grads, key_at, value_grad)
        return unused

    repeat(0, count, key_tile, 0)
    for piece in range(count):
        for half in range(2):
            rank = ranks[2 * piece + half]
            span = slice(half * block, (half + 1) * block)
            result_ref[piece, 0, 0, :, span] = query_grads[rank].astype(low_type)
            result_ref[piece, 1, 0, :, span] = key_grads[rank]
            result_ref[piece, 2, 0, :, span] = value_grads[rank]


def attention_forward(ranks, mixed):
    count, _, heads, depth, rows = mixed.shape
    blocks = (2 * count, depth, rows // 2)
    return pl.pallas_call(
        forward_kernel,
        out_shape=(
            jax.ShapeDtypeStruct((count, heads, depth, rows), low_type),
            jax.ShapeDtypeStruct((heads, count, rows), full_type),
        ),
        grid_spec=pltpu.PrefetchScalarGridSpec(
            num_scalar_prefetch=1,
            grid=(heads,),
            in_specs=[
                pl.BlockSpec((count, 3, 1, depth, rows), lambda head, _: (0, 0, head, 0, 0))
            ],
            out_specs=(
                pl.BlockSpec((count, 1, depth, rows), lambda head, _: (0, head, 0, 0)),
                pl.BlockSpec((1, count, rows), lambda head, _: (head, 0, 0)),
            ),
            scratch_shapes=[pltpu.VMEM(blocks, low_type) for _ in range(4)],
        ),
        compiler_params=pltpu.CompilerParams(vmem_limit_bytes=40 * 2**20),
        cost_estimate=pl.CostEstimate(flops=0, bytes_accessed=0, transcendentals=0),
    )(ranks, mixed)


def attention_backward(ranks, mixed, outs, grads, lse):
    count, _, heads, depth, rows = mixed.shape
    blocks = (2 * count, depth, rows // 2)
    three = pl.BlockSpec((count, 3, 1, depth, rows), lambda head, _: (0, 0, head, 0, 0))
    one = pl.BlockSpec((count, 1, depth, rows), lambda head, _: (0, head, 0, 0))
    return pl.pallas_call(
        backward_kernel,
        out_shape=jax.ShapeDtypeStruct(mixed.shape, low_type),
        grid_spec=pltpu.PrefetchScalarGridSpec(
            num_scalar_prefetch=1,
            grid=(heads,),
            in_specs=[
                three,
                one,
                one,
                pl.BlockSpec((1, count, rows), lambda head, _: (head, 0, 0)),
            ],
            out_specs=three,
            scratch_shapes=[pltpu.VMEM(blocks, low_type) for _ in range(5)]
            + [pltpu.VMEM(blocks, full_type)]
            + [pltpu.VMEM(blocks, low_type) for _ in range(2)]
            + [pltpu.VMEM((count, rows), full_type)],
        ),
        compiler_params=pltpu.CompilerParams(vmem_limit_bytes=40 * 2**20),
        cost_estimate=pl.CostEstimate(flops=0, bytes_accessed=0, transcendentals=0),
    )(ranks, mixed, outs, grads, lse)


def swapped(array):
    return lax.ppermute(array, "wt", [(0, 1), (1, 0)])


def part_of(array, index, size, axis=0):
    return lax.dynamic_slice_in_dim(array, index * size, size, axis)


def in_order(first, second, flip, axis):
    return jnp.where(
        flip, jnp.concatenate([second, first], axis), jnp.concatenate([first, second], axis)
    )


def scattered(send):
    count = lax.axis_size("ctx")
    place = lax.axis_index("ctx")
    pieces = []
    for shift in range(count):
        piece = lax.dynamic_index_in_dim(send, lax.rem(place + shift, count), 0, False)
        if shift:
            hops = [(one, (one + shift) % count) for one in range(count)]
            piece = lax.ppermute(piece, "ctx", hops)
        pieces.append(piece)
    return jnp.stack(pieces)


def returned(pieces, axis):
    count = lax.axis_size("ctx")
    place = lax.axis_index("ctx")
    size = pieces.shape[axis + 1]
    shape = list(pieces.shape[1:])
    shape[axis] = size * count
    result = jnp.zeros(shape, pieces.dtype)
    for shift in range(count):
        piece = pieces[shift]
        if shift:
            hops = [(one, (one - shift) % count) for one in range(count)]
            piece = lax.ppermute(piece, "ctx", hops)
        source = lax.rem(place + shift, count)
        result = lax.dynamic_update_slice_in_dim(result, piece, source * size, axis)
    return result


def dp_hops(bit):
    return [(one, one ^ (1 << bit)) for one in range(lax.axis_size("dp"))]


def reduced(array, order):
    index = lax.axis_index("dp")
    for bit in order:
        half = array.shape[0] // 2
        high = lax.rem(lax.div(index, 1 << bit), 2)
        kept = part_of(array, high, half)
        arrived = lax.ppermute(part_of(array, 1 - high, half), "dp", dp_hops(bit))
        array = (kept.astype(full_type) + arrived.astype(full_type)).astype(low_type)
    return array


def spread(array, order):
    index = lax.axis_index("dp")
    for bit in reversed(order):
        high = lax.rem(lax.div(index, 1 << bit), 2)
        arrived = lax.ppermute(array, "dp", dp_hops(bit))
        array = in_order(array, arrived, high == 1, 0)
    return array


def halves_of_all(array, axes):
    index = lax.axis_index("dp")
    half = array.shape[0] // 2
    forth = tuple(range(len(axes)))
    gathered = []
    for part, order in ((array[:half], forth), (array[half:], forth[::-1])):
        for bit in order:
            high = lax.rem(lax.div(index, 1 << bit), 2)
            arrived = lax.ppermute(part, "dp", dp_hops(bit))
            part = in_order(part, arrived, high == 1, axes[bit])
        gathered.append(part)
    return gathered


def joined(forth, back, bits):
    forth = forth.reshape((2,) * bits + (-1, forth.shape[1]))
    forth = jnp.transpose(forth, (*reversed(range(bits)), bits, bits + 1))
    return jnp.stack([forth, back.reshape(forth.shape)], axis=bits).reshape(-1, forth.shape[-1])


def row_major(array):
    return with_layout_constraint(array, Layout(major_to_minor=(0, 1)))


def tied(*arrays):
    return lax.optimization_barrier(arrays)


def small_total_over_group(array):
    for bit in range(int(math.log2(lax.axis_size("dp")))):
        array = array + lax.ppermute(array, "dp", dp_hops(bit))
    count = lax.axis_size("ctx")
    total = array
    for shift in range(1, count):
        hops = [(one, (one + shift) % count) for one in range(count)]
        total = total + lax.ppermute(array, "ctx", hops)
    return total


def local(
    hidden,
    block_order,
    ln1_gain,
    ln1_bias,
    w_qkv,
    q_bias,
    v_bias,
    w_proj,
    proj_bias,
    ln2_gain,
    ln2_bias,
    w_up,
    up_bias,
    w_down,
    down_bias,
    cotangent,
):
    seqs, seq_dev, width = hidden.shape
    depth = width // HEADS
    scale = 1.0 / math.sqrt(depth)
    count = lax.axis_size("ctx")
    place = lax.axis_index("ctx")
    core = lax.axis_index("wt")
    half_width = width // 2
    rows = 2 * seq_dev
    group = -(-HEADS // count)
    padded = group * count
    bits = int(math.log2(lax.axis_size("dp")))
    upward = tuple(range(bits))
    downward = tuple(reversed(upward))

    def by_sequence(array):
        mine = lax.dynamic_index_in_dim(array, core, 0, False)
        theirs = lax.dynamic_index_in_dim(array, 1 - core, 0, False)
        return jnp.concatenate([mine, swapped(theirs)], axis=0)

    def by_rows(array):
        mine = array[:seq_dev]
        arrived = swapped(array[seq_dev:])
        return in_order(mine[None], arrived[None], core == 1, 0)

    sources = lax.rem(place - jnp.arange(count, dtype=jnp.int32) + count, count)
    slots = jnp.stack([2 * sources + core, 2 * sources + 1 - core], axis=1).reshape(-1)
    ranks = block_order[slots]

    rows_low = by_sequence(hidden)
    other_qkv = swapped(w_qkv)
    other_proj = swapped(w_proj)
    grad_low = by_sequence(cotangent)
    grad_rows = jnp.concatenate([grad_low, swapped(grad_low)], axis=0)
    grad_rows_near = lax.ppermute(grad_rows, "dp", dp_hops(0))
    grad_act = contract(w_down, grad_rows, 1, 1)

    inputs = wide(rows_low)
    normed, norm_one_pull = jax.vjp(layer_norm, inputs, wide(ln1_gain), wide(ln1_bias))
    normed_low = normed.astype(low_type)
    normed_own = part_of(normed_low, core, half_width, 1)
    normed_other = part_of(normed_low, 1 - core, half_width, 1)
    mixed = contract(w_qkv, normed_own, 0, 1) + contract(other_qkv, normed_other, 0, 1)
    offsets = jnp.concatenate([wide(q_bias), jnp.zeros((width,), full_type), wide(v_bias)])
    scales = jnp.concatenate([jnp.full((width,), scale, full_type), jnp.ones((2 * width,), full_type)])
    mixed = ((mixed + offsets[:, None]) * scales[:, None]).astype(low_type)

    def own_half(array):
        return part_of(array, core, half_width, 1) + swapped(
            part_of(array, 1 - core, half_width, 1)
        )

    def to_heads(array):
        array = array.reshape(-1, HEADS, depth, rows)
        array = jnp.pad(array, ((0, 0), (0, padded - HEADS), (0, 0), (0, 0)))
        array = array.reshape(-1, count, group, depth, rows)
        return jnp.transpose(array, (1, 0, 2, 3, 4))

    def from_heads(array):
        array = array.reshape(-1, padded, depth, rows)
        return array[:, :HEADS].reshape(-1, rows)

    mixed_heads = scattered(to_heads(mixed))
    out_heads, lse = attention_forward(ranks, mixed_heads)
    attended = from_heads(returned(out_heads, 0))
    attended_own = part_of(attended, core, half_width)
    attended_other = part_of(attended, 1 - core, half_width)
    branch = contract(attended_own, w_proj, 0, 0) + contract(attended_other, other_proj, 0, 0)
    middle = inputs + branch + wide(proj_bias)

    normed_two, norm_two_pull = jax.vjp(layer_norm, middle, wide(ln2_gain), wide(ln2_bias))
    normed_two_low = normed_two.astype(low_type)
    rows_two = jnp.concatenate([normed_two_low, swapped(normed_two_low)], axis=0)
    index = lax.axis_index("dp")
    low_high, top_high = lax.rem(index, 2), lax.div(index, 1 << (bits - 1))
    half_units = w_down.shape[0] // 2
    rows_two_near = lax.ppermute(rows_two, "dp", dp_hops(bits - 1))
    pre_act = contract(w_up, rows_two, 0, 1) + wide(up_bias)[:, None]
    activated, gelu_pull = jax.vjp(gelu_tanh, pre_act)
    act_low = row_major(activated.astype(low_type))
    act_near = lax.ppermute(part_of(act_low, 1 - low_high, half_units), "dp", dp_hops(0))
    grad_pre = row_major(gelu_pull(grad_act)[0].astype(low_type))
    grad_pre_near = lax.ppermute(part_of(grad_pre, 1 - top_high, half_units), "dp", dp_hops(bits - 1))
    grad_up_bias = jnp.sum(wide(grad_pre), axis=1)

    back_terms = contract(grad_pre, w_up, 0, 1)
    grad_norm_two = back_terms[:rows] + wide(swapped(back_terms[rows:].astype(low_type)))
    grad_out = wide(grad_low)
    grad_down_bias = jnp.sum(grad_out, axis=0)
    grad_mid_norm, grad_ln2_gain, grad_ln2_bias = norm_two_pull(grad_norm_two)
    grad_mid = grad_out + grad_mid_norm
    grad_branch = grad_mid.astype(low_type)
    grad_proj_bias = jnp.sum(wide(grad_branch), axis=0)
    grad_attended = in_order(
        contract(w_proj, grad_branch, 1, 1).astype(low_type),
        contract(other_proj, grad_branch, 1, 1).astype(low_type),
        core == 1,
        0,
    )
    grad_heads = scattered(to_heads(grad_attended))[:, 0]

    grad_heads, act_later, grad_pre_later = tied(grad_heads, act_low, grad_pre)
    grad_w_down = contract(part_of(act_later, low_high, half_units), grad_rows, 1, 0) + contract(
        act_near, grad_rows_near, 1, 0
    )
    grad_w_up = contract(rows_two, part_of(grad_pre_later, top_high, half_units), 0, 1) + contract(
        rows_two_near, grad_pre_near, 0, 1
    )
    grad_w_down = row_major(grad_w_down.astype(low_type))
    grad_w_up = row_major(grad_w_up.astype(low_type))
    grad_heads, grad_w_down, grad_w_up = tied(grad_heads, grad_w_down, grad_w_up)
    down_share = reduced(grad_w_down, upward[1:])
    up_share = reduced(grad_w_up, downward[1:])

    grad_mixed_heads = attention_backward(ranks, mixed_heads, out_heads, grad_heads, lse)
    (grad_mixed_heads, act_late, attended_late, branch_late, down_share, up_share) = tied(
        grad_mixed_heads, act_low, attended_other, grad_branch, down_share, up_share
    )
    down_share, up_share = lax.psum((down_share, up_share), "ctx")
    grad_mixed = from_heads(returned(grad_mixed_heads, 1))
    query_rows = lax.broadcasted_iota(jnp.int32, (3 * width, 1), 0) < width
    grad_mixed = jnp.where(query_rows, grad_mixed * low_type(scale), grad_mixed)
    grad_mixed_sums = jnp.sum(wide(grad_mixed), axis=1)

    down_terms = contract(act_late, w_down, 0, 0)
    mlp_sum = down_terms[:rows] + wide(swapped(down_terms[rows:].astype(low_type)))
    output = by_rows((middle + mlp_sum + wide(down_bias)).astype(low_type))

    attended_both = jnp.concatenate([attended_own, swapped(attended_late)], axis=1)
    branch_both = jnp.concatenate([branch_late, swapped(branch_late)], axis=0)
    grad_w_proj = contract(attended_both, branch_both, 1, 0)
    proj_share = reduced(row_major(grad_w_proj.astype(low_type)), downward)

    small_early = own_half(
        jnp.stack(
            [
                grad_mixed_sums[:width],
                grad_mixed_sums[2 * width :],
                grad_proj_bias,
                grad_ln2_gain,
                grad_ln2_bias,
                grad_down_bias,
            ]
        )
    )
    wide_rows = -(-grad_up_bias.shape[0] // half_width)
    up_bias_rows = jnp.pad(grad_up_bias, (0, wide_rows * half_width - grad_up_bias.shape[0]))
    small_early = jnp.concatenate([small_early, up_bias_rows.reshape(wide_rows, half_width)])

    normed_both = jnp.concatenate([normed_own, swapped(normed_other)], axis=0)
    grad_mixed_both = jnp.concatenate([grad_mixed, swapped(grad_mixed)], axis=1)
    grad_w_qkv = contract(normed_both, grad_mixed_both, 0, 1)
    grad_w_qkv = row_major(grad_w_qkv.astype(low_type))
    first_share = reduced(grad_w_qkv[:, : 2 * width], upward)
    second_share = reduced(grad_w_qkv[:, 2 * width :], downward)

    (down_share, up_share, first_share, second_share, proj_share, small_later) = tied(
        down_share, up_share, first_share, second_share, proj_share, small_early
    )
    down_total = wide(joined(*halves_of_all(down_share, (0,) * bits), bits))
    up_total = wide(joined(*halves_of_all(up_share, (0,) * (bits - 1) + (1,)), bits - 1))
    first_share, second_share, proj_share = lax.psum((first_share, second_share, proj_share), "ctx")
    qkv_total = jnp.concatenate(
        [wide(spread(first_share, upward)), wide(spread(second_share, downward))], axis=1
    )
    proj_total = wide(spread(proj_share, downward))

    grad_norm_one = in_order(
        contract(grad_mixed, w_qkv, 0, 1), contract(grad_mixed, other_qkv, 0, 1), core == 1, 1
    )
    grad_in_norm, grad_ln1_gain, grad_ln1_bias = norm_one_pull(grad_norm_one)
    grad_hidden = by_rows((grad_mid + grad_in_norm).astype(low_type))

    small_rows = jnp.stack([grad_ln1_gain, grad_ln1_bias])
    small_own = own_half(small_rows)
    small_total = small_total_over_group(jnp.concatenate([small_own, small_later]))
    up_bias_total = small_total[8:].reshape(-1)[: grad_up_bias.shape[0]]
    return (
        output,
        grad_hidden,
        small_total[0],
        small_total[1],
        qkv_total,
        small_total[2],
        small_total[3],
        proj_total,
        small_total[4],
        small_total[5],
        small_total[6],
        up_total,
        up_bias_total,
        down_total,
        small_total[7],
    )


def solution(mesh):
    placed = (
        P("dp", ("ctx", "wt"), None),
        P(),
        P(),
        P(),
        P("wt", None),
        P(),
        P(),
        P("wt", None),
        P(),
        P(),
        P(),
        P(None, "wt"),
        P("wt"),
        P("wt", None),
        P(),
        P("dp", ("ctx", "wt"), None),
    )
    return jax.shard_map(
        local,
        mesh=mesh,
        in_specs=placed,
        out_specs=(
            P("dp", ("ctx", "wt"), None),
            P("dp", ("ctx", "wt"), None),
            P("wt"),
            P("wt"),
            P("wt", None),
            P("wt"),
            P("wt"),
            P("wt", None),
            P("wt"),
            P("wt"),
            P("wt"),
            P(None, "wt"),
            P("wt"),
            P("wt", None),
            P("wt"),
        ),
        check_vma=False,
    )
```

time: 1460 us -> 573 us (0.39)
  blocking collectives: 741 us -> 0 us
  local copies, waits for them, and re-layouts: 159 us -> 38.3 us
  starting transfers between devices: 1.27 us -> 72.3 us
  waiting for transfers between devices: 330 us -> 280 us
  loops' own time: 40.7 us -> 0 us
  matrix products: 103 us -> 67.6 us
  Pallas kernels: 0 us -> 24.8 us
  other arithmetic: 50.8 us -> 66.8 us
    psum x1 -> x0, blocking collectives: 734 us -> none  [local(): lax.psum((qkv_shard, proj_shard, small_shard, grad_w_up, grad_up_bias, gr...]
    ppermute x0 -> x59, waiting for transfers between devices: none -> 234 us  [the longest x6 61.8 us: scattered(): piece = lax.ppermute(piece, 'ctx', hops)]
    reduce_scatter x3 -> x0, waiting for transfers between devices: 98.4 us -> none  [the longest x1 81.6 us: local(): lax.psum_scatter(pair_grad.astype(jnp.bfloat16), 'ctx', scatter_dimension...]
    all_gather x8 -> x0, waiting for transfers between devices: 94.5 us -> none  [the longest x1 46.5 us: local(): lax.all_gather(keys[None], 'ctx', axis=0, tiled=True)]
    psum x2, waiting for transfers between devices: 122 us -> 45.4 us  [the longest x1 28.6 us: local(): lax.psum((first_share, second_share, proj_share), 'ctx')]
    ppermute x0 -> x59, starting transfers between devices: none -> 72 us  [the longest x3 23.6 us: small_total_over_group(): total = total + lax.ppermute(array, 'ctx', hops)]
    another operation x27 -> x0, loops' own time: 40.7 us -> none  [the longest x1 13.6 us: local(): lax.fori_loop(0, ctx_count, backward_step, (start_query, start_pair))]
    unnamed x105 -> x127, local copies, waits for them, and re-layouts: 50.6 us -> 14.8 us
  transfers between devices with their start and end apart: 17 -> 61, of which waited for: 12 -> 29; matrix products, arithmetic and copies ran while one was open for 11% -> 27% of each run, Pallas kernels for 0% -> 4%
where the time goes in v1:
time: 573 us; the launch traced here: 565 us
  waiting for transfers between devices  280 us (49%)
  starting transfers between devices  72.3 us (13%)
  matrix products  67.6 us (12%)
  other arithmetic  66.8 us (12%)
  local copies, waits for them, and re-layouts  38.3 us (7%)
  Pallas kernels  24.8 us (4%)
  between operations  15.8 us (3%)
    dot_general x18, matrix products, contract(): lax.dot_general(first, second, (((first_dim,), (second_dim,)), ((), ())),...  67.6 us
    ppermute x6, waiting for transfers between devices, scattered(): piece = lax.ppermute(piece, 'ctx', hops)  61.8 us
    ppermute x6, waiting for transfers between devices, returned(): piece = lax.ppermute(piece, 'ctx', hops)  47.6 us
    ppermute x8, waiting for transfers between devices, reduced(): arrived = lax.ppermute(part_of(array, 1 - high, half), 'dp', dp_hops(bit))  45.6 us
    ppermute x6, waiting for transfers between devices, spread(): arrived = lax.ppermute(array, 'dp', dp_hops(bit))  44.8 us
    psum x1, waiting for transfers between devices, local(): lax.psum((first_share, second_share, proj_share), 'ctx')  28.6 us
    select_n x16, other arithmetic, in_order(): jnp.where(flip, jnp.concatenate([second, first], axis), jnp.concatenate([...  23.7 us
    ppermute x3, starting transfers between devices, small_total_over_group(): total = total + lax.ppermute(array, 'ctx', hops)  23.6 us
  transfers between devices with their start and end apart: 61, of which 29 were waited for; matrix products, arithmetic and copies ran while one was open for 27% of the time, Pallas kernels for 4%

profile of v1, /device:TPU:0, one launch (start us, length us, event | category | flops | bytes accessed | tf_op | source)
XLA Modules:
  0.0 565.1 jit_solution(9778884636858227146)
XLA Ops:
  32.1 10.0 %collective-permute-done.4 = bf16[3,5,64,256]{3,2,1,0:T(8,128)(2,1)S(1)} collective-permute-done((bf16[3,5,64,256]{3,2,1,0:T(8,128)(2,1)}, bf16[3,5,64,256]{3,2,1,0:T(8,128)(2,1)S(1)}, u32[]{:S(2)}, u32[]{:S(2)}) %collective-permute-start.4) | collective-permute-done | bytes 491552 | tf_op jit(solution)/shard_map/ppermute | solution.py:277
  42.1 30.5 %collective-permute-done.3 = bf16[3,5,64,256]{3,2,1,0:T(8,128)(2,1)S(1)} collective-permute-done((bf16[3,5,64,256]{3,2,1,0:T(8,128)(2,1)S(1)}, bf16[3,5,64,256]{3,2,1,0:T(8,128)(2,1)S(1)}, u32[]{:S(2)}, u32[]{:S(2)}) %collective-permute-start.3) | collective-permute-done | bytes 491552 | tf_op jit(solution)/shard_map/ppermute | solution.py:277
  75.0 9.7 %shard_map.271 = (bf16[4,5,64,256]{3,2,1,0:T(8,128)(2,1)S(1)}, f32[5,4,256]{2,1,0:T(4,128)S(1)}) custom-call(s32[8]{0:T(128)S(1)} %gather_fusion, bf16[4,3,5,64,256]{4,3,2,1,0:T(8,128)(2,1)S(1)} %pad_maximum_fusion.1.mixed_ref), custom_call_target="tpu_custom_call" | custom-call | tf_op jit(solution)/shard_map/pallas_call | solution.py:204
  90.8 11.5 %collective-permute-done.6 = bf16[5,64,256]{2,1,0:T(8,128)(2,1)S(1)} collective-permute-done((bf16[5,64,256]{2,1,0:T(8,128)(2,1)S(1)}, bf16[5,64,256]{2,1,0:T(8,128)(2,1)S(1)}, u32[]{:S(2)}, u32[]{:S(2)}) %collective-permute-start.6) | collective-permute-done | bytes 163872 | tf_op jit(solution)/shard_map/ppermute | solution.py:293
  112.6 7.0 %multiply_convert_fusion = (bf16[2176,512]{1,0:T(8,128)(2,1)S(1)}, f32[2176,512]{1,0:T(8,128)S(1)}) fusion(f32[2176]{0:T(1024)S(1)} %convert_element_type.208, bf16[1088,2176]{1,0:T(8,128)(2,1)} %param.27, bf16[256,1088]{0,1:T(8,128)(2,1)} %collective-permute-done.11, bf16[256,1088]{0,1:T(8,128)(2,1)S(1)} %add_convert_fusion.7), kind=kOutput, calls=%fused_computation.26 | convolution fusion | flops 2437677056 | bytes 12542464 | tf_op jit(solution)/shard_map/dot_general | solution.py:35
  119.6 8.7 %convert_reduce_fusion = (f32[2176]{0:T(1024)S(1)}, bf16[2176,512]{1,0:T(8,128)(2,1)S(1)}) fusion(f32[2176,512]{1,0:T(8,128)S(1)} %get-tuple-element.131, bf16[2176,1088]{0,1:T(8,128)(2,1)S(1)} %bitcast.141, bf16[256,1088]{0,1:T(8,128)(2,1)} %collective-permute-done.10, bf16[128,1088]{0,1:T(8,128)(2,1)} %collective-permute-done.9, ...), kind=kOutput, calls=%fused_computation.25 | convolution fusion | flops 2452158464 | bytes 12542464 | tf_op jit(solution)/shard_map/dot_general | solution.py:35
  151.7 9.2 %collective-permute-done.14 = bf16[1,5,64,256]{3,2,1,0:T(8,128)(2,1)S(1)} collective-permute-done((bf16[1,5,64,256]{3,2,1,0:T(8,128)(2,1)S(1)}, bf16[1,5,64,256]{3,2,1,0:T(8,128)(2,1)S(1)}, u32[]{:S(2)}, u32[]{:S(2)}) %collective-permute-start.14) | collective-permute-done | bytes 163872 | tf_op jit(solution)/shard_map/ppermute | solution.py:277
  161.3 7.5 %collective-permute-done.13 = bf16[1,5,64,256]{3,2,1,0:T(8,128)(2,1)S(1)} collective-permute-done((bf16[1,5,64,256]{3,2,1,0:T(8,128)(2,1)S(1)}, bf16[1,5,64,256]{3,2,1,0:T(8,128)(2,1)S(1)}, u32[]{:S(2)}, u32[]{:S(2)}) %collective-permute-start.13) | collective-permute-done | bytes 163872 | tf_op jit(solution)/shard_map/ppermute | solution.py:277
  170.6 14.0 %collective-permute-done.19 = bf16[1088,512]{1,0:T(8,128)(2,1)} collective-permute-done((bf16[1088,512]{1,0:T(8,128)(2,1)}, bf16[1088,512]{1,0:T(8,128)(2,1)}, u32[]{:S(2)}, u32[]{:S(2)}) %collective-permute-start.19) | collective-permute-done | bytes 1114144 | tf_op jit(solution)/shard_map/ppermute | solution.py:461
  205.0 15.1 %shard_map.272 = bf16[4,3,5,64,256]{4,3,2,1,0:T(8,128)(2,1)S(1)} custom-call(s32[8]{0:T(128)S(1)} %gather_fusion, bf16[4,3,5,64,256]{4,3,2,1,0:T(8,128)(2,1)S(1)} %pad_maximum_fusion.1.mixed_ref, bf16[4,5,64,256]{3,2,1,0:T(8,128)(2,1)S(1)} %get-tuple-element.35.out_ref, bf16[4,5,64,256]{3,2,1,0:T(8,128)(2,1)S(1)} %maximum_bitcast_fusion.grad_ref, ...), custom_call_target="tpu_custom_call" | custom-call | tf_op jit(solution)/shard_map/pallas_call | solution.py:232
  220.1 9.5 %collective-permute-done.21 = bf16[544,1088]{1,0:T(8,128)(2,1)} collective-permute-done((bf16[544,1088]{1,0:T(8,128)(2,1)}, bf16[544,1088]{1,0:T(8,128)(2,1)}, u32[]{:S(2)}, u32[]{:S(2)}) %collective-permute-start.21) | collective-permute-done | bytes 1183776 | tf_op jit(solution)/shard_map/ppermute | solution.py:309
  237.3 6.5 %fusion.75 = f32[512,1088]{0,1:T(8,128)} fusion(bf16[2176,1088]{0,1:T(8,128)(2,1)} %param.29, bf16[2176,512]{1,0:T(8,128)(2,1)S(1)} %copy-done.33), kind=kOutput, calls=%fused_computation.221 | convolution fusion | flops 2424307712 | bytes 9191424 | tf_op jit(solution)/shard_map/dot_general | solution.py:35
  247.4 17.2 %collective-permute-done.24 = bf16[3,5,64,256]{3,2,1,0:T(8,128)(2,1)S(1)} collective-permute-done((bf16[3,5,64,256]{3,2,1,0:T(8,128)(2,1)}, bf16[3,5,64,256]{3,2,1,0:T(8,128)(2,1)S(1)}, u32[]{:S(2)}, u32[]{:S(2)}) %collective-permute-start.24) | collective-permute-done | bytes 491552 | tf_op jit(solution)/shard_map/ppermute | solution.py:293
  268.3 15.3 %collective-permute-done.26 = bf16[3,5,64,256]{3,2,1,0:T(8,128)(2,1)S(1)} collective-permute-done((bf16[3,5,64,256]{3,2,1,0:T(8,128)(2,1)}, bf16[3,5,64,256]{3,2,1,0:T(8,128)(2,1)S(1)}, u32[]{:S(2)}, u32[]{:S(2)}) %collective-permute-start.26) | collective-permute-done | bytes 491552 | tf_op jit(solution)/shard_map/ppermute | solution.py:293
  312.7 9.2 %collective-permute-done.37 = bf16[272,1088]{1,0:T(8,128)(2,1)S(1)} collective-permute-done((bf16[272,1088]{1,0:T(8,128)(2,1)S(1)}, bf16[272,1088]{1,0:T(8,128)(2,1)S(1)}, u32[]{:S(2)}, u32[]{:S(2)}) %collective-permute-start.37) | collective-permute-done | bytes 591904 | tf_op jit(solution)/shard_map/ppermute | solution.py:309
  323.2 11.6 %collective-permute-done.33 = bf16[272,1088]{1,0:T(8,128)(2,1)S(1)} collective-permute-done((bf16[272,1088]{1,0:T(8,128)(2,1)S(1)}, bf16[272,1088]{1,0:T(8,128)(2,1)S(1)}, u32[]{:S(2)}, u32[]{:S(2)}) %collective-permute-start.33) | collective-permute-done | bytes 591904 | tf_op jit(solution)/shard_map/ppermute | solution.py:309
  355.5 16.7 %all-reduce.9.cloned.1.call-done = (bf16[544,1088]{1,0:T(8,128)(2,1)}, bf16[544,1088]{1,0:T(8,128)(2,1)}) async-done(((bf16[544,1088]{1,0:T(8,128)(2,1)}, bf16[544,1088]{1,0:T(8,128)(2,1)}), (bf16[544,1088]{1,0:T(8,128)(2,1)}, bf16[544,1088]{1,0:T(8,128)(2,1)})) %all-reduce.9.cloned.1.call-update) | async-done | bytes 2367504 | tf_op jit(solution)/shard_map/psum | solution.py:497
  380.4 7.0 %collective-permute-start.44 = (f32[12,544]{1,0:T(8,128)S(1)}, f32[12,544]{1,0:T(8,128)S(1)}, u32[]{:S(2)}, u32[]{:S(2)}) collective-permute-start(f32[12,544]{1,0:T(8,128)S(1)} %add.418), channel_id=1, source_target_pairs={{0,6},{2,0},{4,2},{6,4},{1,7},{3,1},{5,3},{7,5},{8,14},{10,8},{12,... | collective-permute-start | bytes 78344 | tf_op jit(solution)/shard_map/ppermute | solution.py:358
  387.4 14.4 %collective-permute-start.43 = (f32[12,544]{1,0:T(8,128)S(1)}, f32[12,544]{1,0:T(8,128)S(1)}, u32[]{:S(2)}, u32[]{:S(2)}) collective-permute-start(f32[12,544]{1,0:T(8,128)S(1)} %add.418), channel_id=1, source_target_pairs={{0,4},{2,6},{4,0},{6,2},{1,5},{3,7},{5,1},{7,3},{8,12},{10,14},{12... | collective-permute-start | bytes 78344 | tf_op jit(solution)/shard_map/ppermute | solution.py:358
  412.1 11.5 %collective-permute-done.53 = bf16[272,1088]{1,0:T(8,128)(2,1)} collective-permute-done((bf16[272,1088]{1,0:T(8,128)(2,1)}, bf16[272,1088]{1,0:T(8,128)(2,1)}, u32[]{:S(2)}, u32[]{:S(2)}) %collective-permute-start.53) | collective-permute-done | bytes 591904 | tf_op jit(solution)/shard_map/ppermute | solution.py:331
  427.0 28.6 %all-reduce.7.cloned.1.call-done = (bf16[136,1088]{1,0:T(8,128)(2,1)}, bf16[136,2176]{1,0:T(8,128)(2,1)}, bf16[136,1088]{1,0:T(8,128)(2,1)}) async-done(((bf16[136,1088]{1,0:T(8,128)(2,1)}, bf16[136,2176]{1,0:T(8,128)(2,1)}, bf16[136,1088]{1,0:T(8,128)(2,1)}), (bf16[136,1088]{1,0:T(8,128)(2,1)}, bf16[136,2176]{1,0:T(8,128)(2,1)}, bf16[136,1088]{1,0:T(8,128)(2,1)})) %all-reduce.7.cloned.1.call-update) | async-done | bytes 1183760 | tf_op jit(solution)/shard_map/psum | solution.py:540
  467.8 31.0 %collective-permute-done.49 = bf16[136,1088]{1,0:T(8,128)(2,1)S(1)} collective-permute-done((bf16[136,1088]{1,0:T(8,128)(2,1)S(1)}, bf16[136,1088]{1,0:T(8,128)(2,1)S(1)}, u32[]{:S(2)}, u32[]{:S(2)}) %collective-permute-start.49) | collective-permute-done | bytes 295968 | tf_op jit(solution)/shard_map/ppermute | solution.py:318
  504.7 10.5 %collective-permute-done.45 = bf16[136,2176]{1,0:T(8,128)(2,1)S(1)} collective-permute-done((bf16[136,2176]{1,0:T(8,128)(2,1)S(1)}, bf16[136,2176]{1,0:T(8,128)(2,1)S(1)}, u32[]{:S(2)}, u32[]{:S(2)}) %collective-permute-start.45) | collective-permute-done | bytes 591904 | tf_op jit(solution)/shard_map/ppermute | solution.py:318
  534.9 12.1 %copy.41 = f32[2176,1088]{0,1:T(8,128)} copy(f32[2176,1088]{1,0:T(8,128)} %bitcast_convert_fusion) | data formatting | bytes 18939904
  (386 shorter events, 224.7 us)
Async XLA Ops:
  7.2 365.0 %all-reduce.9.cloned.1.call-start = ((), (), s32[]{:S(2)}) async-start(), calls=%async_computation.1 | async-start | bytes 5013504 | tf_op jit(solution)/shard_map/psum | solution.py:497
  9.8 75.1 %collective-permute-start.9 = (bf16[128,1088]{0,1:T(8,128)(2,1)}, bf16[128,1088]{0,1:T(8,128)(2,1)}, u32[]{:S(2)}, u32[]{:S(2)}) collective-permute-start(bf16[128,1088]{0,1:T(8,128)(2,1)} %get-tuple-element.119), channel_id=1, source_target_pairs={{0,1},{1,0},{2,3},{3,2},{4,5},{5,4},{6,7},{7,6},{8,9},{9,8},{10,11... | collective-permute-start | bytes 835592 | tf_op jit(solution)/shard_map/ppermute | solution.py:256
  10.2 95.1 %collective-permute-start.8 = (bf16[544,1088]{1,0:T(8,128)(2,1)}, bf16[544,1088]{1,0:T(8,128)(2,1)}, u32[]{:S(2)}, u32[]{:S(2)}) collective-permute-start(bf16[544,1088]{1,0:T(8,128)(2,1)} %param.23), channel_id=1, source_target_pairs={{0,1},{1,0},{2,3},{3,2},{4,5},{5,4},{6,7},{7,6},{8,9},{9,8},{10,11... | collective-permute-start | bytes 3551240 | tf_op jit(solution)/shard_map/ppermute | solution.py:256
  30.2 42.5 %collective-permute-start.3 = (bf16[3,5,64,256]{3,2,1,0:T(8,128)(2,1)S(1)}, bf16[3,5,64,256]{3,2,1,0:T(8,128)(2,1)S(1)}, u32[]{:S(2)}, u32[]{:S(2)}) collective-permute-start(bf16[3,5,64,256]{3,2,1,0:T(8,128)(2,1)S(1)} %get-tuple-element.99), channel_id=1, source_target_pairs={{0,4},{2,6},{4,0},{6,2},{1,5},{3,7},{5,1},{7,3},{8,12},{10,14},{12... | collective-permute-start | bytes 1474568 | tf_op jit(solution)/shard_map/ppermute | solution.py:277
  30.2 42.5 %collective-permute-start.2 = (bf16[3,5,64,256]{3,2,1,0:T(8,128)(2,1)S(1)}, bf16[3,5,64,256]{3,2,1,0:T(8,128)(2,1)}, u32[]{:S(2)}, u32[]{:S(2)}) collective-permute-start(bf16[3,5,64,256]{3,2,1,0:T(8,128)(2,1)S(1)} %get-tuple-element.100), channel_id=1, source_target_pairs={{0,2},{2,4},{4,6},{6,0},{1,3},{3,5},{5,7},{7,1},{8,10},{10,12},{12... | collective-permute-start | bytes 1474568 | tf_op jit(solution)/shard_map/ppermute | solution.py:277
  111.1 76.8 %collective-permute-start.17 = (bf16[512,1088]{0,1:T(8,128)(2,1)}, bf16[512,1088]{0,1:T(8,128)(2,1)}, u32[]{:S(2)}, u32[]{:S(2)}) collective-permute-start(bf16[512,1088]{0,1:T(8,128)(2,1)} %pad_maximum_fusion.2), channel_id=1, source_target_pairs={{0,8},{8,0},{16,24},{24,16},{1,9},{9,1},{17,25},{25,17},{2,10},{10... | collective-permute-start | bytes 3342344 | tf_op jit(solution)/shard_map/ppermute | solution.py:413
  133.6 37.0 %collective-permute-start.18 = (bf16[512,1088]{0,1:T(8,128)(2,1)}, bf16[512,1088]{0,1:T(8,128)(2,1)}, u32[]{:S(2)}, u32[]{:S(2)}) collective-permute-start(bf16[512,1088]{0,1:T(8,128)(2,1)} %pad_maximum_fusion.3), channel_id=1, source_target_pairs={{0,16},{8,24},{16,0},{24,8},{1,17},{9,25},{17,1},{25,9},{2,18},{10... | collective-permute-start | bytes 3342344 | tf_op jit(solution)/shard_map/ppermute | solution.py:455
  136.2 51.7 %collective-permute-start.16 = (bf16[1088,512]{1,0:T(8,128)(2,1)}, bf16[1088,512]{1,0:T(8,128)(2,1)}, u32[]{:S(2)}, u32[]{:S(2)}) collective-permute-start(bf16[1088,512]{1,0:T(8,128)(2,1)} %constant_dynamic-slice_fusion.14), channel_id=1, source_target_pairs={{0,8},{8,0},{16,24},{24,16},{1,9},{9,1},{17,25},{25,17},{2,10},{10... | collective-permute-start | bytes 3342344 | tf_op jit(solution)/shard_map/ppermute | solution.py:459
  137.9 46.8 %collective-permute-start.19 = (bf16[1088,512]{1,0:T(8,128)(2,1)}, bf16[1088,512]{1,0:T(8,128)(2,1)}, u32[]{:S(2)}, u32[]{:S(2)}) collective-permute-start(bf16[1088,512]{1,0:T(8,128)(2,1)} %constant_dynamic-slice_fusion.13), channel_id=1, source_target_pairs={{0,16},{8,24},{16,0},{24,8},{1,17},{9,25},{17,1},{25,9},{2,18},{10... | collective-permute-start | bytes 3342344 | tf_op jit(solution)/shard_map/ppermute | solution.py:461
  204.8 102.3 %collective-permute-start.29 = (bf16[256,544]{0,1:T(8,128)(2,1)}, bf16[256,544]{0,1:T(8,128)(2,1)}, u32[]{:S(2)}, u32[]{:S(2)}) collective-permute-start(bf16[256,544]{0,1:T(8,128)(2,1)} %copy-done.39), channel_id=1, source_target_pairs={{0,1},{1,0},{2,3},{3,2},{4,5},{5,4},{6,7},{7,6},{8,9},{9,8},{10,11... | collective-permute-start | bytes 835592 | tf_op jit(solution)/shard_map/ppermute | solution.py:256
  243.8 58.6 %collective-permute-start.35 = (bf16[544,256]{1,0:T(8,128)(2,1)}, bf16[544,256]{1,0:T(8,128)(2,1)}, u32[]{:S(2)}, u32[]{:S(2)}) collective-permute-start(bf16[544,256]{1,0:T(8,128)(2,1)} %get-tuple-element.47), channel_id=1, source_target_pairs={{0,1},{1,0},{2,3},{3,2},{4,5},{5,4},{6,7},{7,6},{8,9},{9,8},{10,11... | collective-permute-start | bytes 835592 | tf_op jit(solution)/shard_map/ppermute | solution.py:256
  245.9 37.7 %collective-permute-start.26 = (bf16[3,5,64,256]{3,2,1,0:T(8,128)(2,1)}, bf16[3,5,64,256]{3,2,1,0:T(8,128)(2,1)S(1)}, u32[]{:S(2)}, u32[]{:S(2)}) collective-permute-start(bf16[3,5,64,256]{3,2,1,0:T(8,128)(2,1)} %get-tuple-element.94), channel_id=1, source_target_pairs={{0,2},{2,4},{4,6},{6,0},{1,3},{3,5},{5,7},{7,1},{8,10},{10,12},{12... | collective-permute-start | bytes 1474568 | tf_op jit(solution)/shard_map/ppermute | solution.py:293
  246.9 208.8 %all-reduce.7.cloned.1.call-start = ((), (), s32[]{:S(2)}) async-start(), calls=%async_computation | async-start | bytes 2437120 | tf_op jit(solution)/shard_map/psum | solution.py:540
  264.6 35.6 %collective-permute-start.22 = (bf16[256,1088]{0,1:T(8,128)(2,1)}, bf16[256,1088]{0,1:T(8,128)(2,1)}, u32[]{:S(2)}, u32[]{:S(2)}) collective-permute-start(bf16[256,1088]{0,1:T(8,128)(2,1)} %slice.206), channel_id=1, source_target_pairs={{0,1},{1,0},{2,3},{3,2},{4,5},{5,4},{6,7},{7,6},{8,9},{9,8},{10,11... | collective-permute-start | bytes 1671176 | tf_op jit(solution)/shard_map/ppermute | solution.py:256
  302.4 71.4 %collective-permute-start.23 = (bf16[128,1088]{0,1:T(8,128)(2,1)S(1)}, bf16[128,1088]{0,1:T(8,128)(2,1)S(1)}, u32[]{:S(2)}, u32[]{:S(2)}) collective-permute-start(bf16[128,1088]{0,1:T(8,128)(2,1)S(1)} %get-tuple-element.116), channel_id=1, source_target_pairs={{0,1},{1,0},{2,3},{3,2},{4,5},{5,4},{6,7},{7,6},{8,9},{9,8},{10,11... | collective-permute-start | bytes 835592 | tf_op jit(solution)/shard_map/ppermute | solution.py:256
  405.1 54.2 %collective-permute-start.51 = (bf16[272,1088]{1,0:T(8,128)(2,1)}, bf16[272,1088]{1,0:T(8,128)(2,1)}, u32[]{:S(2)}, u32[]{:S(2)}) collective-permute-start(bf16[272,1088]{1,0:T(8,128)(2,1)} %get-tuple-element.103), channel_id=1, source_target_pairs={{0,8},{8,0},{16,24},{24,16},{1,9},{9,1},{17,25},{25,17},{2,10},{10... | collective-permute-start | bytes 1775624 | tf_op jit(solution)/shard_map/ppermute | solution.py:331
  406.9 50.2 %collective-permute-start.57 = (bf16[272,1088]{1,0:T(8,128)(2,1)S(1)}, bf16[272,1088]{1,0:T(8,128)(2,1)}, u32[]{:S(2)}, u32[]{:S(2)}) collective-permute-start(bf16[272,1088]{1,0:T(8,128)(2,1)S(1)} %get-tuple-element.102), channel_id=1, source_target_pairs={{0,16},{8,24},{16,0},{24,8},{1,17},{9,25},{17,1},{25,9},{2,18},{10... | collective-permute-start | bytes 1775624 | tf_op jit(solution)/shard_map/ppermute | solution.py:331
  411.5 89.8 %collective-permute-start.56 = (bf16[544,1088]{1,0:T(8,128)(2,1)S(1)}, bf16[544,1088]{1,0:T(8,128)(2,1)}, u32[]{:S(2)}, u32[]{:S(2)}) collective-permute-start(bf16[544,1088]{1,0:T(8,128)(2,1)S(1)} %maximum_select_fusion.8), channel_id=1, source_target_pairs={{0,16},{8,24},{16,0},{24,8},{1,17},{9,25},{17,1},{25,9},{2,18},{10... | collective-permute-start | bytes 3551240 | tf_op jit(solution)/shard_map/ppermute | solution.py:331
  426.1 101.6 %collective-permute-start.54 = (bf16[272,2176]{1,0:T(8,128)(2,1)S(1)}, bf16[272,2176]{1,0:T(8,128)(2,1)}, u32[]{:S(2)}, u32[]{:S(2)}) collective-permute-start(bf16[272,2176]{1,0:T(8,128)(2,1)S(1)} %maximum_select_fusion.11), channel_id=1, source_target_pairs={{0,8},{8,0},{16,24},{24,16},{1,9},{9,1},{17,25},{25,17},{2,10},{10... | collective-permute-start | bytes 3551240 | tf_op jit(solution)/shard_map/ppermute | solution.py:331
  458.7 58.1 %collective-permute-start.58 = (bf16[544,1088]{1,0:T(8,128)(2,1)S(1)}, bf16[544,1088]{1,0:T(8,128)(2,1)S(1)}, u32[]{:S(2)}, u32[]{:S(2)}) collective-permute-start(bf16[544,1088]{1,0:T(8,128)(2,1)S(1)} %maximum_select_fusion.9), channel_id=1, source_target_pairs={{0,8},{8,0},{16,24},{24,16},{1,9},{9,1},{17,25},{25,17},{2,10},{10... | collective-permute-start | bytes 3551240 | tf_op jit(solution)/shard_map/ppermute | solution.py:331
  459.4 39.4 %collective-permute-start.49 = (bf16[136,1088]{1,0:T(8,128)(2,1)S(1)}, bf16[136,1088]{1,0:T(8,128)(2,1)S(1)}, u32[]{:S(2)}, u32[]{:S(2)}) collective-permute-start(bf16[136,1088]{1,0:T(8,128)(2,1)S(1)} %copy-done.37), channel_id=1, source_target_pairs={{0,8},{8,0},{16,24},{24,16},{1,9},{9,1},{17,25},{25,17},{2,10},{10... | collective-permute-start | bytes 887816 | tf_op jit(solution)/shard_map/ppermute | solution.py:318
  466.1 58.8 %collective-permute-start.52 = (bf16[544,1088]{1,0:T(8,128)(2,1)S(1)}, bf16[544,1088]{1,0:T(8,128)(2,1)S(1)}, u32[]{:S(2)}, u32[]{:S(2)}) collective-permute-start(bf16[544,1088]{1,0:T(8,128)(2,1)S(1)} %maximum_select_fusion.7), channel_id=1, source_target_pairs={{0,16},{8,24},{16,0},{24,8},{1,17},{9,25},{17,1},{25,9},{2,18},{10... | collective-permute-start | bytes 3551240 | tf_op jit(solution)/shard_map/ppermute | solution.py:331
  501.3 47.4 %collective-permute-start.50 = (bf16[272,1088]{1,0:T(8,128)(2,1)}, bf16[272,1088]{1,0:T(8,128)(2,1)}, u32[]{:S(2)}, u32[]{:S(2)}) collective-permute-start(bf16[272,1088]{1,0:T(8,128)(2,1)} %maximum_select_fusion.14), channel_id=1, source_target_pairs={{0,16},{8,24},{16,0},{24,8},{1,17},{9,25},{17,1},{25,9},{2,18},{10... | collective-permute-start | bytes 1775624 | tf_op jit(solution)/shard_map/ppermute | solution.py:318
  516.9 35.2 %collective-permute-start.46 = (bf16[272,2176]{1,0:T(8,128)(2,1)S(1)}, bf16[272,2176]{1,0:T(8,128)(2,1)}, u32[]{:S(2)}, u32[]{:S(2)}) collective-permute-start(bf16[272,2176]{1,0:T(8,128)(2,1)S(1)} %maximum_select_fusion.10), channel_id=1, source_target_pairs={{0,8},{8,0},{16,24},{24,16},{1,9},{9,1},{17,25},{25,17},{2,10},{10... | collective-permute-start | bytes 3551240 | tf_op jit(solution)/shard_map/ppermute | solution.py:318
  (100 other events, 1330.1 us)
Sparse Core Ops, SparseCore 0:
  247.0 125.1 all-reduce.8
  379.7 75.9 all-reduce.6

commit v2 on v1

--- a/solution.py
+++ b/solution.py
@@ -220,28 +220,34 @@
             scratch_shapes=[pltpu.VMEM(blocks, low_type) for _ in range(4)],
         ),
         compiler_params=pltpu.CompilerParams(vmem_limit_bytes=40 * 2**20),
-        cost_estimate=pl.CostEstimate(flops=0, bytes_accessed=0, transcendentals=0),
+        cost_estimate=pl.CostEstimate(
+            flops=2 * heads * count * (count + 1) * rows * rows * depth,
+            bytes_accessed=8 * heads * count * depth * rows,
+            transcendentals=heads * count * (count + 1) * rows * rows // 2,
+        ),
     )(ranks, mixed)
 
 
-def attention_backward(ranks, mixed, outs, grads, lse):
-    count, _, heads, depth, rows = mixed.shape
+def attention_backward(ranks, mixed, outs, grads, lse, part):
+    count, _, _, depth, rows = mixed.shape
+    start, stop = part
     blocks = (2 * count, depth, rows // 2)
-    three = pl.BlockSpec((count, 3, 1, depth, rows), lambda head, _: (0, 0, head, 0, 0))
-    one = pl.BlockSpec((count, 1, depth, rows), lambda head, _: (0, head, 0, 0))
+    three_block = (count, 3, 1, depth, rows)
+    three = pl.BlockSpec(three_block, lambda head, _: (0, 0, head + start, 0, 0))
+    one = pl.BlockSpec((count, 1, depth, rows), lambda head, _: (0, head + start, 0, 0))
     return pl.pallas_call(
         backward_kernel,
-        out_shape=jax.ShapeDtypeStruct(mixed.shape, low_type),
+        out_shape=jax.ShapeDtypeStruct((count, 3, stop - start, depth, rows), low_type),
         grid_spec=pltpu.PrefetchScalarGridSpec(
             num_scalar_prefetch=1,
-            grid=(heads,),
+            grid=(stop - start,),
             in_specs=[
                 three,
                 one,
                 one,
-                pl.BlockSpec((1, count, rows), lambda head, _: (head, 0, 0)),
+                pl.BlockSpec((1, count, rows), lambda head, _: (head + start, 0, 0)),
             ],
-            out_specs=three,
+            out_specs=pl.BlockSpec(three_block, lambda head, _: (0, 0, head, 0, 0)),
             scratch_shapes=[pltpu.VMEM(blocks, low_type) for _ in range(5)]
             + [pltpu.VMEM(blocks, full_type)]
             + [pltpu.VMEM(blocks, low_type) for _ in range(2)]
@@ -279,62 +285,67 @@
     return jnp.stack(pieces)
 
 
-def returned(pieces, axis):
+def sent_back(pieces):
     count = lax.axis_size("ctx")
-    place = lax.axis_index("ctx")
-    size = pieces.shape[axis + 1]
-    shape = list(pieces.shape[1:])
-    shape[axis] = size * count
-    result = jnp.zeros(shape, pieces.dtype)
-    for shift in range(count):
-        piece = pieces[shift]
-        if shift:
-            hops = [(one, (one - shift) % count) for one in range(count)]
-            piece = lax.ppermute(piece, "ctx", hops)
-        source = lax.rem(place + shift, count)
-        result = lax.dynamic_update_slice_in_dim(result, piece, source * size, axis)
+    back = [pieces[0]]
+    for shift in range(1, count):
+        hops = [(one, (one - shift) % count) for one in range(count)]
+        back.append(lax.ppermute(pieces[shift], "ctx", hops))
+    return back
+
+
+def assembled(backs, parts):
+    count = len(backs[0])
+    lead, (depth, rows) = backs[0][0].shape[:-3], backs[0][0].shape[-2:]
+    result = jnp.zeros((*lead, count, parts[-1][1], depth, rows), low_type)
+    for back, (start, _) in zip(backs, parts):
+        for shift, piece in enumerate(back):
+            source = lax.rem(lax.axis_index("ctx") + shift, count)
+            at = (0,) * len(lead) + (source, start, 0, 0)
+            result = lax.dynamic_update_slice(result, jnp.expand_dims(piece, len(lead)), at)
     return result
 
 
-def dp_hops(bit):
-    return [(one, one ^ (1 << bit)) for one in range(lax.axis_size("dp"))]
-
-
-def reduced(array, order):
-    index = lax.axis_index("dp")
+def pair_hops(axis, bit):
+    return [(one, one ^ (1 << bit)) for one in range(lax.axis_size(axis))]
+
+
+def bit_of(axis, bit):
+    return lax.rem(lax.div(lax.axis_index(axis), 1 << bit), 2)
+
+
+def reduced(array, axis, order):
     for bit in order:
         half = array.shape[0] // 2
-        high = lax.rem(lax.div(index, 1 << bit), 2)
+        high = bit_of(axis, bit)
         kept = part_of(array, high, half)
-        arrived = lax.ppermute(part_of(array, 1 - high, half), "dp", dp_hops(bit))
-        array = (kept.astype(full_type) + arrived.astype(full_type)).astype(low_type)
+        arrived = lax.ppermute(part_of(array, 1 - high, half), axis, pair_hops(axis, bit))
+        array = (wide(kept) + wide(arrived)).astype(low_type)
     return array
 
 
-def spread(array, order):
-    index = lax.axis_index("dp")
-    for bit in reversed(order):
-        high = lax.rem(lax.div(index, 1 << bit), 2)
-        arrived = lax.ppermute(array, "dp", dp_hops(bit))
-        array = in_order(array, arrived, high == 1, 0)
+def spread(array, axis, order, dim=0):
+    for bit in order:
+        arrived = lax.ppermute(array, axis, pair_hops(axis, bit))
+        array = in_order(array, arrived, bit_of(axis, bit) == 1, dim)
     return array
 
 
-def halves_of_all(array, axes):
-    index = lax.axis_index("dp")
+def spread_both(parts, dims, step):
+    order = range(len(dims))
+    return tuple(
+        spread(part, "dp", (bits[step],), dims[bits[step]])
+        for part, bits in zip(parts, (order, order[::-1]))
+    )
+
+
+def in_two(array):
     half = array.shape[0] // 2
-    forth = tuple(range(len(axes)))
-    gathered = []
-    for part, order in ((array[:half], forth), (array[half:], forth[::-1])):
-        for bit in order:
-            high = lax.rem(lax.div(index, 1 << bit), 2)
-            arrived = lax.ppermute(part, "dp", dp_hops(bit))
-            part = in_order(part, arrived, high == 1, axes[bit])
-        gathered.append(part)
-    return gathered
-
-
-def joined(forth, back, bits):
+    return array[:half], array[half:]
+
+
+def joined(parts, bits):
+    forth, back = parts
     forth = forth.reshape((2,) * bits + (-1, forth.shape[1]))
     forth = jnp.transpose(forth, (*reversed(range(bits)), bits, bits + 1))
     return jnp.stack([forth, back.reshape(forth.shape)], axis=bits).reshape(-1, forth.shape[-1])
@@ -348,15 +359,10 @@
     return lax.optimization_barrier(arrays)
 
 
-def small_total_over_group(array):
-    for bit in range(int(math.log2(lax.axis_size("dp")))):
-        array = array + lax.ppermute(array, "dp", dp_hops(bit))
-    count = lax.axis_size("ctx")
-    total = array
-    for shift in range(1, count):
-        hops = [(one, (one + shift) % count) for one in range(count)]
-        total = total + lax.ppermute(array, "ctx", hops)
-    return total
+def summed(array, axis, order):
+    for bit in order:
+        array = array + lax.ppermute(array, axis, pair_hops(axis, bit))
+    return array
 
 
 def local(
@@ -410,7 +416,7 @@
     other_proj = swapped(w_proj)
     grad_low = by_sequence(cotangent)
     grad_rows = jnp.concatenate([grad_low, swapped(grad_low)], axis=0)
-    grad_rows_near = lax.ppermute(grad_rows, "dp", dp_hops(0))
+    grad_rows_near = lax.ppermute(grad_rows, "dp", pair_hops("dp", 0))
     grad_act = contract(w_down, grad_rows, 1, 1)
 
     inputs = wide(rows_low)
@@ -438,27 +444,30 @@
         array = array.reshape(-1, padded, depth, rows)
         return array[:, :HEADS].reshape(-1, rows)
 
-    mixed_heads = scattered(to_heads(mixed))
+    normed_near = swapped(normed_other)
+    mixed_heads, grad_act, grad_rows_near, normed_near = tied(
+        scattered(to_heads(mixed)), grad_act, grad_rows_near, normed_near
+    )
     out_heads, lse = attention_forward(ranks, mixed_heads)
-    attended = from_heads(returned(out_heads, 0))
+    attended = from_heads(assembled([sent_back(out_heads)], ((0, group),)))
     attended_own = part_of(attended, core, half_width)
     attended_other = part_of(attended, 1 - core, half_width)
     branch = contract(attended_own, w_proj, 0, 0) + contract(attended_other, other_proj, 0, 0)
     middle = inputs + branch + wide(proj_bias)
 
     normed_two, norm_two_pull = jax.vjp(layer_norm, middle, wide(ln2_gain), wide(ln2_bias))
-    normed_two_low = normed_two.astype(low_type)
+    normed_two_low, attended_near = tied(normed_two.astype(low_type), swapped(attended_other))
     rows_two = jnp.concatenate([normed_two_low, swapped(normed_two_low)], axis=0)
-    index = lax.axis_index("dp")
-    low_high, top_high = lax.rem(index, 2), lax.div(index, 1 << (bits - 1))
+    low_high, top_high = bit_of("dp", 0), bit_of("dp", bits - 1)
     half_units = w_down.shape[0] // 2
-    rows_two_near = lax.ppermute(rows_two, "dp", dp_hops(bits - 1))
     pre_act = contract(w_up, rows_two, 0, 1) + wide(up_bias)[:, None]
     activated, gelu_pull = jax.vjp(gelu_tanh, pre_act)
     act_low = row_major(activated.astype(low_type))
-    act_near = lax.ppermute(part_of(act_low, 1 - low_high, half_units), "dp", dp_hops(0))
+    act_near = lax.ppermute(part_of(act_low, 1 - low_high, half_units), "dp", pair_hops("dp", 0))
     grad_pre = row_major(gelu_pull(grad_act)[0].astype(low_type))
-    grad_pre_near = lax.ppermute(part_of(grad_pre, 1 - top_high, half_units), "dp", dp_hops(bits - 1))
+    up_send = jnp.concatenate([rows_two.T, part_of(grad_pre, 1 - top_high, half_units)])
+    up_send, grad_pre = tied(up_send, grad_pre)
+    up_near = lax.ppermute(up_send, "dp", pair_hops("dp", bits - 1))
     grad_up_bias = jnp.sum(wide(grad_pre), axis=1)
 
     back_terms = contract(grad_pre, w_up, 0, 1)
@@ -476,38 +485,44 @@
         0,
     )
     grad_heads = scattered(to_heads(grad_attended))[:, 0]
-
-    grad_heads, act_later, grad_pre_later = tied(grad_heads, act_low, grad_pre)
-    grad_w_down = contract(part_of(act_later, low_high, half_units), grad_rows, 1, 0) + contract(
-        act_near, grad_rows_near, 1, 0
-    )
-    grad_w_up = contract(rows_two, part_of(grad_pre_later, top_high, half_units), 0, 1) + contract(
-        rows_two_near, grad_pre_near, 0, 1
-    )
-    grad_w_down = row_major(grad_w_down.astype(low_type))
+    branch_near = swapped(grad_branch)
+
+    grad_w_down = contract(grad_rows, part_of(act_low, low_high, half_units), 0, 1) + contract(
+        grad_rows_near, act_near, 0, 1
+    )
+    grad_heads, grad_w_down, branch_near = tied(
+        grad_heads, row_major(grad_w_down.astype(low_type)), branch_near
+    )
+    down_share = reduced(grad_w_down, "dp", upward[1:])
+
+    cut = (group + 1) // 2
+    parts = ((0, cut), (cut, group)) if cut < group else ((0, group),)
+    grads_of = [
+        attention_backward(ranks, mixed_heads, out_heads, grad_heads, lse, part) for part in parts
+    ]
+    grads_of[0], grad_pre_late = tied(grads_of[0], grad_pre)
+    grad_w_up = contract(rows_two, part_of(grad_pre_late, top_high, half_units), 0, 1) + contract(
+        up_near[:width], up_near[width:], 1, 1
+    )
     grad_w_up = row_major(grad_w_up.astype(low_type))
-    grad_heads, grad_w_down, grad_w_up = tied(grad_heads, grad_w_down, grad_w_up)
-    down_share = reduced(grad_w_down, upward[1:])
-    up_share = reduced(grad_w_up, downward[1:])
-
-    grad_mixed_heads = attention_backward(ranks, mixed_heads, out_heads, grad_heads, lse)
-    (grad_mixed_heads, act_late, attended_late, branch_late, down_share, up_share) = tied(
-        grad_mixed_heads, act_low, attended_other, grad_branch, down_share, up_share
-    )
-    down_share, up_share = lax.psum((down_share, up_share), "ctx")
-    grad_mixed = from_heads(returned(grad_mixed_heads, 1))
+    backs = [sent_back(grads_of[0])]
+    for later in grads_of[1:]:
+        backs[-1], later, grad_w_up, branch_late, down_share = tied(
+            backs[-1], later, grad_w_up, grad_branch, down_share
+        )
+        backs.append(sent_back(later))
+    turns = int(math.log2(count))
+    down_share = reduced(down_share, "ctx", range(turns))
+    up_share = reduced(grad_w_up, "dp", downward[1:])
+    attended_both = jnp.concatenate([attended_own, attended_near], axis=1)
+    branch_both = jnp.concatenate([grad_branch if cut == group else branch_late, branch_near])
+    grad_w_proj = contract(attended_both, branch_both, 1, 0)
+    grad_mixed, up_share, grad_w_proj, down_share = tied(
+        from_heads(assembled(backs, parts)), up_share, grad_w_proj, down_share
+    )
     query_rows = lax.broadcasted_iota(jnp.int32, (3 * width, 1), 0) < width
     grad_mixed = jnp.where(query_rows, grad_mixed * low_type(scale), grad_mixed)
     grad_mixed_sums = jnp.sum(wide(grad_mixed), axis=1)
-
-    down_terms = contract(act_late, w_down, 0, 0)
-    mlp_sum = down_terms[:rows] + wide(swapped(down_terms[rows:].astype(low_type)))
-    output = by_rows((middle + mlp_sum + wide(down_bias)).astype(low_type))
-
-    attended_both = jnp.concatenate([attended_own, swapped(attended_late)], axis=1)
-    branch_both = jnp.concatenate([branch_late, swapped(branch_late)], axis=0)
-    grad_w_proj = contract(attended_both, branch_both, 1, 0)
-    proj_share = reduced(row_major(grad_w_proj.astype(low_type)), downward)
 
     small_early = own_half(
         jnp.stack(
@@ -525,33 +540,79 @@
     up_bias_rows = jnp.pad(grad_up_bias, (0, wide_rows * half_width - grad_up_bias.shape[0]))
     small_early = jnp.concatenate([small_early, up_bias_rows.reshape(wide_rows, half_width)])
 
-    normed_both = jnp.concatenate([normed_own, swapped(normed_other)], axis=0)
+    normed_both = jnp.concatenate([normed_own, normed_near], axis=0)
     grad_mixed_both = jnp.concatenate([grad_mixed, swapped(grad_mixed)], axis=1)
     grad_w_qkv = contract(normed_both, grad_mixed_both, 0, 1)
-    grad_w_qkv = row_major(grad_w_qkv.astype(low_type))
-    first_share = reduced(grad_w_qkv[:, : 2 * width], upward)
-    second_share = reduced(grad_w_qkv[:, 2 * width :], downward)
-
-    (down_share, up_share, first_share, second_share, proj_share, small_later) = tied(
-        down_share, up_share, first_share, second_share, proj_share, small_early
-    )
-    down_total = wide(joined(*halves_of_all(down_share, (0,) * bits), bits))
-    up_total = wide(joined(*halves_of_all(up_share, (0,) * (bits - 1) + (1,)), bits - 1))
-    first_share, second_share, proj_share = lax.psum((first_share, second_share, proj_share), "ctx")
-    qkv_total = jnp.concatenate(
-        [wide(spread(first_share, upward)), wide(spread(second_share, downward))], axis=1
-    )
-    proj_total = wide(spread(proj_share, downward))
-
+
+    first = row_major(grad_w_qkv[:, : 2 * width].astype(low_type))
+    second = row_major(
+        jnp.concatenate([grad_w_qkv[:, 2 * width :], grad_w_proj], axis=1).astype(low_type)
+    )
+    first, second, up_share, down_share = tied(first, second, up_share, down_share)
+
+    first, second = reduced(first, "dp", upward[:1]), reduced(second, "dp", downward[:1])
+    up_share = reduced(up_share, "ctx", range(1))
+    down_share = spread(down_share, "ctx", range(1, turns)[::-1])
+    first, second, up_share, down_share, act_late, small_late = tied(
+        first, second, up_share, down_share, act_low, small_early
+    )
+
+    down_terms = contract(act_late, w_down, 0, 0)
+    mlp_sum = down_terms[:rows] + wide(swapped(down_terms[rows:].astype(low_type)))
+    output = by_rows((middle + mlp_sum + wide(down_bias)).astype(low_type))
+
+    down_dims = (1,) + (0,) * (bits - 1)
+    up_dims = (0,) * (bits - 1) + (1,)
+    first, second = reduced(first, "dp", upward[1:]), reduced(second, "dp", downward[1:])
+    up_share = reduced(up_share, "ctx", range(1, turns))
+    down_share = spread(down_share, "ctx", range(1))
+    first, second, up_share, down_share, output, grad_mixed = tied(
+        first, second, up_share, down_share, output, grad_mixed
+    )
+
+    last = jnp.concatenate([first, second])
+    sliced = last.shape[0] % count == 0
+    down_parts = spread_both(in_two(down_share), down_dims, 0)
+    up_share = spread(up_share, "ctx", range(1, turns)[::-1])
+    last = reduced(last, "ctx", range(1)) if sliced else lax.psum(last, "ctx")
     grad_norm_one = in_order(
         contract(grad_mixed, w_qkv, 0, 1), contract(grad_mixed, other_qkv, 0, 1), core == 1, 1
     )
+    down_parts, up_share, last, grad_norm_one, small_late = tied(
+        down_parts, up_share, last, grad_norm_one, small_late
+    )
+
+    down_parts = spread_both(down_parts, down_dims, 1)
+    up_share = spread(up_share, "ctx", range(1))
+    last = reduced(last, "ctx", range(1, turns)) if sliced else last
     grad_in_norm, grad_ln1_gain, grad_ln1_bias = norm_one_pull(grad_norm_one)
     grad_hidden = by_rows((grad_mid + grad_in_norm).astype(low_type))
-
-    small_rows = jnp.stack([grad_ln1_gain, grad_ln1_bias])
-    small_own = own_half(small_rows)
-    small_total = small_total_over_group(jnp.concatenate([small_own, small_later]))
+    small = jnp.concatenate([own_half(jnp.stack([grad_ln1_gain, grad_ln1_bias])), small_late])
+    down_parts, up_share, last, small, grad_hidden = tied(
+        down_parts, up_share, last, small, grad_hidden
+    )
+
+    down_total = wide(joined(down_parts, bits - 1)).T
+    up_parts = spread_both(in_two(up_share), up_dims, 0)
+    last = spread(last, "ctx", range(1, turns)[::-1]) if sliced else last
+    small = summed(small, "dp", upward[:1])
+    up_parts, last, small = tied(up_parts, last, small)
+
+    up_parts = spread_both(up_parts, up_dims, 1)
+    last = spread(last, "ctx", range(1)) if sliced else last
+    small = summed(small, "dp", upward[1:])
+    up_parts, last, small, down_total = tied(up_parts, last, small, down_total)
+
+    up_total = wide(joined(up_parts, bits - 1))
+    first, second = in_two(last)
+    first, second = spread(first, "dp", downward[:1]), spread(second, "dp", upward[:1])
+    small = summed(small, "ctx", range(1))
+    first, second, small, up_total = tied(first, second, small, up_total)
+
+    small_total = summed(small, "ctx", range(1, turns))
+    first, second = spread(first, "dp", downward[1:]), spread(second, "dp", upward[1:])
+    qkv_total = jnp.concatenate([wide(first), wide(second[:, :width])], axis=1)
+    proj_total = wide(second[:, width:])
     up_bias_total = small_total[8:].reshape(-1)[: grad_up_bias.shape[0]]
     return (
         output,

time: 573 us -> 498 us (0.87)
  waiting for transfers between devices: 280 us -> 246 us
  other arithmetic: 66.8 us -> 44.3 us
  between operations: 15.8 us -> 2.85 us
  matrix products: 67.6 us -> 56.2 us
    psum x2 -> x0, waiting for transfers between devices: 45.4 us -> none  [the longest x1 28.6 us: local(): lax.psum((first_share, second_share, proj_share), 'ctx')]
    ppermute x37 -> x46, waiting for transfers between devices: 166 us -> 195 us  [the longest x18 87.8 us: spread(): arrived = lax.ppermute(array, axis, pair_hops(axis, bit))]
    ppermute x6, waiting for transfers between devices: 61.8 us -> 44 us  [scattered(): piece = lax.ppermute(piece, 'ctx', hops)]
    dot_general x18, matrix products: 67.6 us -> 56.2 us  [contract(): lax.dot_general(first, second, (((first_dim,), (second_dim,)), ((), ())),...]
    select_n x16 -> x22, other arithmetic: 23.7 us -> 16.9 us  [in_order(): jnp.where(flip, jnp.concatenate([second, first], axis), jnp.concatenate([...]
    unnamed x127 -> x146, local copies, waits for them, and re-layouts: 14.8 us -> 10.3 us
    ppermute x37 -> x46, starting transfers between devices: 62 us -> 61.4 us  [the longest x12 18.7 us: reduced(): lax.ppermute(part_of(array, 1 - high, half), axis, pair_hops(axis, bit))]
    pallas_call x1 -> x2, Pallas kernels: 15.1 us -> 15.6 us  [attention_backward(): pl.pallas_call(backward_kernel, out_shape=jax.ShapeDtypeStruct((count, 3,...]
  transfers between devices with their start and end apart: 61 -> 68, of which waited for: 29 -> 36; matrix products, arithmetic and copies ran while one was open for 27% -> 17% of each run, Pallas kernels for 4% -> 3%
where the time goes in v2:
time: 498 us; the launch traced here: 489 us
  waiting for transfers between devices  246 us (49%)
  starting transfers between devices  76.2 us (15%)
  matrix products  56.2 us (11%)
  other arithmetic  44.3 us (9%)
  local copies, waits for them, and re-layouts  38.5 us (8%)
  Pallas kernels  25.3 us (5%)
    ppermute x18, waiting for transfers between devices, spread(): arrived = lax.ppermute(array, axis, pair_hops(axis, bit))  87.8 us
    ppermute x12, waiting for transfers between devices, reduced(): lax.ppermute(part_of(array, 1 - high, half), axis, pair_hops(axis, bit))  71.4 us
    dot_general x18, matrix products, contract(): lax.dot_general(first, second, (((first_dim,), (second_dim,)), ((), ())),...  56.2 us
    ppermute x6, waiting for transfers between devices, scattered(): piece = lax.ppermute(piece, 'ctx', hops)  44 us
    ppermute x9, waiting for transfers between devices, sent_back(): back.append(lax.ppermute(pieces[shift], 'ctx', hops))  30.7 us
    ppermute x12, starting transfers between devices, reduced(): lax.ppermute(part_of(array, 1 - high, half), axis, pair_hops(axis, bit))  18.7 us
    ppermute x18, starting transfers between devices, spread(): arrived = lax.ppermute(array, axis, pair_hops(axis, bit))  17 us
    select_n x22, other arithmetic, in_order(): jnp.where(flip, jnp.concatenate([second, first], axis), jnp.concatenate([...  16.9 us
  transfers between devices with their start and end apart: 68, of which 36 were waited for; matrix products, arithmetic and copies ran while one was open for 17% of the time, Pallas kernels for 3%

profile of v2, /device:TPU:0, one launch (start us, length us, event | category | flops | bytes accessed | tf_op | source)
XLA Modules:
  0.0 489.4 jit_solution(16857594244208863026)
XLA Ops:
  24.8 5.8 %convolution_bitcast_fusion = f32[2176,512]{1,0:T(8,128)} fusion(bf16[2176,1088]{0,1:T(8,128)(2,1)S(1)} %bitcast.174, bf16[256,1088]{0,1:T(8,128)(2,1)S(1)} %collective-permute-done.6, bf16[128,1088]{0,1:T(8,128)(2,1)S(1)} %collective-permute-done.5, bf16[128,1088]{0,1:T(8,128)(2,1)S(1)} %get-tuple-element.207), kind=kOutput, calls=%fused_computation.12 | convolution fusion | flops 2427650048 | bytes 10305536 | tf_op jit(solution)/shard_map/dot_general | solution.py:35
  35.4 11.5 %collective-permute-done.2 = bf16[3,5,64,256]{3,2,1,0:T(8,128)(2,1)S(1)} collective-permute-done((bf16[3,5,64,256]{3,2,1,0:T(8,128)(2,1)S(1)}, bf16[3,5,64,256]{3,2,1,0:T(8,128)(2,1)S(1)}, u32[]{:S(2)}, u32[]{:S(2)}) %collective-permute-start.2) | collective-permute-done | bytes 491552 | tf_op jit(solution)/shard_map/ppermute | solution.py:283
  46.9 19.0 %collective-permute-done.3 = bf16[3,5,64,256]{3,2,1,0:T(8,128)(2,1)S(1)} collective-permute-done((bf16[3,5,64,256]{3,2,1,0:T(8,128)(2,1)S(1)}, bf16[3,5,64,256]{3,2,1,0:T(8,128)(2,1)S(1)}, u32[]{:S(2)}, u32[]{:S(2)}) %collective-permute-start.3) | collective-permute-done | bytes 491552 | tf_op jit(solution)/shard_map/ppermute | solution.py:283
  66.2 9.7 %shard_map.271 = (bf16[4,5,64,256]{3,2,1,0:T(8,128)(2,1)S(1)}, f32[5,4,256]{2,1,0:T(4,128)S(1)}) custom-call(s32[8]{0:T(128)S(1)} %gather_fusion, bf16[4,3,5,64,256]{4,3,2,1,0:T(8,128)(2,1)S(1)} %pad_maximum_fusion.2.mixed_ref), custom_call_target="tpu_custom_call" | custom-call | flops 838860800 | bytes 2621440 | tf_op jit(solution)/shard_map/pallas_call | solution.py:204
  83.4 9.2 %collective-permute-done.10 = bf16[5,64,256]{2,1,0:T(8,128)(2,1)S(1)} collective-permute-done((bf16[5,64,256]{2,1,0:T(8,128)(2,1)S(1)}, bf16[5,64,256]{2,1,0:T(8,128)(2,1)S(1)}, u32[]{:S(2)}, u32[]{:S(2)}) %collective-permute-start.10) | collective-permute-done | bytes 163872 | tf_op jit(solution)/shard_map/ppermute | solution.py:293
  99.7 10.5 %multiply_convert_fusion = (bf16[2176,512]{1,0:T(8,128)(2,1)}, bf16[2176,512]{1,0:T(8,128)(2,1)S(1)}) fusion(f32[2176,512]{1,0:T(8,128)} %convolution_bitcast_fusion, f32[2176]{0:T(1024)S(1)} %convert_element_type.237, bf16[512,1088]{0,1:T(8,128)(2,1)S(1)} %constant_dynamic-update-slice_fusion, bf16[1088,2176]{1,0:T(8,128)(2,1)} %param.27), kind=kOutput, calls=%fused_computation.25 | convolution fusion | flops 2449932288 | bytes 14770688 | tf_op jit(solution)/shard_map/dot_general | solution.py:35
  140.4 5.7 %collective-permute-done.17 = bf16[1,5,64,256]{3,2,1,0:T(8,128)(2,1)S(1)} collective-permute-done((bf16[1,5,64,256]{3,2,1,0:T(8,128)(2,1)S(1)}, bf16[1,5,64,256]{3,2,1,0:T(8,128)(2,1)S(1)}, u32[]{:S(2)}, u32[]{:S(2)}) %collective-permute-start.17) | collective-permute-done | bytes 163872 | tf_op jit(solution)/shard_map/ppermute | solution.py:283
  155.2 9.3 %shard_map.272 = bf16[4,3,3,64,256]{4,3,2,1,0:T(8,128)(2,1)S(1)} custom-call(s32[8]{0:T(128)S(1)} %gather_fusion, bf16[4,3,5,64,256]{4,3,2,1,0:T(8,128)(2,1)S(1)} %pad_maximum_fusion.2.mixed_ref, bf16[4,5,64,256]{3,2,1,0:T(8,128)(2,1)S(1)} %get-tuple-element.85.out_ref, bf16[4,5,64,256]{3,2,1,0:T(8,128)(2,1)S(1)} %maximum_bitcast_fusion.grad_ref, ...), custom_call_target="tpu_custom_call" | custom-call | tf_op jit(solution)/shard_map/pallas_call | solution.py:238
  164.5 6.4 %shard_map.273 = bf16[4,3,2,64,256]{4,3,2,1,0:T(8,128)(2,1)S(1)} custom-call(s32[8]{0:T(128)S(1)} %gather_fusion, bf16[4,3,5,64,256]{4,3,2,1,0:T(8,128)(2,1)S(1)} %pad_maximum_fusion.2.mixed_ref, bf16[4,5,64,256]{3,2,1,0:T(8,128)(2,1)S(1)} %get-tuple-element.85.out_ref, bf16[4,5,64,256]{3,2,1,0:T(8,128)(2,1)S(1)} %maximum_bitcast_fusion.grad_ref, ...), custom_call_target="tpu_custom_call" | custom-call | tf_op jit(solution)/shard_map/pallas_call | solution.py:238
  181.9 16.6 %collective-permute-done.25 = bf16[544,1088]{1,0:T(8,128)(2,1)} collective-permute-done((bf16[544,1088]{1,0:T(8,128)(2,1)}, bf16[544,1088]{1,0:T(8,128)(2,1)}, u32[]{:S(2)}, u32[]{:S(2)}) %collective-permute-start.25) | collective-permute-done | bytes 1183776 | tf_op jit(solution)/shard_map/ppermute | solution.py:322
  210.9 12.9 %collective-permute-done.26 = bf16[3,2,64,256]{3,2,1,0:T(8,128)(2,1)S(1)} collective-permute-done((bf16[3,2,64,256]{3,2,1,0:T(8,128)(2,1)S(1)}, bf16[3,2,64,256]{3,2,1,0:T(8,128)(2,1)S(1)}, u32[]{:S(2)}, u32[]{:S(2)}) %collective-permute-start.26) | collective-permute-done | bytes 196640 | tf_op jit(solution)/shard_map/ppermute | solution.py:293
  226.4 5.9 %collective-permute-done.28 = bf16[3,2,64,256]{3,2,1,0:T(8,128)(2,1)S(1)} collective-permute-done((bf16[3,2,64,256]{3,2,1,0:T(8,128)(2,1)S(1)}, bf16[3,2,64,256]{3,2,1,0:T(8,128)(2,1)S(1)}, u32[]{:S(2)}, u32[]{:S(2)}) %collective-permute-start.28) | collective-permute-done | bytes 196640 | tf_op jit(solution)/shard_map/ppermute | solution.py:293
  232.5 11.1 %collective-permute-done.31 = bf16[136,1088]{1,0:T(8,128)(2,1)S(1)} collective-permute-done((bf16[136,1088]{1,0:T(8,128)(2,1)S(1)}, bf16[136,1088]{1,0:T(8,128)(2,1)S(1)}, u32[]{:S(2)}, u32[]{:S(2)}) %collective-permute-start.31) | collective-permute-done | bytes 295968 | tf_op jit(solution)/shard_map/ppermute | solution.py:322
  265.2 10.1 %collective-permute-done.36 = bf16[136,1088]{1,0:T(8,128)(2,1)S(1)} collective-permute-done((bf16[136,1088]{1,0:T(8,128)(2,1)S(1)}, bf16[136,1088]{1,0:T(8,128)(2,1)S(1)}, u32[]{:S(2)}, u32[]{:S(2)}) %collective-permute-start.36) | collective-permute-done | bytes 295968 | tf_op jit(solution)/shard_map/ppermute | solution.py:329
  275.5 11.4 %collective-permute-done.35 = bf16[272,1088]{1,0:T(8,128)(2,1)S(1)} collective-permute-done((bf16[272,1088]{1,0:T(8,128)(2,1)S(1)}, bf16[272,1088]{1,0:T(8,128)(2,1)S(1)}, u32[]{:S(2)}, u32[]{:S(2)}) %collective-permute-start.35) | collective-permute-done | bytes 591904 | tf_op jit(solution)/shard_map/ppermute | solution.py:322
  301.9 16.2 %collective-permute-done.40 = bf16[136,1088]{1,0:T(8,128)(2,1)S(1)} collective-permute-done((bf16[136,1088]{1,0:T(8,128)(2,1)S(1)}, bf16[136,1088]{1,0:T(8,128)(2,1)S(1)}, u32[]{:S(2)}, u32[]{:S(2)}) %collective-permute-start.40) | collective-permute-done | bytes 295968 | tf_op jit(solution)/shard_map/ppermute | solution.py:322
  333.7 13.8 %collective-permute-done.46 = bf16[136,1088]{1,0:T(8,128)(2,1)S(1)} collective-permute-done((bf16[136,1088]{1,0:T(8,128)(2,1)S(1)}, bf16[136,1088]{1,0:T(8,128)(2,1)S(1)}, u32[]{:S(2)}, u32[]{:S(2)}) %collective-permute-start.46) | collective-permute-done | bytes 295968 | tf_op jit(solution)/shard_map/ppermute | solution.py:329
  359.6 11.0 %collective-permute-done.51 = bf16[68,2176]{1,0:T(8,128)(2,1)S(1)} collective-permute-done((bf16[68,2176]{1,0:T(8,128)(2,1)S(1)}, bf16[68,2176]{1,0:T(8,128)(2,1)S(1)}, u32[]{:S(2)}, u32[]{:S(2)}) %collective-permute-start.51) | collective-permute-done | bytes 295968 | tf_op jit(solution)/shard_map/ppermute | solution.py:322
  370.7 6.8 %collective-permute-done.50 = bf16[272,1088]{1,0:T(8,128)(2,1)S(1)} collective-permute-done((bf16[272,1088]{1,0:T(8,128)(2,1)S(1)}, bf16[272,1088]{1,0:T(8,128)(2,1)S(1)}, u32[]{:S(2)}, u32[]{:S(2)}) %collective-permute-start.50) | collective-permute-done | bytes 591904 | tf_op jit(solution)/shard_map/ppermute | solution.py:329
  378.0 7.4 %collective-permute-done.49 = bf16[544,1088]{1,0:T(8,128)(2,1)S(1)} collective-permute-done((bf16[544,1088]{1,0:T(8,128)(2,1)S(1)}, bf16[544,1088]{1,0:T(8,128)(2,1)S(1)}, u32[]{:S(2)}, u32[]{:S(2)}) %collective-permute-start.49) | collective-permute-done | bytes 1183776 | tf_op jit(solution)/shard_map/ppermute | solution.py:329
  395.7 8.9 %collective-permute-done.56 = bf16[68,2176]{1,0:T(8,128)(2,1)S(1)} collective-permute-done((bf16[68,2176]{1,0:T(8,128)(2,1)S(1)}, bf16[68,2176]{1,0:T(8,128)(2,1)S(1)}, u32[]{:S(2)}, u32[]{:S(2)}) %collective-permute-start.56) | collective-permute-done | bytes 295968 | tf_op jit(solution)/shard_map/ppermute | solution.py:329
  416.7 5.7 %collective-permute-done.60 = bf16[136,2176]{1,0:T(8,128)(2,1)S(1)} collective-permute-done((bf16[136,2176]{1,0:T(8,128)(2,1)S(1)}, bf16[136,2176]{1,0:T(8,128)(2,1)S(1)}, u32[]{:S(2)}, u32[]{:S(2)}) %collective-permute-start.60) | collective-permute-done | bytes 591904 | tf_op jit(solution)/shard_map/ppermute | solution.py:329
  422.6 10.5 %collective-permute-done.59 = bf16[272,2176]{1,0:T(8,128)(2,1)S(1)} collective-permute-done((bf16[272,2176]{1,0:T(8,128)(2,1)S(1)}, bf16[272,2176]{1,0:T(8,128)(2,1)S(1)}, u32[]{:S(2)}, u32[]{:S(2)}) %collective-permute-start.59) | collective-permute-done | bytes 1183776 | tf_op jit(solution)/shard_map/ppermute | solution.py:329
  466.5 13.5 %collective-permute-done.67 = bf16[272,2176]{1,0:T(8,128)(2,1)} collective-permute-done((bf16[272,2176]{1,0:T(8,128)(2,1)S(1)}, bf16[272,2176]{1,0:T(8,128)(2,1)}, u32[]{:S(2)}, u32[]{:S(2)}) %collective-permute-start.67) | collective-permute-done | bytes 1183776 | tf_op jit(solution)/shard_map/ppermute | solution.py:329
  (441 shorter events, 237.6 us)
Async XLA Ops:
  9.3 56.8 %collective-permute-start.8 = (bf16[256,544]{0,1:T(8,128)(2,1)S(1)}, bf16[256,544]{0,1:T(8,128)(2,1)S(1)}, u32[]{:S(2)}, u32[]{:S(2)}) collective-permute-start(bf16[256,544]{0,1:T(8,128)(2,1)S(1)} %get-tuple-element.209), channel_id=1, source_target_pairs={{0,1},{1,0},{2,3},{3,2},{4,5},{5,4},{6,7},{7,6},{8,9},{9,8},{10,11... | collective-permute-start | bytes 835592 | tf_op jit(solution)/shard_map/ppermute | solution.py:262
  12.3 53.8 %collective-permute-start.7 = (bf16[512,1088]{0,1:T(8,128)(2,1)S(1)}, bf16[512,1088]{0,1:T(8,128)(2,1)S(1)}, u32[]{:S(2)}, u32[]{:S(2)}) collective-permute-start(bf16[512,1088]{0,1:T(8,128)(2,1)S(1)} %pad_maximum_fusion.3), channel_id=1, source_target_pairs={{0,8},{8,0},{16,24},{24,16},{1,9},{9,1},{17,25},{25,17},{2,10},{10... | collective-permute-start | bytes 3342344 | tf_op jit(solution)/shard_map/ppermute | solution.py:419
  23.8 23.1 %collective-permute-start.2 = (bf16[3,5,64,256]{3,2,1,0:T(8,128)(2,1)S(1)}, bf16[3,5,64,256]{3,2,1,0:T(8,128)(2,1)S(1)}, u32[]{:S(2)}, u32[]{:S(2)}) collective-permute-start(bf16[3,5,64,256]{3,2,1,0:T(8,128)(2,1)S(1)} %get-tuple-element.178), channel_id=1, source_target_pairs={{0,2},{2,4},{4,6},{6,0},{1,3},{3,5},{5,7},{7,1},{8,10},{10,12},{12... | collective-permute-start | bytes 1474568 | tf_op jit(solution)/shard_map/ppermute | solution.py:283
  23.8 42.1 %collective-permute-start.3 = (bf16[3,5,64,256]{3,2,1,0:T(8,128)(2,1)S(1)}, bf16[3,5,64,256]{3,2,1,0:T(8,128)(2,1)S(1)}, u32[]{:S(2)}, u32[]{:S(2)}) collective-permute-start(bf16[3,5,64,256]{3,2,1,0:T(8,128)(2,1)S(1)} %get-tuple-element.177), channel_id=1, source_target_pairs={{0,4},{2,6},{4,0},{6,2},{1,5},{3,7},{5,1},{7,3},{8,12},{10,14},{12... | collective-permute-start | bytes 1474568 | tf_op jit(solution)/shard_map/ppermute | solution.py:283
  120.1 27.8 %collective-permute-start.19 = (bf16[1088,512]{1,0:T(8,128)(2,1)}, bf16[1088,512]{1,0:T(8,128)(2,1)}, u32[]{:S(2)}, u32[]{:S(2)}) collective-permute-start(bf16[1088,512]{1,0:T(8,128)(2,1)} %constant_dynamic-slice_fusion.17), channel_id=1, source_target_pairs={{0,8},{8,0},{16,24},{24,16},{1,9},{9,1},{17,25},{25,17},{2,10},{10... | collective-permute-start | bytes 3342344 | tf_op jit(solution)/shard_map/ppermute | solution.py:466
  121.2 55.5 %collective-permute-start.24 = (bf16[2176,512]{1,0:T(8,128)(2,1)}, bf16[2176,512]{1,0:T(8,128)(2,1)}, u32[]{:S(2)}, u32[]{:S(2)}) collective-permute-start(bf16[2176,512]{1,0:T(8,128)(2,1)} %pad_maximum_fusion.1), channel_id=1, source_target_pairs={{0,16},{8,24},{16,0},{24,8},{1,17},{9,25},{17,1},{25,9},{2,18},{10... | collective-permute-start | bytes 6684680 | tf_op jit(solution)/shard_map/ppermute | solution.py:470
  154.6 44.0 %collective-permute-start.25 = (bf16[544,1088]{1,0:T(8,128)(2,1)}, bf16[544,1088]{1,0:T(8,128)(2,1)}, u32[]{:S(2)}, u32[]{:S(2)}) collective-permute-start(bf16[544,1088]{1,0:T(8,128)(2,1)} %constant_dynamic-slice_fusion.16), channel_id=1, source_target_pairs={{0,16},{8,24},{16,0},{24,8},{1,17},{9,25},{17,1},{25,9},{2,18},{10... | collective-permute-start | bytes 3551240 | tf_op jit(solution)/shard_map/ppermute | solution.py:322
  171.0 29.3 %collective-permute-start.21 = (bf16[3,3,64,256]{3,2,1,0:T(8,128)(2,1)S(1)}, bf16[3,3,64,256]{3,2,1,0:T(8,128)(2,1)S(1)}, u32[]{:S(2)}, u32[]{:S(2)}) collective-permute-start(bf16[3,3,64,256]{3,2,1,0:T(8,128)(2,1)S(1)} %get-tuple-element.187), channel_id=1, source_target_pairs={{0,6},{2,0},{4,2},{6,4},{1,7},{3,1},{5,3},{7,5},{8,14},{10,8},{12,... | collective-permute-start | bytes 884744 | tf_op jit(solution)/shard_map/ppermute | solution.py:293
  176.1 24.2 %collective-permute-start.22 = (bf16[3,3,64,256]{3,2,1,0:T(8,128)(2,1)S(1)}, bf16[3,3,64,256]{3,2,1,0:T(8,128)(2,1)S(1)}, u32[]{:S(2)}, u32[]{:S(2)}) collective-permute-start(bf16[3,3,64,256]{3,2,1,0:T(8,128)(2,1)S(1)} %get-tuple-element.186), channel_id=1, source_target_pairs={{0,4},{2,6},{4,0},{6,2},{1,5},{3,7},{5,1},{7,3},{8,12},{10,14},{12... | collective-permute-start | bytes 884744 | tf_op jit(solution)/shard_map/ppermute | solution.py:293
  176.1 24.2 %collective-permute-start.23 = (bf16[3,3,64,256]{3,2,1,0:T(8,128)(2,1)S(1)}, bf16[3,3,64,256]{3,2,1,0:T(8,128)(2,1)S(1)}, u32[]{:S(2)}, u32[]{:S(2)}) collective-permute-start(bf16[3,3,64,256]{3,2,1,0:T(8,128)(2,1)S(1)} %get-tuple-element.185), channel_id=1, source_target_pairs={{0,2},{2,4},{4,6},{6,0},{1,3},{3,5},{5,7},{7,1},{8,10},{10,12},{12... | collective-permute-start | bytes 884744 | tf_op jit(solution)/shard_map/ppermute | solution.py:293
  200.3 23.5 %collective-permute-start.30 = (bf16[272,1088]{1,0:T(8,128)(2,1)S(1)}, bf16[272,1088]{1,0:T(8,128)(2,1)S(1)}, u32[]{:S(2)}, u32[]{:S(2)}) collective-permute-start(bf16[272,1088]{1,0:T(8,128)(2,1)S(1)} %constant_dynamic-slice_fusion.14), channel_id=1, source_target_pairs={{0,2},{2,0},{4,6},{6,4},{1,3},{3,1},{5,7},{7,5},{8,10},{10,8},{12,... | collective-permute-start | bytes 1775624 | tf_op jit(solution)/shard_map/ppermute | solution.py:322
  201.3 43.1 %collective-permute-start.29 = (bf16[544,1088]{1,0:T(8,128)(2,1)S(1)}, bf16[544,1088]{1,0:T(8,128)(2,1)S(1)}, u32[]{:S(2)}, u32[]{:S(2)}) collective-permute-start(bf16[544,1088]{1,0:T(8,128)(2,1)S(1)} %constant_dynamic-slice_fusion.15), channel_id=1, source_target_pairs={{0,8},{8,0},{16,24},{24,16},{1,9},{9,1},{17,25},{25,17},{2,10},{10... | collective-permute-start | bytes 3551240 | tf_op jit(solution)/shard_map/ppermute | solution.py:322
  205.8 26.5 %collective-permute-start.28 = (bf16[3,2,64,256]{3,2,1,0:T(8,128)(2,1)S(1)}, bf16[3,2,64,256]{3,2,1,0:T(8,128)(2,1)S(1)}, u32[]{:S(2)}, u32[]{:S(2)}) collective-permute-start(bf16[3,2,64,256]{3,2,1,0:T(8,128)(2,1)S(1)} %get-tuple-element.189), channel_id=1, source_target_pairs={{0,2},{2,4},{4,6},{6,0},{1,3},{3,5},{5,7},{7,1},{8,10},{10,12},{12... | collective-permute-start | bytes 589832 | tf_op jit(solution)/shard_map/ppermute | solution.py:293
  262.5 28.4 %collective-permute-start.34 = (bf16[272,2176]{1,0:T(8,128)(2,1)S(1)}, bf16[272,2176]{1,0:T(8,128)(2,1)S(1)}, u32[]{:S(2)}, u32[]{:S(2)}) collective-permute-start(bf16[272,2176]{1,0:T(8,128)(2,1)S(1)} %constant_dynamic-slice_fusion.11), channel_id=1, source_target_pairs={{0,16},{8,24},{16,0},{24,8},{1,17},{9,25},{17,1},{25,9},{2,18},{10... | collective-permute-start | bytes 3551240 | tf_op jit(solution)/shard_map/ppermute | solution.py:322
  264.1 22.8 %collective-permute-start.35 = (bf16[272,1088]{1,0:T(8,128)(2,1)S(1)}, bf16[272,1088]{1,0:T(8,128)(2,1)S(1)}, u32[]{:S(2)}, u32[]{:S(2)}) collective-permute-start(bf16[272,1088]{1,0:T(8,128)(2,1)S(1)} %constant_dynamic-slice_fusion.10), channel_id=1, source_target_pairs={{0,2},{2,0},{4,6},{6,4},{1,3},{3,1},{5,7},{7,5},{8,10},{10,8},{12,... | collective-permute-start | bytes 1775624 | tf_op jit(solution)/shard_map/ppermute | solution.py:322
  264.2 28.1 %collective-permute-start.33 = (bf16[272,2176]{1,0:T(8,128)(2,1)S(1)}, bf16[272,2176]{1,0:T(8,128)(2,1)S(1)}, u32[]{:S(2)}, u32[]{:S(2)}) collective-permute-start(bf16[272,2176]{1,0:T(8,128)(2,1)S(1)} %constant_dynamic-slice_fusion.12), channel_id=1, source_target_pairs={{0,8},{8,0},{16,24},{24,16},{1,9},{9,1},{17,25},{25,17},{2,10},{10... | collective-permute-start | bytes 3551240 | tf_op jit(solution)/shard_map/ppermute | solution.py:322
  295.7 23.2 %collective-permute-start.41 = (bf16[272,1088]{1,0:T(8,128)(2,1)S(1)}, bf16[272,1088]{1,0:T(8,128)(2,1)S(1)}, u32[]{:S(2)}, u32[]{:S(2)}) collective-permute-start(bf16[272,1088]{1,0:T(8,128)(2,1)S(1)} %maximum_select_fusion.16), channel_id=1, source_target_pairs={{0,2},{2,0},{4,6},{6,4},{1,3},{3,1},{5,7},{7,5},{8,10},{10,8},{12,... | collective-permute-start | bytes 1775624 | tf_op jit(solution)/shard_map/ppermute | solution.py:329
  323.8 24.5 %collective-permute-start.47 = (bf16[136,2176]{1,0:T(8,128)(2,1)S(1)}, bf16[136,2176]{1,0:T(8,128)(2,1)S(1)}, u32[]{:S(2)}, u32[]{:S(2)}) collective-permute-start(bf16[136,2176]{1,0:T(8,128)(2,1)S(1)} %constant_dynamic-slice_fusion.5), channel_id=1, source_target_pairs={{0,2},{2,0},{4,6},{6,4},{1,3},{3,1},{5,7},{7,5},{8,10},{10,8},{12,... | collective-permute-start | bytes 1775624 | tf_op jit(solution)/shard_map/ppermute | solution.py:322
  356.2 29.2 %collective-permute-start.49 = (bf16[544,1088]{1,0:T(8,128)(2,1)S(1)}, bf16[544,1088]{1,0:T(8,128)(2,1)S(1)}, u32[]{:S(2)}, u32[]{:S(2)}) collective-permute-start(bf16[544,1088]{1,0:T(8,128)(2,1)S(1)} %maximum_select_fusion.7), channel_id=1, source_target_pairs={{0,8},{8,0},{16,24},{24,16},{1,9},{9,1},{17,25},{25,17},{2,10},{10... | collective-permute-start | bytes 3551240 | tf_op jit(solution)/shard_map/ppermute | solution.py:329
  357.1 30.7 %collective-permute-start.48 = (bf16[272,2176]{1,0:T(8,128)(2,1)S(1)}, bf16[272,2176]{1,0:T(8,128)(2,1)S(1)}, u32[]{:S(2)}, u32[]{:S(2)}) collective-permute-start(bf16[272,2176]{1,0:T(8,128)(2,1)S(1)} %maximum_select_fusion.10), channel_id=1, source_target_pairs={{0,16},{8,24},{16,0},{24,8},{1,17},{9,25},{17,1},{25,9},{2,18},{10... | collective-permute-start | bytes 3551240 | tf_op jit(solution)/shard_map/ppermute | solution.py:329
  406.8 26.4 %collective-permute-start.59 = (bf16[272,2176]{1,0:T(8,128)(2,1)S(1)}, bf16[272,2176]{1,0:T(8,128)(2,1)S(1)}, u32[]{:S(2)}, u32[]{:S(2)}) collective-permute-start(bf16[272,2176]{1,0:T(8,128)(2,1)S(1)} %maximum_select_fusion.11), channel_id=1, source_target_pairs={{0,8},{8,0},{16,24},{24,16},{1,9},{9,1},{17,25},{25,17},{2,10},{10... | collective-permute-start | bytes 3551240 | tf_op jit(solution)/shard_map/ppermute | solution.py:329
  410.2 26.8 %collective-permute-start.58 = (bf16[544,1088]{1,0:T(8,128)(2,1)S(1)}, bf16[544,1088]{1,0:T(8,128)(2,1)S(1)}, u32[]{:S(2)}, u32[]{:S(2)}) collective-permute-start(bf16[544,1088]{1,0:T(8,128)(2,1)S(1)} %maximum_select_fusion.9), channel_id=1, source_target_pairs={{0,16},{8,24},{16,0},{24,8},{1,17},{9,25},{17,1},{25,9},{2,18},{10... | collective-permute-start | bytes 3551240 | tf_op jit(solution)/shard_map/ppermute | solution.py:329
  456.2 23.8 %collective-permute-start.67 = (bf16[272,2176]{1,0:T(8,128)(2,1)S(1)}, bf16[272,2176]{1,0:T(8,128)(2,1)}, u32[]{:S(2)}, u32[]{:S(2)}) collective-permute-start(bf16[272,2176]{1,0:T(8,128)(2,1)S(1)} %maximum_select_fusion.14), channel_id=1, source_target_pairs={{0,16},{8,24},{16,0},{24,8},{1,17},{9,25},{17,1},{25,9},{2,18},{10... | collective-permute-start | bytes 3551240 | tf_op jit(solution)/shard_map/ppermute | solution.py:329
  458.4 26.1 %collective-permute-start.66 = (bf16[272,2176]{1,0:T(8,128)(2,1)S(1)}, bf16[272,2176]{1,0:T(8,128)(2,1)S(1)}, u32[]{:S(2)}, u32[]{:S(2)}) collective-permute-start(bf16[272,2176]{1,0:T(8,128)(2,1)S(1)} %maximum_select_fusion.13), channel_id=1, source_target_pairs={{0,8},{8,0},{16,24},{24,16},{1,9},{9,1},{17,25},{25,17},{2,10},{10... | collective-permute-start | bytes 3551240 | tf_op jit(solution)/shard_map/ppermute | solution.py:329
  (116 other events, 1078.9 us)

commit v3 on v2

--- a/solution.py
+++ b/solution.py
@@ -512,7 +512,7 @@
         )
         backs.append(sent_back(later))
     turns = int(math.log2(count))
-    down_share = reduced(down_share, "ctx", range(turns))
+    down_share = reduced(down_share, "ctx", range(turns - 1))
     up_share = reduced(grad_w_up, "dp", downward[1:])
     attended_both = jnp.concatenate([attended_own, attended_near], axis=1)
     branch_both = jnp.concatenate([grad_branch if cut == group else branch_late, branch_near])
@@ -548,7 +548,16 @@
     second = row_major(
         jnp.concatenate([grad_w_qkv[:, 2 * width :], grad_w_proj], axis=1).astype(low_type)
     )
-    first, second, up_share, down_share = tied(first, second, up_share, down_share)
+    half = down_share.shape[0] // 2
+    high = bit_of("ctx", turns - 1)
+    down_kept = part_of(down_share, high, half)
+    down_near = lax.ppermute(
+        part_of(down_share, 1 - high, half), "ctx", pair_hops("ctx", turns - 1)
+    )
+    first, second, up_share, down_kept, down_near = tied(
+        first, second, up_share, down_kept, down_near
+    )
+    down_share = (wide(down_kept) + wide(down_near)).astype(low_type)
 
     first, second = reduced(first, "dp", upward[:1]), reduced(second, "dp", downward[:1])
     up_share = reduced(up_share, "ctx", range(1))

time: 498 us -> 489 us (0.982)
    ppermute x12 -> x11, waiting for transfers between devices: 71.4 us -> 59.5 us  [reduced(): lax.ppermute(part_of(array, 1 - high, half), axis, pair_hops(axis, bit))]
    ppermute x0 -> x1, waiting for transfers between devices: none -> 8.86 us  [local(): lax.ppermute(part_of(down_share, 1 - high, half), 'ctx', pair_hops('ctx',...]
    ppermute x12 -> x11, starting transfers between devices: 18.7 us -> 16.7 us  [reduced(): lax.ppermute(part_of(array, 1 - high, half), axis, pair_hops(axis, bit))]
    unnamed x146 -> x156, local copies, waits for them, and re-layouts: 10.3 us -> 10.5 us
  transfers between devices with their start and end apart: 68 -> 68, of which waited for: 36 -> 38; matrix products, arithmetic and copies ran while one was open for 17% -> 18% of each run, Pallas kernels for 3% -> 3%
where the time goes in v3:
time: 489 us; the launch traced here: 481 us
  waiting for transfers between devices  242 us (49%)
  starting transfers between devices  75 us (15%)
  matrix products  56.1 us (11%)
  other arithmetic  43.6 us (9%)
  local copies, waits for them, and re-layouts  35.6 us (7%)
  Pallas kernels  25.3 us (5%)
    ppermute x18, waiting for transfers between devices, spread(): arrived = lax.ppermute(array, axis, pair_hops(axis, bit))  86.9 us
    ppermute x11, waiting for transfers between devices, reduced(): lax.ppermute(part_of(array, 1 - high, half), axis, pair_hops(axis, bit))  59.5 us
    dot_general x18, matrix products, contract(): lax.dot_general(first, second, (((first_dim,), (second_dim,)), ((), ())),...  56.1 us
    ppermute x6, waiting for transfers between devices, scattered(): piece = lax.ppermute(piece, 'ctx', hops)  44 us
    ppermute x9, waiting for transfers between devices, sent_back(): back.append(lax.ppermute(pieces[shift], 'ctx', hops))  31.1 us
    ppermute x18, starting transfers between devices, spread(): arrived = lax.ppermute(array, axis, pair_hops(axis, bit))  19.7 us
    select_n x22, other arithmetic, in_order(): jnp.where(flip, jnp.concatenate([second, first], axis), jnp.concatenate([...  16.9 us
    ppermute x11, starting transfers between devices, reduced(): lax.ppermute(part_of(array, 1 - high, half), axis, pair_hops(axis, bit))  16.7 us
  transfers between devices with their start and end apart: 68, of which 38 were waited for; matrix products, arithmetic and copies ran while one was open for 18% of the time, Pallas kernels for 3%

profile of v3, /device:TPU:0, one launch (start us, length us, event | category | flops | bytes accessed | tf_op | source)
XLA Modules:
  0.0 480.8 jit_solution(17938321376115144967)
XLA Ops:
  24.8 5.8 %convolution_bitcast_fusion = f32[2176,512]{1,0:T(8,128)} fusion(bf16[2176,1088]{0,1:T(8,128)(2,1)S(1)} %bitcast.174, bf16[256,1088]{0,1:T(8,128)(2,1)S(1)} %collective-permute-done.6, bf16[128,1088]{0,1:T(8,128)(2,1)S(1)} %collective-permute-done.5, bf16[128,1088]{0,1:T(8,128)(2,1)S(1)} %get-tuple-element.211), kind=kOutput, calls=%fused_computation.12 | convolution fusion | flops 2427650048 | bytes 10305536 | tf_op jit(solution)/shard_map/dot_general | solution.py:35
  35.4 11.5 %collective-permute-done.2 = bf16[3,5,64,256]{3,2,1,0:T(8,128)(2,1)S(1)} collective-permute-done((bf16[3,5,64,256]{3,2,1,0:T(8,128)(2,1)S(1)}, bf16[3,5,64,256]{3,2,1,0:T(8,128)(2,1)S(1)}, u32[]{:S(2)}, u32[]{:S(2)}) %collective-permute-start.2) | collective-permute-done | bytes 491552 | tf_op jit(solution)/shard_map/ppermute | solution.py:283
  46.9 19.0 %collective-permute-done.3 = bf16[3,5,64,256]{3,2,1,0:T(8,128)(2,1)S(1)} collective-permute-done((bf16[3,5,64,256]{3,2,1,0:T(8,128)(2,1)S(1)}, bf16[3,5,64,256]{3,2,1,0:T(8,128)(2,1)S(1)}, u32[]{:S(2)}, u32[]{:S(2)}) %collective-permute-start.3) | collective-permute-done | bytes 491552 | tf_op jit(solution)/shard_map/ppermute | solution.py:283
  66.8 9.7 %shard_map.271 = (bf16[4,5,64,256]{3,2,1,0:T(8,128)(2,1)S(1)}, f32[5,4,256]{2,1,0:T(4,128)S(1)}) custom-call(s32[8]{0:T(128)S(1)} %gather_fusion, bf16[4,3,5,64,256]{4,3,2,1,0:T(8,128)(2,1)S(1)} %pad_maximum_fusion.2.mixed_ref), custom_call_target="tpu_custom_call" | custom-call | flops 838860800 | bytes 2621440 | tf_op jit(solution)/shard_map/pallas_call | solution.py:204
  84.1 9.2 %collective-permute-done.10 = bf16[5,64,256]{2,1,0:T(8,128)(2,1)S(1)} collective-permute-done((bf16[5,64,256]{2,1,0:T(8,128)(2,1)S(1)}, bf16[5,64,256]{2,1,0:T(8,128)(2,1)S(1)}, u32[]{:S(2)}, u32[]{:S(2)}) %collective-permute-start.10) | collective-permute-done | bytes 163872 | tf_op jit(solution)/shard_map/ppermute | solution.py:293
  100.4 10.5 %multiply_convert_fusion = (bf16[2176,512]{1,0:T(8,128)(2,1)}, bf16[2176,512]{1,0:T(8,128)(2,1)S(1)}) fusion(f32[2176,512]{1,0:T(8,128)} %convolution_bitcast_fusion, f32[2176]{0:T(1024)S(1)} %convert_element_type.237, bf16[512,1088]{0,1:T(8,128)(2,1)S(1)} %constant_dynamic-update-slice_fusion, bf16[1088,2176]{1,0:T(8,128)(2,1)} %param.27), kind=kOutput, calls=%fused_computation.25 | convolution fusion | flops 2449932288 | bytes 14770688 | tf_op jit(solution)/shard_map/dot_general | solution.py:35
  141.0 5.7 %collective-permute-done.17 = bf16[1,5,64,256]{3,2,1,0:T(8,128)(2,1)S(1)} collective-permute-done((bf16[1,5,64,256]{3,2,1,0:T(8,128)(2,1)S(1)}, bf16[1,5,64,256]{3,2,1,0:T(8,128)(2,1)S(1)}, u32[]{:S(2)}, u32[]{:S(2)}) %collective-permute-start.17) | collective-permute-done | bytes 163872 | tf_op jit(solution)/shard_map/ppermute | solution.py:283
  155.8 9.2 %shard_map.272 = bf16[4,3,3,64,256]{4,3,2,1,0:T(8,128)(2,1)S(1)} custom-call(s32[8]{0:T(128)S(1)} %gather_fusion, bf16[4,3,5,64,256]{4,3,2,1,0:T(8,128)(2,1)S(1)} %pad_maximum_fusion.2.mixed_ref, bf16[4,5,64,256]{3,2,1,0:T(8,128)(2,1)S(1)} %get-tuple-element.86.out_ref, bf16[4,5,64,256]{3,2,1,0:T(8,128)(2,1)S(1)} %maximum_bitcast_fusion.grad_ref, ...), custom_call_target="tpu_custom_call" | custom-call | tf_op jit(solution)/shard_map/pallas_call | solution.py:238
  165.1 6.4 %shard_map.273 = bf16[4,3,2,64,256]{4,3,2,1,0:T(8,128)(2,1)S(1)} custom-call(s32[8]{0:T(128)S(1)} %gather_fusion, bf16[4,3,5,64,256]{4,3,2,1,0:T(8,128)(2,1)S(1)} %pad_maximum_fusion.2.mixed_ref, bf16[4,5,64,256]{3,2,1,0:T(8,128)(2,1)S(1)} %get-tuple-element.86.out_ref, bf16[4,5,64,256]{3,2,1,0:T(8,128)(2,1)S(1)} %maximum_bitcast_fusion.grad_ref, ...), custom_call_target="tpu_custom_call" | custom-call | tf_op jit(solution)/shard_map/pallas_call | solution.py:238
  171.6 5.1 %collective-permute-start.21 = (bf16[3,3,64,256]{3,2,1,0:T(8,128)(2,1)S(1)}, bf16[3,3,64,256]{3,2,1,0:T(8,128)(2,1)S(1)}, u32[]{:S(2)}, u32[]{:S(2)}) collective-permute-start(bf16[3,3,64,256]{3,2,1,0:T(8,128)(2,1)S(1)} %get-tuple-element.189), channel_id=1, source_target_pairs={{0,6},{2,0},{4,2},{6,4},{1,7},{3,1},{5,3},{7,5},{8,14},{10,8},{12,... | collective-permute-start | bytes 884744 | tf_op jit(solution)/shard_map/ppermute | solution.py:293
  182.5 16.7 %collective-permute-done.25 = bf16[544,1088]{1,0:T(8,128)(2,1)} collective-permute-done((bf16[544,1088]{1,0:T(8,128)(2,1)}, bf16[544,1088]{1,0:T(8,128)(2,1)}, u32[]{:S(2)}, u32[]{:S(2)}) %collective-permute-start.25) | collective-permute-done | bytes 1183776 | tf_op jit(solution)/shard_map/ppermute | solution.py:322
  211.5 13.0 %collective-permute-done.26 = bf16[3,2,64,256]{3,2,1,0:T(8,128)(2,1)S(1)} collective-permute-done((bf16[3,2,64,256]{3,2,1,0:T(8,128)(2,1)S(1)}, bf16[3,2,64,256]{3,2,1,0:T(8,128)(2,1)S(1)}, u32[]{:S(2)}, u32[]{:S(2)}) %collective-permute-start.26) | collective-permute-done | bytes 196640 | tf_op jit(solution)/shard_map/ppermute | solution.py:293
  224.8 6.0 %collective-permute-done.28 = bf16[3,2,64,256]{3,2,1,0:T(8,128)(2,1)S(1)} collective-permute-done((bf16[3,2,64,256]{3,2,1,0:T(8,128)(2,1)S(1)}, bf16[3,2,64,256]{3,2,1,0:T(8,128)(2,1)S(1)}, u32[]{:S(2)}, u32[]{:S(2)}) %collective-permute-start.28) | collective-permute-done | bytes 196640 | tf_op jit(solution)/shard_map/ppermute | solution.py:293
  245.7 8.9 %collective-permute-done.32 = bf16[136,1088]{1,0:T(8,128)(2,1)S(1)} collective-permute-done((bf16[136,1088]{1,0:T(8,128)(2,1)S(1)}, bf16[136,1088]{1,0:T(8,128)(2,1)S(1)}, u32[]{:S(2)}, u32[]{:S(2)}) %collective-permute-start.32) | collective-permute-done | bytes 295968 | tf_op jit(solution)/shard_map/ppermute | solution.py:554
  260.5 11.0 %collective-permute-done.36 = bf16[136,1088]{1,0:T(8,128)(2,1)S(1)} collective-permute-done((bf16[136,1088]{1,0:T(8,128)(2,1)S(1)}, bf16[136,1088]{1,0:T(8,128)(2,1)S(1)}, u32[]{:S(2)}, u32[]{:S(2)}) %collective-permute-start.36) | collective-permute-done | bytes 295968 | tf_op jit(solution)/shard_map/ppermute | solution.py:329
  271.6 8.1 %collective-permute-done.35 = bf16[272,1088]{1,0:T(8,128)(2,1)S(1)} collective-permute-done((bf16[272,1088]{1,0:T(8,128)(2,1)S(1)}, bf16[272,1088]{1,0:T(8,128)(2,1)S(1)}, u32[]{:S(2)}, u32[]{:S(2)}) %collective-permute-start.35) | collective-permute-done | bytes 591904 | tf_op jit(solution)/shard_map/ppermute | solution.py:322
  293.9 17.3 %collective-permute-done.40 = bf16[136,1088]{1,0:T(8,128)(2,1)S(1)} collective-permute-done((bf16[136,1088]{1,0:T(8,128)(2,1)S(1)}, bf16[136,1088]{1,0:T(8,128)(2,1)S(1)}, u32[]{:S(2)}, u32[]{:S(2)}) %collective-permute-start.40) | collective-permute-done | bytes 295968 | tf_op jit(solution)/shard_map/ppermute | solution.py:322
  326.7 12.8 %collective-permute-done.46 = bf16[136,1088]{1,0:T(8,128)(2,1)S(1)} collective-permute-done((bf16[136,1088]{1,0:T(8,128)(2,1)S(1)}, bf16[136,1088]{1,0:T(8,128)(2,1)S(1)}, u32[]{:S(2)}, u32[]{:S(2)}) %collective-permute-start.46) | collective-permute-done | bytes 295968 | tf_op jit(solution)/shard_map/ppermute | solution.py:329
  351.8 10.9 %collective-permute-done.51 = bf16[68,2176]{1,0:T(8,128)(2,1)S(1)} collective-permute-done((bf16[68,2176]{1,0:T(8,128)(2,1)S(1)}, bf16[68,2176]{1,0:T(8,128)(2,1)S(1)}, u32[]{:S(2)}, u32[]{:S(2)}) %collective-permute-start.51) | collective-permute-done | bytes 295968 | tf_op jit(solution)/shard_map/ppermute | solution.py:322
  362.8 6.5 %collective-permute-done.50 = bf16[272,1088]{1,0:T(8,128)(2,1)S(1)} collective-permute-done((bf16[272,1088]{1,0:T(8,128)(2,1)S(1)}, bf16[272,1088]{1,0:T(8,128)(2,1)S(1)}, u32[]{:S(2)}, u32[]{:S(2)}) %collective-permute-start.50) | collective-permute-done | bytes 591904 | tf_op jit(solution)/shard_map/ppermute | solution.py:329
  369.8 7.8 %collective-permute-done.49 = bf16[544,1088]{1,0:T(8,128)(2,1)S(1)} collective-permute-done((bf16[544,1088]{1,0:T(8,128)(2,1)S(1)}, bf16[544,1088]{1,0:T(8,128)(2,1)S(1)}, u32[]{:S(2)}, u32[]{:S(2)}) %collective-permute-start.49) | collective-permute-done | bytes 1183776 | tf_op jit(solution)/shard_map/ppermute | solution.py:329
  389.8 7.1 %collective-permute-done.56 = bf16[68,2176]{1,0:T(8,128)(2,1)S(1)} collective-permute-done((bf16[68,2176]{1,0:T(8,128)(2,1)S(1)}, bf16[68,2176]{1,0:T(8,128)(2,1)S(1)}, u32[]{:S(2)}, u32[]{:S(2)}) %collective-permute-start.56) | collective-permute-done | bytes 295968 | tf_op jit(solution)/shard_map/ppermute | solution.py:329
  414.9 11.2 %collective-permute-done.59 = bf16[272,2176]{1,0:T(8,128)(2,1)S(1)} collective-permute-done((bf16[272,2176]{1,0:T(8,128)(2,1)S(1)}, bf16[272,2176]{1,0:T(8,128)(2,1)S(1)}, u32[]{:S(2)}, u32[]{:S(2)}) %collective-permute-start.59) | collective-permute-done | bytes 1183776 | tf_op jit(solution)/shard_map/ppermute | solution.py:329
  459.1 12.3 %collective-permute-done.67 = bf16[272,2176]{1,0:T(8,128)(2,1)} collective-permute-done((bf16[272,2176]{1,0:T(8,128)(2,1)S(1)}, bf16[272,2176]{1,0:T(8,128)(2,1)}, u32[]{:S(2)}, u32[]{:S(2)}) %collective-permute-start.67) | collective-permute-done | bytes 1183776 | tf_op jit(solution)/shard_map/ppermute | solution.py:329
  (451 shorter events, 236.3 us)
Async XLA Ops:
  9.4 56.8 %collective-permute-start.8 = (bf16[256,544]{0,1:T(8,128)(2,1)S(1)}, bf16[256,544]{0,1:T(8,128)(2,1)S(1)}, u32[]{:S(2)}, u32[]{:S(2)}) collective-permute-start(bf16[256,544]{0,1:T(8,128)(2,1)S(1)} %get-tuple-element.213), channel_id=1, source_target_pairs={{0,1},{1,0},{2,3},{3,2},{4,5},{5,4},{6,7},{7,6},{8,9},{9,8},{10,11... | collective-permute-start | bytes 835592 | tf_op jit(solution)/shard_map/ppermute | solution.py:262
  12.4 53.8 %collective-permute-start.7 = (bf16[512,1088]{0,1:T(8,128)(2,1)S(1)}, bf16[512,1088]{0,1:T(8,128)(2,1)S(1)}, u32[]{:S(2)}, u32[]{:S(2)}) collective-permute-start(bf16[512,1088]{0,1:T(8,128)(2,1)S(1)} %pad_maximum_fusion.3), channel_id=1, source_target_pairs={{0,8},{8,0},{16,24},{24,16},{1,9},{9,1},{17,25},{25,17},{2,10},{10... | collective-permute-start | bytes 3342344 | tf_op jit(solution)/shard_map/ppermute | solution.py:419
  23.8 23.2 %collective-permute-start.2 = (bf16[3,5,64,256]{3,2,1,0:T(8,128)(2,1)S(1)}, bf16[3,5,64,256]{3,2,1,0:T(8,128)(2,1)S(1)}, u32[]{:S(2)}, u32[]{:S(2)}) collective-permute-start(bf16[3,5,64,256]{3,2,1,0:T(8,128)(2,1)S(1)} %get-tuple-element.180), channel_id=1, source_target_pairs={{0,2},{2,4},{4,6},{6,0},{1,3},{3,5},{5,7},{7,1},{8,10},{10,12},{12... | collective-permute-start | bytes 1474568 | tf_op jit(solution)/shard_map/ppermute | solution.py:283
  23.8 42.1 %collective-permute-start.3 = (bf16[3,5,64,256]{3,2,1,0:T(8,128)(2,1)S(1)}, bf16[3,5,64,256]{3,2,1,0:T(8,128)(2,1)S(1)}, u32[]{:S(2)}, u32[]{:S(2)}) collective-permute-start(bf16[3,5,64,256]{3,2,1,0:T(8,128)(2,1)S(1)} %get-tuple-element.179), channel_id=1, source_target_pairs={{0,4},{2,6},{4,0},{6,2},{1,5},{3,7},{5,1},{7,3},{8,12},{10,14},{12... | collective-permute-start | bytes 1474568 | tf_op jit(solution)/shard_map/ppermute | solution.py:283
  120.7 27.8 %collective-permute-start.19 = (bf16[1088,512]{1,0:T(8,128)(2,1)}, bf16[1088,512]{1,0:T(8,128)(2,1)}, u32[]{:S(2)}, u32[]{:S(2)}) collective-permute-start(bf16[1088,512]{1,0:T(8,128)(2,1)} %constant_dynamic-slice_fusion.18), channel_id=1, source_target_pairs={{0,8},{8,0},{16,24},{24,16},{1,9},{9,1},{17,25},{25,17},{2,10},{10... | collective-permute-start | bytes 3342344 | tf_op jit(solution)/shard_map/ppermute | solution.py:466
  121.8 55.5 %collective-permute-start.24 = (bf16[2176,512]{1,0:T(8,128)(2,1)}, bf16[2176,512]{1,0:T(8,128)(2,1)}, u32[]{:S(2)}, u32[]{:S(2)}) collective-permute-start(bf16[2176,512]{1,0:T(8,128)(2,1)} %pad_maximum_fusion.1), channel_id=1, source_target_pairs={{0,16},{8,24},{16,0},{24,8},{1,17},{9,25},{17,1},{25,9},{2,18},{10... | collective-permute-start | bytes 6684680 | tf_op jit(solution)/shard_map/ppermute | solution.py:470
  155.2 44.0 %collective-permute-start.25 = (bf16[544,1088]{1,0:T(8,128)(2,1)}, bf16[544,1088]{1,0:T(8,128)(2,1)}, u32[]{:S(2)}, u32[]{:S(2)}) collective-permute-start(bf16[544,1088]{1,0:T(8,128)(2,1)} %constant_dynamic-slice_fusion.17), channel_id=1, source_target_pairs={{0,16},{8,24},{16,0},{24,8},{1,17},{9,25},{17,1},{25,9},{2,18},{10... | collective-permute-start | bytes 3551240 | tf_op jit(solution)/shard_map/ppermute | solution.py:322
  171.6 29.3 %collective-permute-start.21 = (bf16[3,3,64,256]{3,2,1,0:T(8,128)(2,1)S(1)}, bf16[3,3,64,256]{3,2,1,0:T(8,128)(2,1)S(1)}, u32[]{:S(2)}, u32[]{:S(2)}) collective-permute-start(bf16[3,3,64,256]{3,2,1,0:T(8,128)(2,1)S(1)} %get-tuple-element.189), channel_id=1, source_target_pairs={{0,6},{2,0},{4,2},{6,4},{1,7},{3,1},{5,3},{7,5},{8,14},{10,8},{12,... | collective-permute-start | bytes 884744 | tf_op jit(solution)/shard_map/ppermute | solution.py:293
  176.6 24.2 %collective-permute-start.22 = (bf16[3,3,64,256]{3,2,1,0:T(8,128)(2,1)S(1)}, bf16[3,3,64,256]{3,2,1,0:T(8,128)(2,1)S(1)}, u32[]{:S(2)}, u32[]{:S(2)}) collective-permute-start(bf16[3,3,64,256]{3,2,1,0:T(8,128)(2,1)S(1)} %get-tuple-element.188), channel_id=1, source_target_pairs={{0,4},{2,6},{4,0},{6,2},{1,5},{3,7},{5,1},{7,3},{8,12},{10,14},{12... | collective-permute-start | bytes 884744 | tf_op jit(solution)/shard_map/ppermute | solution.py:293
  176.6 24.2 %collective-permute-start.23 = (bf16[3,3,64,256]{3,2,1,0:T(8,128)(2,1)S(1)}, bf16[3,3,64,256]{3,2,1,0:T(8,128)(2,1)S(1)}, u32[]{:S(2)}, u32[]{:S(2)}) collective-permute-start(bf16[3,3,64,256]{3,2,1,0:T(8,128)(2,1)S(1)} %get-tuple-element.187), channel_id=1, source_target_pairs={{0,2},{2,4},{4,6},{6,0},{1,3},{3,5},{5,7},{7,1},{8,10},{10,12},{12... | collective-permute-start | bytes 884744 | tf_op jit(solution)/shard_map/ppermute | solution.py:293
  201.0 30.0 %collective-permute-start.30 = (bf16[272,1088]{1,0:T(8,128)(2,1)S(1)}, bf16[272,1088]{1,0:T(8,128)(2,1)S(1)}, u32[]{:S(2)}, u32[]{:S(2)}) collective-permute-start(bf16[272,1088]{1,0:T(8,128)(2,1)S(1)} %constant_dynamic-slice_fusion.15), channel_id=1, source_target_pairs={{0,2},{2,0},{4,6},{6,4},{1,3},{3,1},{5,7},{7,5},{8,10},{10,8},{12,... | collective-permute-start | bytes 1775624 | tf_op jit(solution)/shard_map/ppermute | solution.py:322
  201.9 30.1 %collective-permute-start.29 = (bf16[544,1088]{1,0:T(8,128)(2,1)S(1)}, bf16[544,1088]{1,0:T(8,128)(2,1)S(1)}, u32[]{:S(2)}, u32[]{:S(2)}) collective-permute-start(bf16[544,1088]{1,0:T(8,128)(2,1)S(1)} %constant_dynamic-slice_fusion.16), channel_id=1, source_target_pairs={{0,8},{8,0},{16,24},{24,16},{1,9},{9,1},{17,25},{25,17},{2,10},{10... | collective-permute-start | bytes 3551240 | tf_op jit(solution)/shard_map/ppermute | solution.py:322
  206.4 24.4 %collective-permute-start.28 = (bf16[3,2,64,256]{3,2,1,0:T(8,128)(2,1)S(1)}, bf16[3,2,64,256]{3,2,1,0:T(8,128)(2,1)S(1)}, u32[]{:S(2)}, u32[]{:S(2)}) collective-permute-start(bf16[3,2,64,256]{3,2,1,0:T(8,128)(2,1)S(1)} %get-tuple-element.191), channel_id=1, source_target_pairs={{0,2},{2,4},{4,6},{6,0},{1,3},{3,5},{5,7},{7,1},{8,10},{10,12},{12... | collective-permute-start | bytes 589832 | tf_op jit(solution)/shard_map/ppermute | solution.py:293
  254.8 28.1 %collective-permute-start.34 = (bf16[272,2176]{1,0:T(8,128)(2,1)S(1)}, bf16[272,2176]{1,0:T(8,128)(2,1)S(1)}, u32[]{:S(2)}, u32[]{:S(2)}) collective-permute-start(bf16[272,2176]{1,0:T(8,128)(2,1)S(1)} %constant_dynamic-slice_fusion.11), channel_id=1, source_target_pairs={{0,16},{8,24},{16,0},{24,8},{1,17},{9,25},{17,1},{25,9},{2,18},{10... | collective-permute-start | bytes 3551240 | tf_op jit(solution)/shard_map/ppermute | solution.py:322
  256.4 23.4 %collective-permute-start.35 = (bf16[272,1088]{1,0:T(8,128)(2,1)S(1)}, bf16[272,1088]{1,0:T(8,128)(2,1)S(1)}, u32[]{:S(2)}, u32[]{:S(2)}) collective-permute-start(bf16[272,1088]{1,0:T(8,128)(2,1)S(1)} %constant_dynamic-slice_fusion.10), channel_id=1, source_target_pairs={{0,2},{2,0},{4,6},{6,4},{1,3},{3,1},{5,7},{7,5},{8,10},{10,8},{12,... | collective-permute-start | bytes 1775624 | tf_op jit(solution)/shard_map/ppermute | solution.py:322
  259.5 27.2 %collective-permute-start.33 = (bf16[272,2176]{1,0:T(8,128)(2,1)S(1)}, bf16[272,2176]{1,0:T(8,128)(2,1)S(1)}, u32[]{:S(2)}, u32[]{:S(2)}) collective-permute-start(bf16[272,2176]{1,0:T(8,128)(2,1)S(1)} %constant_dynamic-slice_fusion.12), channel_id=1, source_target_pairs={{0,8},{8,0},{16,24},{24,16},{1,9},{9,1},{17,25},{25,17},{2,10},{10... | collective-permute-start | bytes 3551240 | tf_op jit(solution)/shard_map/ppermute | solution.py:322
  290.0 23.2 %collective-permute-start.41 = (bf16[272,1088]{1,0:T(8,128)(2,1)S(1)}, bf16[272,1088]{1,0:T(8,128)(2,1)S(1)}, u32[]{:S(2)}, u32[]{:S(2)}) collective-permute-start(bf16[272,1088]{1,0:T(8,128)(2,1)S(1)} %maximum_select_fusion.16), channel_id=1, source_target_pairs={{0,2},{2,0},{4,6},{6,4},{1,3},{3,1},{5,7},{7,5},{8,10},{10,8},{12,... | collective-permute-start | bytes 1775624 | tf_op jit(solution)/shard_map/ppermute | solution.py:329
  317.4 22.9 %collective-permute-start.47 = (bf16[136,2176]{1,0:T(8,128)(2,1)S(1)}, bf16[136,2176]{1,0:T(8,128)(2,1)S(1)}, u32[]{:S(2)}, u32[]{:S(2)}) collective-permute-start(bf16[136,2176]{1,0:T(8,128)(2,1)S(1)} %constant_dynamic-slice_fusion.5), channel_id=1, source_target_pairs={{0,2},{2,0},{4,6},{6,4},{1,3},{3,1},{5,7},{7,5},{8,10},{10,8},{12,... | collective-permute-start | bytes 1775624 | tf_op jit(solution)/shard_map/ppermute | solution.py:322
  348.4 29.2 %collective-permute-start.49 = (bf16[544,1088]{1,0:T(8,128)(2,1)S(1)}, bf16[544,1088]{1,0:T(8,128)(2,1)S(1)}, u32[]{:S(2)}, u32[]{:S(2)}) collective-permute-start(bf16[544,1088]{1,0:T(8,128)(2,1)S(1)} %maximum_select_fusion.7), channel_id=1, source_target_pairs={{0,8},{8,0},{16,24},{24,16},{1,9},{9,1},{17,25},{25,17},{2,10},{10... | collective-permute-start | bytes 3551240 | tf_op jit(solution)/shard_map/ppermute | solution.py:329
  349.3 30.7 %collective-permute-start.48 = (bf16[272,2176]{1,0:T(8,128)(2,1)S(1)}, bf16[272,2176]{1,0:T(8,128)(2,1)S(1)}, u32[]{:S(2)}, u32[]{:S(2)}) collective-permute-start(bf16[272,2176]{1,0:T(8,128)(2,1)S(1)} %maximum_select_fusion.10), channel_id=1, source_target_pairs={{0,16},{8,24},{16,0},{24,8},{1,17},{9,25},{17,1},{25,9},{2,18},{10... | collective-permute-start | bytes 3551240 | tf_op jit(solution)/shard_map/ppermute | solution.py:329
  400.9 25.3 %collective-permute-start.59 = (bf16[272,2176]{1,0:T(8,128)(2,1)S(1)}, bf16[272,2176]{1,0:T(8,128)(2,1)S(1)}, u32[]{:S(2)}, u32[]{:S(2)}) collective-permute-start(bf16[272,2176]{1,0:T(8,128)(2,1)S(1)} %maximum_select_fusion.11), channel_id=1, source_target_pairs={{0,8},{8,0},{16,24},{24,16},{1,9},{9,1},{17,25},{25,17},{2,10},{10... | collective-permute-start | bytes 3551240 | tf_op jit(solution)/shard_map/ppermute | solution.py:329
  403.2 26.6 %collective-permute-start.58 = (bf16[544,1088]{1,0:T(8,128)(2,1)S(1)}, bf16[544,1088]{1,0:T(8,128)(2,1)S(1)}, u32[]{:S(2)}, u32[]{:S(2)}) collective-permute-start(bf16[544,1088]{1,0:T(8,128)(2,1)S(1)} %maximum_select_fusion.9), channel_id=1, source_target_pairs={{0,16},{8,24},{16,0},{24,8},{1,17},{9,25},{17,1},{25,9},{2,18},{10... | collective-permute-start | bytes 3551240 | tf_op jit(solution)/shard_map/ppermute | solution.py:329
  448.5 22.9 %collective-permute-start.67 = (bf16[272,2176]{1,0:T(8,128)(2,1)S(1)}, bf16[272,2176]{1,0:T(8,128)(2,1)}, u32[]{:S(2)}, u32[]{:S(2)}) collective-permute-start(bf16[272,2176]{1,0:T(8,128)(2,1)S(1)} %maximum_select_fusion.14), channel_id=1, source_target_pairs={{0,16},{8,24},{16,0},{24,8},{1,17},{9,25},{17,1},{25,9},{2,18},{10... | collective-permute-start | bytes 3551240 | tf_op jit(solution)/shard_map/ppermute | solution.py:329
  450.4 25.5 %collective-permute-start.66 = (bf16[272,2176]{1,0:T(8,128)(2,1)S(1)}, bf16[272,2176]{1,0:T(8,128)(2,1)S(1)}, u32[]{:S(2)}, u32[]{:S(2)}) collective-permute-start(bf16[272,2176]{1,0:T(8,128)(2,1)S(1)} %maximum_select_fusion.13), channel_id=1, source_target_pairs={{0,8},{8,0},{16,24},{24,16},{1,9},{9,1},{17,25},{25,17},{2,10},{10... | collective-permute-start | bytes 3551240 | tf_op jit(solution)/shard_map/ppermute | solution.py:329
  (121 other events, 1109.8 us)

commit v4 on v3

--- a/solution.py
+++ b/solution.py
@@ -416,8 +416,6 @@
     other_proj = swapped(w_proj)
     grad_low = by_sequence(cotangent)
     grad_rows = jnp.concatenate([grad_low, swapped(grad_low)], axis=0)
-    grad_rows_near = lax.ppermute(grad_rows, "dp", pair_hops("dp", 0))
-    grad_act = contract(w_down, grad_rows, 1, 1)
 
     inputs = wide(rows_low)
     normed, norm_one_pull = jax.vjp(layer_norm, inputs, wide(ln1_gain), wide(ln1_bias))
@@ -445,8 +443,11 @@
         return array[:, :HEADS].reshape(-1, rows)
 
     normed_near = swapped(normed_other)
+    sends, grad_rows = tied(to_heads(mixed), grad_rows)
+    grad_rows_near = lax.ppermute(grad_rows, "dp", pair_hops("dp", 0))
+    grad_act = contract(w_down, grad_rows, 1, 1)
     mixed_heads, grad_act, grad_rows_near, normed_near = tied(
-        scattered(to_heads(mixed)), grad_act, grad_rows_near, normed_near
+        scattered(sends), grad_act, grad_rows_near, normed_near
     )
     out_heads, lse = attention_forward(ranks, mixed_heads)
     attended = from_heads(assembled([sent_back(out_heads)], ((0, group),)))
@@ -619,9 +620,22 @@
     first, second, small, up_total = tied(first, second, small, up_total)
 
     small_total = summed(small, "ctx", range(1, turns))
-    first, second = spread(first, "dp", downward[1:]), spread(second, "dp", upward[1:])
-    qkv_total = jnp.concatenate([wide(first), wide(second[:, :width])], axis=1)
-    proj_total = wide(second[:, width:])
+    first, second = spread(first, "dp", downward[1:-1]), spread(second, "dp", upward[1:-1])
+    size = first.shape[0]
+    qkv_total = jnp.zeros((2 * size, 3 * width), full_type)
+    proj_total = jnp.zeros((2 * size, width), full_type)
+    for near in (False, True):
+        ends = []
+        for part, bit in ((first, downward[-1]), (second, upward[-1])):
+            high = bit_of("dp", bit)
+            if near:
+                part = lax.ppermute(part, "dp", pair_hops("dp", bit))
+                high = 1 - high
+            ends.append((wide(part), high * size))
+        (one, one_at), (two, two_at) = ends
+        qkv_total = lax.dynamic_update_slice(qkv_total, one, (one_at, 0))
+        qkv_total = lax.dynamic_update_slice(qkv_total, two[:, :width], (two_at, 2 * width))
+        proj_total = lax.dynamic_update_slice(proj_total, two[:, width:], (two_at, 0))
     up_bias_total = small_total[8:].reshape(-1)[: grad_up_bias.shape[0]]
     return (
         output,

time: 489 us -> 490 us (level)
  waiting for transfers between devices: 242 us -> 232 us
  local copies, waits for them, and re-layouts: 35.6 us -> 44.1 us
    ppermute x18 -> x16, waiting for transfers between devices: 86.9 us -> 73.9 us  [spread(): arrived = lax.ppermute(array, axis, pair_hops(axis, bit))]
    ppermute x6, waiting for transfers between devices: 44 us -> 32.1 us  [scattered(): piece = lax.ppermute(piece, 'ctx', hops)]
    ppermute x0 -> x2, waiting for transfers between devices: none -> 10.2 us  [local(): part = lax.ppermute(part, 'dp', pair_hops('dp', bit))]
    ppermute x9, starting transfers between devices: 14.3 us -> 20.4 us  [sent_back(): back.append(lax.ppermute(pieces[shift], 'ctx', hops))]
    unnamed x156 -> x140, local copies, waits for them, and re-layouts: 10.5 us -> 15.2 us
    ppermute x18 -> x16, starting transfers between devices: 19.7 us -> 15.8 us  [spread(): arrived = lax.ppermute(array, axis, pair_hops(axis, bit))]
    select_n x22 -> x20, other arithmetic: 16.9 us -> 13.6 us  [in_order(): jnp.where(flip, jnp.concatenate([second, first], axis), jnp.concatenate([...]
  transfers between devices with their start and end apart: 68 -> 68, of which waited for: 38 -> 32; matrix products, arithmetic and copies ran while one was open for 18% -> 17% of each run, Pallas kernels for 3% -> 3%
where the time goes in v4:
time: 490 us; the launch traced here: 481 us
  waiting for transfers between devices  232 us (47%)
  starting transfers between devices  79.6 us (16%)
  matrix products  57.1 us (12%)
  local copies, waits for them, and re-layouts  44.1 us (9%)
  other arithmetic  39.6 us (8%)
  Pallas kernels  25.3 us (5%)
    ppermute x16, waiting for transfers between devices, spread(): arrived = lax.ppermute(array, axis, pair_hops(axis, bit))  73.9 us
    ppermute x11, waiting for transfers between devices, reduced(): lax.ppermute(part_of(array, 1 - high, half), axis, pair_hops(axis, bit))  62.2 us
    dot_general x18, matrix products, contract(): lax.dot_general(first, second, (((first_dim,), (second_dim,)), ((), ())),...  57.1 us
    ppermute x6, waiting for transfers between devices, scattered(): piece = lax.ppermute(piece, 'ctx', hops)  32.1 us
    ppermute x9, waiting for transfers between devices, sent_back(): back.append(lax.ppermute(pieces[shift], 'ctx', hops))  31.2 us
    ppermute x9, starting transfers between devices, sent_back(): back.append(lax.ppermute(pieces[shift], 'ctx', hops))  20.4 us
    ppermute x11, starting transfers between devices, reduced(): lax.ppermute(part_of(array, 1 - high, half), axis, pair_hops(axis, bit))  18.2 us
    ppermute x16, starting transfers between devices, spread(): arrived = lax.ppermute(array, axis, pair_hops(axis, bit))  15.8 us
  transfers between devices with their start and end apart: 68, of which 32 were waited for; matrix products, arithmetic and copies ran while one was open for 17% of the time, Pallas kernels for 3%

profile of v4, /device:TPU:0, one launch (start us, length us, event | category | flops | bytes accessed | tf_op | source)
XLA Modules:
  0.0 480.5 jit_solution(2958665442952557390)
XLA Ops:
  26.4 7.9 %convolution_bitcast_fusion = f32[2176,512]{1,0:T(8,128)} fusion(bf16[512,1088]{0,1:T(8,128)(2,1)} %pad_maximum_fusion.3, bf16[2176,1088]{0,1:T(8,128)(2,1)} %param.29), kind=kOutput, calls=%fused_computation.12 | convolution fusion | flops 2424307712 | bytes 10305536 | tf_op jit(solution)/shard_map/dot_general | solution.py:35
  34.2 13.0 %collective-permute-done.5 = bf16[3,5,64,256]{3,2,1,0:T(8,128)(2,1)S(1)} collective-permute-done((bf16[3,5,64,256]{3,2,1,0:T(8,128)(2,1)S(1)}, bf16[3,5,64,256]{3,2,1,0:T(8,128)(2,1)S(1)}, u32[]{:S(2)}, u32[]{:S(2)}) %collective-permute-start.5) | collective-permute-done | bytes 491552 | tf_op jit(solution)/shard_map/ppermute | solution.py:283
  47.2 11.2 %collective-permute-done.4 = bf16[3,5,64,256]{3,2,1,0:T(8,128)(2,1)S(1)} collective-permute-done((bf16[3,5,64,256]{3,2,1,0:T(8,128)(2,1)S(1)}, bf16[3,5,64,256]{3,2,1,0:T(8,128)(2,1)S(1)}, u32[]{:S(2)}, u32[]{:S(2)}) %collective-permute-start.4) | collective-permute-done | bytes 491552 | tf_op jit(solution)/shard_map/ppermute | solution.py:283
  59.5 9.7 %shard_map.271 = (bf16[4,5,64,256]{3,2,1,0:T(8,128)(2,1)S(1)}, f32[5,4,256]{2,1,0:T(4,128)S(1)}) custom-call(s32[8]{0:T(128)S(1)} %gather_fusion, bf16[4,3,5,64,256]{4,3,2,1,0:T(8,128)(2,1)S(1)} %pad_maximum_fusion.2.mixed_ref), custom_call_target="tpu_custom_call" | custom-call | flops 838860800 | bytes 2621440 | tf_op jit(solution)/shard_map/pallas_call | solution.py:204
  72.2 10.5 %collective-permute-start.10 = (bf16[5,64,256]{2,1,0:T(8,128)(2,1)S(1)}, bf16[5,64,256]{2,1,0:T(8,128)(2,1)S(1)}, u32[]{:S(2)}, u32[]{:S(2)}) collective-permute-start(bf16[5,64,256]{2,1,0:T(8,128)(2,1)S(1)} %get-tuple-element.205), channel_id=1, source_target_pairs={{0,4},{2,6},{4,0},{6,2},{1,5},{3,7},{5,1},{7,3},{8,12},{10,14},{12... | collective-permute-start | bytes 491528 | tf_op jit(solution)/shard_map/ppermute | solution.py:293
  84.0 12.4 %collective-permute-done.10 = bf16[5,64,256]{2,1,0:T(8,128)(2,1)S(1)} collective-permute-done((bf16[5,64,256]{2,1,0:T(8,128)(2,1)S(1)}, bf16[5,64,256]{2,1,0:T(8,128)(2,1)S(1)}, u32[]{:S(2)}, u32[]{:S(2)}) %collective-permute-start.10) | collective-permute-done | bytes 163872 | tf_op jit(solution)/shard_map/ppermute | solution.py:293
  103.6 10.5 %multiply_convert_fusion = (bf16[2176,512]{1,0:T(8,128)(2,1)}, bf16[2176,512]{1,0:T(8,128)(2,1)S(1)}) fusion(f32[2176,512]{1,0:T(8,128)} %convolution_bitcast_fusion, f32[2176]{0:T(1024)S(1)} %convert_element_type.244, bf16[512,1088]{0,1:T(8,128)(2,1)S(1)} %constant_dynamic-update-slice_fusion, bf16[1088,2176]{1,0:T(8,128)(2,1)} %param.27), kind=kOutput, calls=%fused_computation.25 | convolution fusion | flops 2449932288 | bytes 14770688 | tf_op jit(solution)/shard_map/dot_general | solution.py:35
  157.2 9.2 %shard_map.272 = bf16[4,3,3,64,256]{4,3,2,1,0:T(8,128)(2,1)S(1)} custom-call(s32[8]{0:T(128)S(1)} %gather_fusion, bf16[4,3,5,64,256]{4,3,2,1,0:T(8,128)(2,1)S(1)} %pad_maximum_fusion.2.mixed_ref, bf16[4,5,64,256]{3,2,1,0:T(8,128)(2,1)S(1)} %get-tuple-element.90.out_ref, bf16[4,5,64,256]{3,2,1,0:T(8,128)(2,1)S(1)} %maximum_bitcast_fusion.grad_ref, ...), custom_call_target="tpu_custom_call" | custom-call | tf_op jit(solution)/shard_map/pallas_call | solution.py:238
  166.4 6.4 %shard_map.273 = bf16[4,3,2,64,256]{4,3,2,1,0:T(8,128)(2,1)S(1)} custom-call(s32[8]{0:T(128)S(1)} %gather_fusion, bf16[4,3,5,64,256]{4,3,2,1,0:T(8,128)(2,1)S(1)} %pad_maximum_fusion.2.mixed_ref, bf16[4,5,64,256]{3,2,1,0:T(8,128)(2,1)S(1)} %get-tuple-element.90.out_ref, bf16[4,5,64,256]{3,2,1,0:T(8,128)(2,1)S(1)} %maximum_bitcast_fusion.grad_ref, ...), custom_call_target="tpu_custom_call" | custom-call | tf_op jit(solution)/shard_map/pallas_call | solution.py:238
  181.3 20.8 %collective-permute-done.25 = bf16[544,1088]{1,0:T(8,128)(2,1)} collective-permute-done((bf16[544,1088]{1,0:T(8,128)(2,1)}, bf16[544,1088]{1,0:T(8,128)(2,1)}, u32[]{:S(2)}, u32[]{:S(2)}) %collective-permute-start.25) | collective-permute-done | bytes 1183776 | tf_op jit(solution)/shard_map/ppermute | solution.py:322
  212.8 18.8 %collective-permute-done.26 = bf16[3,2,64,256]{3,2,1,0:T(8,128)(2,1)S(1)} collective-permute-done((bf16[3,2,64,256]{3,2,1,0:T(8,128)(2,1)S(1)}, bf16[3,2,64,256]{3,2,1,0:T(8,128)(2,1)S(1)}, u32[]{:S(2)}, u32[]{:S(2)}) %collective-permute-start.26) | collective-permute-done | bytes 196640 | tf_op jit(solution)/shard_map/ppermute | solution.py:293
  246.6 10.8 %collective-permute-done.32 = bf16[136,1088]{1,0:T(8,128)(2,1)S(1)} collective-permute-done((bf16[136,1088]{1,0:T(8,128)(2,1)S(1)}, bf16[136,1088]{1,0:T(8,128)(2,1)S(1)}, u32[]{:S(2)}, u32[]{:S(2)}) %collective-permute-start.32) | collective-permute-done | bytes 295968 | tf_op jit(solution)/shard_map/ppermute | solution.py:555
  262.6 10.4 %collective-permute-done.36 = bf16[136,1088]{1,0:T(8,128)(2,1)S(1)} collective-permute-done((bf16[136,1088]{1,0:T(8,128)(2,1)S(1)}, bf16[136,1088]{1,0:T(8,128)(2,1)S(1)}, u32[]{:S(2)}, u32[]{:S(2)}) %collective-permute-start.36) | collective-permute-done | bytes 295968 | tf_op jit(solution)/shard_map/ppermute | solution.py:329
  273.2 8.1 %collective-permute-done.35 = bf16[272,1088]{1,0:T(8,128)(2,1)S(1)} collective-permute-done((bf16[272,1088]{1,0:T(8,128)(2,1)S(1)}, bf16[272,1088]{1,0:T(8,128)(2,1)S(1)}, u32[]{:S(2)}, u32[]{:S(2)}) %collective-permute-start.35) | collective-permute-done | bytes 591904 | tf_op jit(solution)/shard_map/ppermute | solution.py:322
  296.5 16.2 %collective-permute-done.40 = bf16[136,1088]{1,0:T(8,128)(2,1)S(1)} collective-permute-done((bf16[136,1088]{1,0:T(8,128)(2,1)S(1)}, bf16[136,1088]{1,0:T(8,128)(2,1)S(1)}, u32[]{:S(2)}, u32[]{:S(2)}) %collective-permute-start.40) | collective-permute-done | bytes 295968 | tf_op jit(solution)/shard_map/ppermute | solution.py:322
  328.7 12.9 %collective-permute-done.46 = bf16[136,1088]{1,0:T(8,128)(2,1)S(1)} collective-permute-done((bf16[136,1088]{1,0:T(8,128)(2,1)S(1)}, bf16[136,1088]{1,0:T(8,128)(2,1)S(1)}, u32[]{:S(2)}, u32[]{:S(2)}) %collective-permute-start.46) | collective-permute-done | bytes 295968 | tf_op jit(solution)/shard_map/ppermute | solution.py:329
  354.2 10.5 %collective-permute-done.51 = bf16[68,2176]{1,0:T(8,128)(2,1)S(1)} collective-permute-done((bf16[68,2176]{1,0:T(8,128)(2,1)S(1)}, bf16[68,2176]{1,0:T(8,128)(2,1)S(1)}, u32[]{:S(2)}, u32[]{:S(2)}) %collective-permute-start.51) | collective-permute-done | bytes 295968 | tf_op jit(solution)/shard_map/ppermute | solution.py:322
  364.8 6.5 %collective-permute-done.50 = bf16[272,1088]{1,0:T(8,128)(2,1)S(1)} collective-permute-done((bf16[272,1088]{1,0:T(8,128)(2,1)S(1)}, bf16[272,1088]{1,0:T(8,128)(2,1)S(1)}, u32[]{:S(2)}, u32[]{:S(2)}) %collective-permute-start.50) | collective-permute-done | bytes 591904 | tf_op jit(solution)/shard_map/ppermute | solution.py:329
  371.8 7.7 %collective-permute-done.49 = bf16[544,1088]{1,0:T(8,128)(2,1)S(1)} collective-permute-done((bf16[544,1088]{1,0:T(8,128)(2,1)S(1)}, bf16[544,1088]{1,0:T(8,128)(2,1)S(1)}, u32[]{:S(2)}, u32[]{:S(2)}) %collective-permute-start.49) | collective-permute-done | bytes 1183776 | tf_op jit(solution)/shard_map/ppermute | solution.py:329
  391.2 7.6 %collective-permute-done.56 = bf16[68,2176]{1,0:T(8,128)(2,1)S(1)} collective-permute-done((bf16[68,2176]{1,0:T(8,128)(2,1)S(1)}, bf16[68,2176]{1,0:T(8,128)(2,1)S(1)}, u32[]{:S(2)}, u32[]{:S(2)}) %collective-permute-start.56) | collective-permute-done | bytes 295968 | tf_op jit(solution)/shard_map/ppermute | solution.py:329
  411.2 5.8 %collective-permute-done.60 = bf16[136,2176]{1,0:T(8,128)(2,1)S(1)} collective-permute-done((bf16[136,2176]{1,0:T(8,128)(2,1)S(1)}, bf16[136,2176]{1,0:T(8,128)(2,1)S(1)}, u32[]{:S(2)}, u32[]{:S(2)}) %collective-permute-start.60) | collective-permute-done | bytes 591904 | tf_op jit(solution)/shard_map/ppermute | solution.py:329
  417.2 10.8 %collective-permute-done.59 = bf16[272,2176]{1,0:T(8,128)(2,1)S(1)} collective-permute-done((bf16[272,2176]{1,0:T(8,128)(2,1)S(1)}, bf16[272,2176]{1,0:T(8,128)(2,1)S(1)}, u32[]{:S(2)}, u32[]{:S(2)}) %collective-permute-start.59) | collective-permute-done | bytes 1183776 | tf_op jit(solution)/shard_map/ppermute | solution.py:329
  443.1 5.8 %collective-permute-done.63 = bf16[136,2176]{1,0:T(8,128)(2,1)S(1)} collective-permute-done((bf16[136,2176]{1,0:T(8,128)(2,1)S(1)}, bf16[136,2176]{1,0:T(8,128)(2,1)S(1)}, u32[]{:S(2)}, u32[]{:S(2)}) %collective-permute-start.63) | collective-permute-done | bytes 591904 | tf_op jit(solution)/shard_map/ppermute | solution.py:329
  463.2 10.2 %collective-permute-done.67 = bf16[272,2176]{1,0:T(8,128)(2,1)} collective-permute-done((bf16[272,2176]{1,0:T(8,128)(2,1)S(1)}, bf16[272,2176]{1,0:T(8,128)(2,1)}, u32[]{:S(2)}, u32[]{:S(2)}) %collective-permute-start.67) | collective-permute-done | bytes 1183776 | tf_op jit(solution)/shard_map/ppermute | solution.py:632
  (439 shorter events, 224.3 us)
Async XLA Ops:
  17.8 41.7 %collective-permute-start.7 = (bf16[512,1088]{0,1:T(8,128)(2,1)}, bf16[512,1088]{0,1:T(8,128)(2,1)}, u32[]{:S(2)}, u32[]{:S(2)}) collective-permute-start(bf16[512,1088]{0,1:T(8,128)(2,1)} %pad_maximum_fusion.3), channel_id=1, source_target_pairs={{0,8},{8,0},{16,24},{24,16},{1,9},{9,1},{17,25},{25,17},{2,10},{10... | collective-permute-start | bytes 3342344 | tf_op jit(solution)/shard_map/ppermute | solution.py:447
  21.5 37.3 %collective-permute-start.8 = (bf16[256,544]{0,1:T(8,128)(2,1)}, bf16[256,544]{0,1:T(8,128)(2,1)S(1)}, u32[]{:S(2)}, u32[]{:S(2)}) collective-permute-start(bf16[256,544]{0,1:T(8,128)(2,1)} %get-tuple-element.219), channel_id=1, source_target_pairs={{0,1},{1,0},{2,3},{3,2},{4,5},{5,4},{6,7},{7,6},{8,9},{9,8},{10,11... | collective-permute-start | bytes 835592 | tf_op jit(solution)/shard_map/ppermute | solution.py:262
  21.7 25.6 %collective-permute-start.5 = (bf16[3,5,64,256]{3,2,1,0:T(8,128)(2,1)S(1)}, bf16[3,5,64,256]{3,2,1,0:T(8,128)(2,1)S(1)}, u32[]{:S(2)}, u32[]{:S(2)}) collective-permute-start(bf16[3,5,64,256]{3,2,1,0:T(8,128)(2,1)S(1)} %get-tuple-element.185), channel_id=1, source_target_pairs={{0,4},{2,6},{4,0},{6,2},{1,5},{3,7},{5,1},{7,3},{8,12},{10,14},{12... | collective-permute-start | bytes 1474568 | tf_op jit(solution)/shard_map/ppermute | solution.py:283
  25.7 32.8 %collective-permute-start.4 = (bf16[3,5,64,256]{3,2,1,0:T(8,128)(2,1)S(1)}, bf16[3,5,64,256]{3,2,1,0:T(8,128)(2,1)S(1)}, u32[]{:S(2)}, u32[]{:S(2)}) collective-permute-start(bf16[3,5,64,256]{3,2,1,0:T(8,128)(2,1)S(1)} %get-tuple-element.186), channel_id=1, source_target_pairs={{0,2},{2,4},{4,6},{6,0},{1,3},{3,5},{5,7},{7,1},{8,10},{10,12},{12... | collective-permute-start | bytes 1474568 | tf_op jit(solution)/shard_map/ppermute | solution.py:283
  72.1 25.3 %collective-permute-start.12 = (bf16[544,1088]{1,0:T(8,128)(2,1)S(1)}, bf16[544,1088]{1,0:T(8,128)(2,1)S(1)}, u32[]{:S(2)}, u32[]{:S(2)}) collective-permute-start(bf16[544,1088]{1,0:T(8,128)(2,1)S(1)} %copy-done.29), channel_id=1, source_target_pairs={{0,1},{1,0},{2,3},{3,2},{4,5},{5,4},{6,7},{7,6},{8,9},{9,8},{10,11... | collective-permute-start | bytes 3551240 | tf_op jit(solution)/shard_map/ppermute | solution.py:262
  72.2 24.2 %collective-permute-start.10 = (bf16[5,64,256]{2,1,0:T(8,128)(2,1)S(1)}, bf16[5,64,256]{2,1,0:T(8,128)(2,1)S(1)}, u32[]{:S(2)}, u32[]{:S(2)}) collective-permute-start(bf16[5,64,256]{2,1,0:T(8,128)(2,1)S(1)} %get-tuple-element.205), channel_id=1, source_target_pairs={{0,4},{2,6},{4,0},{6,2},{1,5},{3,7},{5,1},{7,3},{8,12},{10,14},{12... | collective-permute-start | bytes 491528 | tf_op jit(solution)/shard_map/ppermute | solution.py:293
  124.2 26.7 %collective-permute-start.19 = (bf16[1088,512]{1,0:T(8,128)(2,1)S(1)}, bf16[1088,512]{1,0:T(8,128)(2,1)S(1)}, u32[]{:S(2)}, u32[]{:S(2)}) collective-permute-start(bf16[1088,512]{1,0:T(8,128)(2,1)S(1)} %constant_dynamic-slice_fusion.18), channel_id=1, source_target_pairs={{0,8},{8,0},{16,24},{24,16},{1,9},{9,1},{17,25},{25,17},{2,10},{10... | collective-permute-start | bytes 3342344 | tf_op jit(solution)/shard_map/ppermute | solution.py:467
  124.7 51.6 %collective-permute-start.24 = (bf16[2176,512]{1,0:T(8,128)(2,1)}, bf16[2176,512]{1,0:T(8,128)(2,1)}, u32[]{:S(2)}, u32[]{:S(2)}) collective-permute-start(bf16[2176,512]{1,0:T(8,128)(2,1)} %pad_maximum_fusion.1), channel_id=1, source_target_pairs={{0,16},{8,24},{16,0},{24,8},{1,17},{9,25},{17,1},{25,9},{2,18},{10... | collective-permute-start | bytes 6684680 | tf_op jit(solution)/shard_map/ppermute | solution.py:471
  155.6 46.5 %collective-permute-start.25 = (bf16[544,1088]{1,0:T(8,128)(2,1)}, bf16[544,1088]{1,0:T(8,128)(2,1)}, u32[]{:S(2)}, u32[]{:S(2)}) collective-permute-start(bf16[544,1088]{1,0:T(8,128)(2,1)} %constant_dynamic-slice_fusion.17), channel_id=1, source_target_pairs={{0,16},{8,24},{16,0},{24,8},{1,17},{9,25},{17,1},{25,9},{2,18},{10... | collective-permute-start | bytes 3551240 | tf_op jit(solution)/shard_map/ppermute | solution.py:322
  172.9 30.9 %collective-permute-start.21 = (bf16[3,3,64,256]{3,2,1,0:T(8,128)(2,1)S(1)}, bf16[3,3,64,256]{3,2,1,0:T(8,128)(2,1)S(1)}, u32[]{:S(2)}, u32[]{:S(2)}) collective-permute-start(bf16[3,3,64,256]{3,2,1,0:T(8,128)(2,1)S(1)} %get-tuple-element.195), channel_id=1, source_target_pairs={{0,6},{2,0},{4,2},{6,4},{1,7},{3,1},{5,3},{7,5},{8,14},{10,8},{12,... | collective-permute-start | bytes 884744 | tf_op jit(solution)/shard_map/ppermute | solution.py:293
  173.0 30.8 %collective-permute-start.22 = (bf16[3,3,64,256]{3,2,1,0:T(8,128)(2,1)S(1)}, bf16[3,3,64,256]{3,2,1,0:T(8,128)(2,1)S(1)}, u32[]{:S(2)}, u32[]{:S(2)}) collective-permute-start(bf16[3,3,64,256]{3,2,1,0:T(8,128)(2,1)S(1)} %get-tuple-element.194), channel_id=1, source_target_pairs={{0,4},{2,6},{4,0},{6,2},{1,5},{3,7},{5,1},{7,3},{8,12},{10,14},{12... | collective-permute-start | bytes 884744 | tf_op jit(solution)/shard_map/ppermute | solution.py:293
  174.4 29.4 %collective-permute-start.23 = (bf16[3,3,64,256]{3,2,1,0:T(8,128)(2,1)S(1)}, bf16[3,3,64,256]{3,2,1,0:T(8,128)(2,1)S(1)}, u32[]{:S(2)}, u32[]{:S(2)}) collective-permute-start(bf16[3,3,64,256]{3,2,1,0:T(8,128)(2,1)S(1)} %get-tuple-element.193), channel_id=1, source_target_pairs={{0,2},{2,4},{4,6},{6,0},{1,3},{3,5},{5,7},{7,1},{8,10},{10,12},{12... | collective-permute-start | bytes 884744 | tf_op jit(solution)/shard_map/ppermute | solution.py:293
  203.9 28.0 %collective-permute-start.30 = (bf16[272,1088]{1,0:T(8,128)(2,1)S(1)}, bf16[272,1088]{1,0:T(8,128)(2,1)S(1)}, u32[]{:S(2)}, u32[]{:S(2)}) collective-permute-start(bf16[272,1088]{1,0:T(8,128)(2,1)S(1)} %constant_dynamic-slice_fusion.15), channel_id=1, source_target_pairs={{0,2},{2,0},{4,6},{6,4},{1,3},{3,1},{5,7},{7,5},{8,10},{10,8},{12,... | collective-permute-start | bytes 1775624 | tf_op jit(solution)/shard_map/ppermute | solution.py:322
  204.1 28.8 %collective-permute-start.29 = (bf16[544,1088]{1,0:T(8,128)(2,1)S(1)}, bf16[544,1088]{1,0:T(8,128)(2,1)S(1)}, u32[]{:S(2)}, u32[]{:S(2)}) collective-permute-start(bf16[544,1088]{1,0:T(8,128)(2,1)S(1)} %constant_dynamic-slice_fusion.16), channel_id=1, source_target_pairs={{0,8},{8,0},{16,24},{24,16},{1,9},{9,1},{17,25},{25,17},{2,10},{10... | collective-permute-start | bytes 3551240 | tf_op jit(solution)/shard_map/ppermute | solution.py:322
  205.7 25.9 %collective-permute-start.26 = (bf16[3,2,64,256]{3,2,1,0:T(8,128)(2,1)S(1)}, bf16[3,2,64,256]{3,2,1,0:T(8,128)(2,1)S(1)}, u32[]{:S(2)}, u32[]{:S(2)}) collective-permute-start(bf16[3,2,64,256]{3,2,1,0:T(8,128)(2,1)S(1)} %get-tuple-element.199), channel_id=1, source_target_pairs={{0,6},{2,0},{4,2},{6,4},{1,7},{3,1},{5,3},{7,5},{8,14},{10,8},{12,... | collective-permute-start | bytes 589832 | tf_op jit(solution)/shard_map/ppermute | solution.py:293
  207.4 24.3 %collective-permute-start.27 = (bf16[3,2,64,256]{3,2,1,0:T(8,128)(2,1)S(1)}, bf16[3,2,64,256]{3,2,1,0:T(8,128)(2,1)S(1)}, u32[]{:S(2)}, u32[]{:S(2)}) collective-permute-start(bf16[3,2,64,256]{3,2,1,0:T(8,128)(2,1)S(1)} %get-tuple-element.198), channel_id=1, source_target_pairs={{0,4},{2,6},{4,0},{6,2},{1,5},{3,7},{5,1},{7,3},{8,12},{10,14},{12... | collective-permute-start | bytes 589832 | tf_op jit(solution)/shard_map/ppermute | solution.py:293
  257.7 27.3 %collective-permute-start.34 = (bf16[272,2176]{1,0:T(8,128)(2,1)S(1)}, bf16[272,2176]{1,0:T(8,128)(2,1)S(1)}, u32[]{:S(2)}, u32[]{:S(2)}) collective-permute-start(bf16[272,2176]{1,0:T(8,128)(2,1)S(1)} %constant_dynamic-slice_fusion.11), channel_id=1, source_target_pairs={{0,16},{8,24},{16,0},{24,8},{1,17},{9,25},{17,1},{25,9},{2,18},{10... | collective-permute-start | bytes 3551240 | tf_op jit(solution)/shard_map/ppermute | solution.py:322
  261.1 27.1 %collective-permute-start.33 = (bf16[272,2176]{1,0:T(8,128)(2,1)S(1)}, bf16[272,2176]{1,0:T(8,128)(2,1)S(1)}, u32[]{:S(2)}, u32[]{:S(2)}) collective-permute-start(bf16[272,2176]{1,0:T(8,128)(2,1)S(1)} %constant_dynamic-slice_fusion.12), channel_id=1, source_target_pairs={{0,8},{8,0},{16,24},{24,16},{1,9},{9,1},{17,25},{25,17},{2,10},{10... | collective-permute-start | bytes 3551240 | tf_op jit(solution)/shard_map/ppermute | solution.py:322
  350.3 29.2 %collective-permute-start.49 = (bf16[544,1088]{1,0:T(8,128)(2,1)S(1)}, bf16[544,1088]{1,0:T(8,128)(2,1)S(1)}, u32[]{:S(2)}, u32[]{:S(2)}) collective-permute-start(bf16[544,1088]{1,0:T(8,128)(2,1)S(1)} %maximum_select_fusion.5), channel_id=1, source_target_pairs={{0,8},{8,0},{16,24},{24,16},{1,9},{9,1},{17,25},{25,17},{2,10},{10... | collective-permute-start | bytes 3551240 | tf_op jit(solution)/shard_map/ppermute | solution.py:329
  351.8 30.2 %collective-permute-start.48 = (bf16[272,2176]{1,0:T(8,128)(2,1)S(1)}, bf16[272,2176]{1,0:T(8,128)(2,1)S(1)}, u32[]{:S(2)}, u32[]{:S(2)}) collective-permute-start(bf16[272,2176]{1,0:T(8,128)(2,1)S(1)} %maximum_select_fusion.8), channel_id=1, source_target_pairs={{0,16},{8,24},{16,0},{24,8},{1,17},{9,25},{17,1},{25,9},{2,18},{10... | collective-permute-start | bytes 3551240 | tf_op jit(solution)/shard_map/ppermute | solution.py:329
  402.8 25.3 %collective-permute-start.59 = (bf16[272,2176]{1,0:T(8,128)(2,1)S(1)}, bf16[272,2176]{1,0:T(8,128)(2,1)S(1)}, u32[]{:S(2)}, u32[]{:S(2)}) collective-permute-start(bf16[272,2176]{1,0:T(8,128)(2,1)S(1)} %maximum_select_fusion.9), channel_id=1, source_target_pairs={{0,8},{8,0},{16,24},{24,16},{1,9},{9,1},{17,25},{25,17},{2,10},{10... | collective-permute-start | bytes 3551240 | tf_op jit(solution)/shard_map/ppermute | solution.py:329
  404.8 26.8 %collective-permute-start.58 = (bf16[544,1088]{1,0:T(8,128)(2,1)S(1)}, bf16[544,1088]{1,0:T(8,128)(2,1)S(1)}, u32[]{:S(2)}, u32[]{:S(2)}) collective-permute-start(bf16[544,1088]{1,0:T(8,128)(2,1)S(1)} %maximum_select_fusion.7), channel_id=1, source_target_pairs={{0,16},{8,24},{16,0},{24,8},{1,17},{9,25},{17,1},{25,9},{2,18},{10... | collective-permute-start | bytes 3551240 | tf_op jit(solution)/shard_map/ppermute | solution.py:329
  449.5 23.9 %collective-permute-start.67 = (bf16[272,2176]{1,0:T(8,128)(2,1)S(1)}, bf16[272,2176]{1,0:T(8,128)(2,1)}, u32[]{:S(2)}, u32[]{:S(2)}) collective-permute-start(bf16[272,2176]{1,0:T(8,128)(2,1)S(1)} %maximum_select_fusion.12), channel_id=1, source_target_pairs={{0,16},{8,24},{16,0},{24,8},{1,17},{9,25},{17,1},{25,9},{2,18},{10... | collective-permute-start | bytes 3551240 | tf_op jit(solution)/shard_map/ppermute | solution.py:632
  450.7 24.1 %collective-permute-start.66 = (bf16[272,2176]{1,0:T(8,128)(2,1)S(1)}, bf16[272,2176]{1,0:T(8,128)(2,1)S(1)}, u32[]{:S(2)}, u32[]{:S(2)}) collective-permute-start(bf16[272,2176]{1,0:T(8,128)(2,1)S(1)} %maximum_select_fusion.11), channel_id=1, source_target_pairs={{0,8},{8,0},{16,24},{24,16},{1,9},{9,1},{17,25},{25,17},{2,10},{10... | collective-permute-start | bytes 3551240 | tf_op jit(solution)/shard_map/ppermute | solution.py:632
  (113 other events, 1200.7 us)
